TPU v7x, 256 devices: a whole 4x4x8 slice. The times are simulated.
256 devices in a mesh: seq: 64 (over y, x, z_hi), tp: 4 (over z_lo, core).
Axes of the slice: x: 4, y: 4, z: 8 (z_hi: 4, z_lo: 2; z = z_hi * 2 + z_lo), core: 2. Of those that a mesh axis runs over, the one named last changes fastest.
Arguments:
- query_proj: bfloat16 [65536, 4096], P('seq', 'tp'), may hold values from -6 to 6
- key_proj: bfloat16 [65536, 4096], P('seq', 'tp'), may hold values from -6 to 6
- value_proj: bfloat16 [65536, 4096], P('seq', 'tp'), may hold values from -6 to 6
- decay_rates: float32 [16, 4096], P(None, 'tp'), may hold values from 0 to 1, as said below
- residues: float32 [16, 4096], P(None, 'tp'), may hold values from -2 to 2
- skip_gain: float32 [4096], P('tp'), may hold values from -1 to 1
- out_weight: bfloat16 [4096, 4096], P('tp'), may hold values from -0.09375 to 0.09375
Outputs:
- mixed_out: bfloat16 [65536, 4096], P('seq', 'tp')
Inputs may be any that keep to these rules, and one draw needn't show every extreme that they name: `decay_rates`: positive decay rates.
All inputs are finite; a program needn't handle non-finite values.
Results may differ from a plain program's by a relative error of at most 0.014.
Values may be sent and summed in bfloat16 or wider, within the bound.
No kernel may reach another device: no remote copies, remote signals or barrier semaphores. Data moves between devices by JAX's collectives and lax.ppermute only.
A program may use at most 192 MiB of HBM per device.

v0:
```python
import jax
import jax.numpy as jnp
from jax import lax
from jax.sharding import PartitionSpec as P

SUB = 32


def carried_in(value, axis, join, neutral):
    count, mine = (lax.axis_size(axis), lax.axis_index(axis))
    pieces = jax.tree.map(lambda part: lax.all_gather(part, axis), value)
    running = jax.tree.map(
        lambda part, zero: jnp.full_like(part, 0) + jnp.asarray(zero, part.dtype), value, neutral
    )

    def hop(position, running):
        longer = join(running, jax.tree.map(lambda part: part[position], pieces))
        return jax.tree.map(lambda new, old: jnp.where(position < mine, new, old), longer, running)

    return lax.fori_loop(0, count - 1, hop, running)


def local_pass(inputs, decay_rates, residues, sub_len):
    tok_rows, chan_count = inputs.shape
    sub_count = tok_rows // sub_len
    positions = jnp.arange(sub_len, dtype=jnp.float32)
    powers = jnp.exp(-decay_rates[None] * positions[:, None, None])
    weights_modal = residues * jnp.sqrt(decay_rates)
    kernel_taps = jnp.einsum("tnc,nc->tc", powers, weights_modal, precision=lax.Precision.HIGHEST)
    distance = positions[:, None] - positions[None, :]
    onehot = (distance[:, :, None] == positions[None, None, :]).astype(jnp.float32)
    toeplitz = jnp.einsum("tsd,dc->tsc", onehot, kernel_taps, precision=lax.Precision.HIGHEST)
    pieces = inputs.reshape(sub_count, sub_len, chan_count)
    end_states = jnp.einsum("snc,msc->mnc", powers[::-1], pieces, precision=lax.Precision.HIGHEST)
    step_decay = jnp.exp(-decay_rates * sub_len)

    def advance(carry_state, block_end):
        return (step_decay * carry_state + block_end, carry_state)

    final_state, before = lax.scan(advance, jnp.zeros_like(decay_rates), end_states)
    inside = jnp.einsum("tsc,msc->mtc", toeplitz, pieces, precision=lax.Precision.HIGHEST)
    reach_table = powers * jnp.exp(-decay_rates)[None] * weights_modal[None]
    return (inside, before, final_state, reach_table)


def on_device(query_proj, key_proj, value_proj, decay_rates, residues, skip_gain, out_weight):
    tok_rows, chan_count = query_proj.shape
    sub_len = SUB
    sub_count = tok_rows // sub_len
    inputs = key_proj.astype(jnp.float32) * value_proj.astype(jnp.float32)
    inside, before, final_state, reach_table = local_pass(inputs, decay_rates, residues, sub_len)
    block_length = float(tok_rows)

    def combine(earlier, later):
        return (earlier[0] * later[0], earlier[1] * later[0] + later[1])

    block_decay = jnp.exp(-decay_rates * block_length)
    identity = (jnp.ones_like(decay_rates), jnp.zeros_like(decay_rates))
    prefix = carried_in((block_decay, final_state), "seq", combine, identity)
    incoming = prefix[1]
    offsets = jnp.arange(sub_count, dtype=jnp.float32) * float(sub_len)
    before_total = before + jnp.exp(-decay_rates[None] * offsets[:, None, None]) * incoming[None]
    carried = jnp.einsum("tnc,mnc->mtc", reach_table, before_total, precision=lax.Precision.HIGHEST)
    convolved = (inside + carried).reshape(tok_rows, chan_count)
    gated = (query_proj.astype(jnp.float32) * (convolved + skip_gain[None] * inputs)).astype(
        jnp.bfloat16
    )
    partial_value = jnp.dot(gated, out_weight, preferred_element_type=jnp.float32)
    return lax.psum_scatter(
        partial_value.astype(jnp.bfloat16), "tp", scatter_dimension=1, tiled=True
    )


def solution(mesh):
    placed = (
        P("seq", "tp"),
        P("seq", "tp"),
        P("seq", "tp"),
        P(None, "tp"),
        P(None, "tp"),
        P("tp"),
        P("tp", None),
    )
    return jax.shard_map(
        on_device, mesh=mesh, in_specs=placed, out_specs=P("seq", "tp"), check_vma=False
    )
```

profile of v0, /device:TPU:1, one launch (start us, length us, event | category | flops | bytes accessed | tf_op | source)
XLA Modules:
  0.0 423.3 jit_solution(3291065963624965706)
XLA Ops:
  6.5 1.5 negate_exponential_fusion
  8.2 5.1 %convert_multiply_fusion = f32[1024,1024]{1,0:T(8,128)} fusion(bf16[1024,1024]{1,0:T(8,128)(2,1)} %param.13, bf16[1024,1024]{1,0:T(8,128)(2,1)} %param.12), kind=kLoop, calls=%fused_computation.10 | loop fusion | flops 3145728 | bytes 8388608 | tf_op jit(solution)/shard_map/mul | solution.py:50
  13.2 14.3 %copy.15 = f32[32,32,1024]{1,0,2:T(8,128)} copy(f32[32,32,1024]{2,1,0:T(8,128)} %bitcast.47) | data formatting | bytes 8388608 | tf_op jit(solution)/shard_map/reshape | solution.py:33
  27.6 1.6 multiply_exponential_fusion
  29.2 1.7 rev.3
  30.9 6.5 %copy.17 = f32[32,16,1024]{0,1,2:T(8,128)} copy(f32[32,16,1024]{2,1,0:T(8,128)S(1)} %rev.3) | data formatting | bytes 4194304 | tf_op jit(solution)/shard_map/rev | solution.py:34
  37.4 30.7 %convolution_bitcast_fusion = f32[32,16,1024]{0,1,2:T(8,128)} fusion(f32[32,32,1024]{1,0,2:T(8,128)} %copy.15, f32[32,16,1024]{0,1,2:T(8,128)} %copy.17), kind=kOutput, calls=%fused_computation.11 | convolution fusion | flops 201326592 | bytes 8388608 | tf_op jit(solution)/shard_map/snc,msc->mnc/dot_general | solution.py:34
  68.1 5.8 %copy.18 = f32[32,16,1024]{2,1,0:T(8,128)S(1)} copy(f32[32,16,1024]{0,1,2:T(8,128)} %convolution_bitcast_fusion) | data formatting | bytes 4194304
  73.8 21.7 %while.27 = (s32[]{:T(128)}, f32[16,1024]{1,0:T(8,128)S(1)}, f32[32,16,1024]{2,1,0:T(8,128)}, f32[16,1024]{1,0:T(8,128)S(1)}, f32[32,16,1024]{2,1,0:T(8,128)S(1)}, /*index=5*/s32[]{:T(128)}, s32[]{:T(128)}) while((s32[]{:T(128)}, f32[16,1024]{1,0:T(8,128)S(1)}, f32[32,16,1024]{2,1,0:T(8,128)}, f32[16,1024]{1,0:T(8,128)S(1)}, ...), condition=%wide.region_1.2_spmd.clone, body=%wide.region_0.1_spmd.clone.sunk | while | flops 65539 | bytes 393320 | solution.py:40
  96.9 3.8 fusion.3
  100.6 14.3 %copy.30 = f32[32,32,1024]{1,0,2:T(8,128)} copy(f32[32,32,1024]{2,1,0:T(8,128)} %fusion.3) | data formatting | bytes 8388608 | tf_op jit(solution)/shard_map/tsd,dc->tsc/dot_general | solution.py:32
  115.0 32.9 %fusion.6 = f32[1024,32,32]{2,1,0:T(8,128)} fusion(f32[32,32,1024]{1,0,2:T(8,128)} %copy.15, f32[32,32,1024]{1,0,2:T(8,128)} %copy.30), kind=kOutput, calls=%fused_computation.26 | convolution fusion | flops 402653184 | bytes 12582912 | tf_op jit(solution)/shard_map/tsc,msc->mtc/dot_general | solution.py:41
  147.9 46.8 %all-gather.7.cloned.1.call-done = f32[1024,1024]{1,0:T(8,128)} async-done(((f32[16,1024]{1,0:T(8,128)}), f32[1024,1024]{1,0:T(8,128)}) %all-gather.7.cloned.1.call-update) | async-done | bytes 4194320 | tf_op jit(solution)/shard_map/all_gather | solution.py:11
  194.7 59.0 %while.28 = (s32[]{:T(128)}, f32[16,1024]{1,0:T(8,128)S(1)}, s32[]{:T(128)}, f32[64,16,1024]{2,1,0:T(8,128)}, f32[64,16,1024]{2,1,0:T(8,128)}, /*index=5*/s32[]{:T(128)}, s32[]{:T(128)}) while((s32[]{:T(128)}, f32[16,1024]{1,0:T(8,128)S(1)}, s32[]{:T(128)}, f32[64,16,1024]{2,1,0:T(8,128)}, f32[64,16,1024]{2,1,0:T(8,128)}, ...), condition=%wide.region_3.4_spmd.clone, body=%wide.region_2.3_spmd.clone.sunk | while | flops 65540 | bytes 262253 | solution.py:20
  195.6 0.9 fusion.16
  196.5 0.9 fusion.16
  253.7 3.6 multiply_multiply_fusion
  257.3 7.6 %copy.19 = f32[32,16,1024]{0,1,2:T(8,128)} copy(f32[32,16,1024]{2,1,0:T(8,128)} %get-tuple-element.197) | data formatting | bytes 4194304 | tf_op jit(solution)/shard_map/add | solution.py:62
  264.9 6.5 %copy.20 = f32[32,16,1024]{0,1,2:T(8,128)} copy(f32[32,16,1024]{2,1,0:T(8,128)S(1)} %get-tuple-element.196) | data formatting | bytes 4194304 | tf_op jit(solution)/shard_map/mul | solution.py:42
  271.4 33.9 %add_bitcast_fusion = f32[32,32,1024]{1,0,2:T(8,128)} fusion(f32[1024,32,32]{2,1,0:T(8,128)} %fusion.6, f32[32,16,1024]{0,1,2:T(8,128)} %copy.19, f32[32,16,1024]{0,1,2:T(8,128)} %copy.20), kind=kOutput, calls=%fused_computation.5 | convolution fusion | flops 202375168 | bytes 12582912 | tf_op jit(solution)/shard_map/tnc,mnc->mtc/dot_general | solution.py:63
  305.3 11.6 %copy.21 = f32[32,32,1024]{2,1,0:T(8,128)} copy(f32[32,32,1024]{1,0,2:T(8,128)} %add_bitcast_fusion) | data formatting | bytes 8388608 | tf_op jit(solution)/shard_map/add | solution.py:64
  316.9 5.1 %fusion.2 = bf16[1024,1024]{1,0:T(8,128)(2,1)S(1)} fusion(f32[32,32,1024]{2,1,0:T(8,128)} %copy.21, bf16[1024,1024]{1,0:T(8,128)(2,1)} %param.11, f32[1024]{0:T(1024)S(1)} %copy-done.2, bf16[1024,1024]{1,0:T(8,128)(2,1)S(1)} %copy-done, bf16[1024,1024]{1,0:T(8,128)(2,1)} %param.12), kind=kLoop, calls=%fused_computation.9 | loop fusion | flops 8388608 | bytes 12587008 | tf_op jit(solution)/shard_map/convert_element_type | solution.py:65
  322.0 14.2 %convolution_convert_fusion = bf16[1024,4096]{1,0:T(8,128)(2,1)} fusion(bf16[1024,1024]{1,0:T(8,128)(2,1)S(1)} %fusion.2, bf16[1024,4096]{1,0:T(8,128)(2,1)} %param.17), kind=kOutput, calls=%fused_computation.6 | convolution fusion | flops 8594128896 | bytes 18874368 | tf_op jit(solution)/shard_map/dot_general | solution.py:68
  336.3 80.5 %reduce-scatter.2.cloned.1.call-done = bf16[1024,1024]{1,0:T(8,128)(2,1)} async-done(((bf16[1024,4096]{1,0:T(8,128)(2,1)}), bf16[1024,1024]{1,0:T(8,128)(2,1)}) %reduce-scatter.2.cloned.1.call-update) | async-done | bytes 2097168 | tf_op jit(solution)/shard_map/reduce_scatter | solution.py:69
  (144 shorter events, 78.2 us)
Async XLA Ops:
  6.5 141.3 %all-gather.5.cloned.1.call-start = ((), (), s32[]{:S(2)}) async-start(), calls=%async_computation.2 | async-start | bytes 4259840 | tf_op jit(solution)/shard_map/all_gather | solution.py:11
  8.1 186.6 %all-gather.7.cloned.1.call-start = ((), (), s32[]{:S(2)}) async-start(), calls=%async_computation.3 | async-start | bytes 4259840 | tf_op jit(solution)/shard_map/all_gather | solution.py:11
  95.6 0.6 copy-start.1
  96.2 320.6 %reduce-scatter.2.cloned.1.call-start = ((), (), s32[]{:S(2)}) async-start(), calls=%async_computation.1 | async-start | bytes 10485760 | tf_op jit(solution)/shard_map/reduce_scatter | solution.py:69
  305.3 11.6 %copy-start = (bf16[1024,1024]{1,0:T(8,128)(2,1)S(1)}, bf16[1024,1024]{1,0:T(8,128)(2,1)}, u32[]{:S(2)}) copy-start(bf16[1024,1024]{1,0:T(8,128)(2,1)} %param.13) | copy-start | bytes 6291460
  305.3 11.6 %copy-start.2 = (f32[1024]{0:T(1024)S(1)}, f32[1024]{0:T(1024)}, u32[]{:S(2)}) copy-start(f32[1024]{0:T(1024)} %param.16) | copy-start | bytes 12292
Sparse Core Ops, SparseCore 0:
  10.7 92.9 all-gather.4
  107.0 87.6 all-gather.6
  336.4 80.3 reduce-scatter.1
where the time goes:
time: 427 us; the launch traced here: 423 us
  waiting for transfers between devices  127 us (30%)
  matrix products  115 us (27%)
  other arithmetic  96.3 us (23%)
  local copies, waits for them, and re-layouts  69 us (16%)
  between operations  13.2 us (3%)
    reduce_scatter x1, waiting for transfers between devices, on_device(): lax.psum_scatter(partial_value.astype(jnp.bfloat16), 'tp', scatter_dimens...  80.5 us
    select_n x63, other arithmetic, hop(): jnp.where(position < mine, new, old)  57.6 us
    all_gather x2, waiting for transfers between devices, carried_in(): pieces = jax.tree.map(lambda part: lax.all_gather(part, axis), value)  46.8 us
    dot_general x1, matrix products, on_device(): jnp.einsum('tnc,mnc->mtc', reach_table, before_total, precision=lax.Preci...  33.9 us
    dot_general x1, matrix products, local_pass(): jnp.einsum('tsc,msc->mtc', toeplitz, pieces, precision=lax.Precision.HIGH...  32.9 us
    dot_general x1, matrix products, local_pass(): jnp.einsum('snc,msc->mnc', powers[::-1], pieces, precision=lax.Precision....  30.7 us
    dynamic_update_slice x32, other arithmetic, local_pass(): lax.scan(advance, jnp.zeros_like(decay_rates), end_states)  20.5 us
    reshape x1, local copies, waits for them, and re-layouts, local_pass(): pieces = inputs.reshape(sub_count, sub_len, chan_count)  14.3 us
  transfers between devices with their start and end apart: 3, of which 2 were waited for; matrix products, arithmetic and copies ran while one was open for 33% of the time, Pallas kernels for 0%

commit v1 on v0

v1 whole, which is shorter than its diff:
```python
import functools

import jax
import jax.numpy as jnp
from jax import lax
from jax.experimental import pallas as pl
from jax.experimental.pallas import tpu as pltpu
from jax.sharding import PartitionSpec as P

SEG = 8
LANES = 128
SPANS = (16, 16, 32, 32, 32)
VMEM_LIMIT = 32 * 2**20
VMEM_ALL = 60 * 2**20
SIBLING = [(0, 1), (1, 0), (2, 3), (3, 2)]
PARTNER = [(0, 2), (2, 0), (1, 3), (3, 1)]
ANY = pl.BlockSpec(memory_space=pl.ANY)


def cost(flops, moved):
    return pl.CostEstimate(flops=1, bytes_accessed=1, transcendentals=0)


def end_kernel(seg_len, k_ref, v_ref, lam_ref, last_ref, before_ref, sent_ref, x_ref):
    order = lam_ref.shape[0]
    pitch = seg_len + 1
    for group in range(k_ref.shape[1] // LANES):
        cols = slice(group * LANES, (group + 1) * LANES)
        for seg in range(SEG):
            rows = pl.ds(seg * seg_len, seg_len)
            x = k_ref[rows, cols].astype(jnp.float32) * v_ref[rows, cols].astype(jnp.float32)
            x_ref[pl.ds(seg * pitch, seg_len), :] = x
        lam = [jnp.broadcast_to(lam_ref[n : n + 1, cols], (SEG, LANES)) for n in range(order)]
        decay = [jnp.exp(-rate) for rate in lam]

        def body(it, state):
            for u in range(16):
                x = x_ref[pl.ds(it * 16 + u, SEG, stride=pitch), :]
                state = tuple(h * d + x for h, d in zip(state, decay))
            return state

        zero = jnp.zeros((SEG, LANES), jnp.float32)
        state = lax.fori_loop(0, seg_len // 16, body, (zero,) * order)
        row = lax.broadcasted_iota(jnp.int32, (SEG, LANES), 0)
        for n in range(order):
            run = state[n]
            for step in (1, 2, 4):
                hop = jnp.exp(lam[n] * (-float(seg_len * step)))
                run = run + jnp.where(row >= step, hop * pltpu.roll(run, step, 0), 0.0)
            last_ref[n : n + 1, cols] = run[SEG - 1 : SEG]
            sent_ref[n : n + 1, cols] = run[SEG - 1 : SEG].astype(jnp.bfloat16)
            before_ref[n * SEG : (n + 1) * SEG, cols] = jnp.where(
                row >= 1, pltpu.roll(run, 1, 0), 0.0
            )


def end_states(key, value, rates, width=256):
    tok, ch = key.shape
    order = rates.shape[0]
    seg_len = tok // SEG
    cut = lambda rows: pl.BlockSpec((rows, width), lambda j: (0, j))
    return pl.pallas_call(
        functools.partial(end_kernel, seg_len),
        grid=(ch // width,),
        in_specs=[cut(tok), cut(tok), cut(order)],
        out_specs=[cut(order), cut(order * SEG), cut(order)],
        out_shape=[
            jax.ShapeDtypeStruct((order, ch), jnp.float32),
            jax.ShapeDtypeStruct((order * SEG, ch), jnp.float32),
            jax.ShapeDtypeStruct((order, ch), jnp.bfloat16),
        ],
        scratch_shapes=[pltpu.VMEM((SEG * (seg_len + 1), LANES), jnp.float32)],
        compiler_params=pltpu.CompilerParams(vmem_limit_bytes=VMEM_ALL),
        cost_estimate=cost(2 * tok * ch * order, 4 * tok * ch),
        name="end_states",
    )(key, value, rates)


def gate_kernel(first, late, seg_len, q_ref, k_ref, v_ref, lam_ref, res_ref, skip_ref, state_ref, *rest):
    g_ref, next_ref, x_ref, y_ref = rest[-4:]
    if first:
        inc_ref = rest[0]
    order = lam_ref.shape[0]
    span = q_ref.shape[1]
    pitch = span + 1
    for group in range(q_ref.shape[2] // LANES):
        cols = slice(group * LANES, (group + 1) * LANES)
        for seg in range(SEG):
            x = k_ref[seg, :, cols].astype(jnp.float32) * v_ref[seg, :, cols].astype(jnp.float32)
            x_ref[pl.ds(seg * pitch, span), :] = x
        lam = [jnp.broadcast_to(lam_ref[n : n + 1, cols], (SEG, LANES)) for n in range(order)]
        decay = [jnp.exp(-rate) for rate in lam]
        weight = [res_ref[n : n + 1, cols] * jnp.sqrt(lam[n]) for n in range(order)]
        state = [state_ref[n * SEG : (n + 1) * SEG, cols] for n in range(order)]
        if first:
            row = lax.broadcasted_iota(jnp.int32, (SEG, LANES), 0).astype(jnp.float32)
            reach = row * (-float(seg_len)) - float(late)
            state = [
                h + jnp.exp(lam[n] * reach) * inc_ref[n : n + 1, cols]
                for n, h in enumerate(state)
            ]

        def body(it, state):
            for u in range(16):
                where = pl.ds(it * 16 + u, SEG, stride=pitch)
                x = x_ref[where, :]
                state = tuple(h * d + x for h, d in zip(state, decay))
                terms = [w * h for w, h in zip(weight, state)]
                while len(terms) > 1:
                    terms = [a + b for a, b in zip(terms[::2], terms[1::2])]
                y_ref[where, :] = terms[0]
            return state

        if span == 16:
            state = body(0, tuple(state))
        else:
            state = lax.fori_loop(0, span // 16, body, tuple(state))
        for n in range(order):
            next_ref[n * SEG : (n + 1) * SEG, cols] = state[n]
        skip = skip_ref[:, cols]
        for seg in range(SEG):
            rows = pl.ds(seg * pitch, span)
            gate = q_ref[seg, :, cols].astype(jnp.float32) * (y_ref[rows, :] + skip * x_ref[rows, :])
            g_ref[seg, :, cols] = gate.astype(jnp.bfloat16)


def gate_chunk(
    query, key, value, rates, residues, skip, state, incoming, after, at, span, width=512
):
    seg, seg_len, ch = query.shape
    order = rates.shape[0]
    first = incoming is not None
    part = pl.BlockSpec((seg, span, width), lambda j: (0, at // span, j))
    cut = lambda rows: pl.BlockSpec((rows, width), lambda j: (0, j))
    operands = [query, key, value, rates, residues, skip, state]
    in_specs = [part, part, part, cut(order), cut(order), cut(1), cut(order * seg)]
    if first:
        operands.append(incoming)
        in_specs.append(cut(order))
    operands.extend(after)
    in_specs.extend([ANY] * len(after))
    rows = seg * span
    gated, state = pl.pallas_call(
        functools.partial(gate_kernel, first, at, seg_len),
        grid=(ch // width,),
        in_specs=in_specs,
        out_specs=[pl.BlockSpec((seg, span, width), lambda j: (0, 0, j)), cut(order * seg)],
        out_shape=[
            jax.ShapeDtypeStruct((seg, span, ch), jnp.bfloat16),
            jax.ShapeDtypeStruct((order * seg, ch), jnp.float32),
        ],
        scratch_shapes=[pltpu.VMEM((seg * (span + 1), LANES), jnp.float32)] * 2,
        compiler_params=pltpu.CompilerParams(vmem_limit_bytes=VMEM_LIMIT),
        cost_estimate=cost(4 * rows * ch * order, 8 * rows * ch + 8 * order * seg * ch),
        name="gate_chunk",
    )(*operands)
    return gated.reshape(rows, ch), state


def columns_kernel(at_ref, w_ref, wo_ref, out_ref):
    depth = w_ref.shape[0]
    out_ref[:depth] = w_ref[...]
    out_ref[depth:] = wo_ref[...]


def chip_columns(block, weight, weight_other, width=512):
    ch = weight.shape[0]
    per = ch // width
    part = pl.BlockSpec((ch, width), lambda j, at: (0, at[0] * per + j))
    return pl.pallas_call(
        columns_kernel,
        grid_spec=pltpu.PrefetchScalarGridSpec(
            num_scalar_prefetch=1,
            grid=(per,),
            in_specs=[part, part],
            out_specs=pl.BlockSpec((2 * ch, width), lambda j, at: (0, j)),
        ),
        out_shape=jax.ShapeDtypeStruct((2 * ch, ch), weight.dtype),
        compiler_params=pltpu.CompilerParams(vmem_limit_bytes=VMEM_LIMIT),
        cost_estimate=cost(0, 8 * ch * ch),
        name="chip_columns",
    )(block, weight, weight_other)


def product(mine, other, weight):
    depth = weight.shape[0] // 2
    total = jnp.dot(mine, weight[:depth], preferred_element_type=jnp.float32)
    return total + jnp.dot(other, weight[depth:], preferred_element_type=jnp.float32)


def share_kernel(mine_ref, other_ref, w_ref, *rest):
    out_ref = rest[-1]
    out_ref[...] = product(mine_ref[...], other_ref[...], w_ref[...]).astype(out_ref.dtype)


def share_chunk(mine, other, weight, after, width=512):
    rows, ch = mine.shape
    whole = pl.BlockSpec((rows, ch), lambda j: (0, 0))
    return pl.pallas_call(
        share_kernel,
        grid=(ch // width,),
        in_specs=[whole, whole, pl.BlockSpec((2 * ch, width), lambda j: (0, j))] + [ANY] * len(after),
        out_specs=pl.BlockSpec((rows, width), lambda j: (0, j)),
        out_shape=jax.ShapeDtypeStruct((rows, ch), jnp.bfloat16),
        compiler_params=pltpu.CompilerParams(vmem_limit_bytes=VMEM_LIMIT),
        cost_estimate=cost(4 * rows * ch * ch, 4 * ch * ch + 6 * rows * ch),
        name="share_chunk",
    )(mine, other, weight, *after)


def own_kernel(count, w_ref, *rest):
    parts, outs = rest[: 2 * count], rest[-count:]
    for i in range(count):
        outs[i][...] = product(parts[2 * i][...], parts[2 * i + 1][...], w_ref[...])


def own_shares(weight, pairs, after, width=256):
    ch = weight.shape[1]
    rows = [mine.shape[0] for mine, _ in pairs]
    whole = [pl.BlockSpec((r, ch), lambda j: (0, 0)) for r in rows for _ in range(2)]
    return pl.pallas_call(
        functools.partial(own_kernel, len(pairs)),
        grid=(ch // width,),
        in_specs=[pl.BlockSpec((2 * ch, width), lambda j: (0, j)), *whole] + [ANY] * len(after),
        out_specs=[pl.BlockSpec((r, width), lambda j: (0, j)) for r in rows],
        out_shape=[jax.ShapeDtypeStruct((r, ch), jnp.float32) for r in rows],
        compiler_params=pltpu.CompilerParams(vmem_limit_bytes=VMEM_LIMIT),
        cost_estimate=cost(4 * sum(rows) * ch * ch, 4 * ch * ch + 8 * sum(rows) * ch),
        name="own_shares",
    )(weight, *[part for pair in pairs for part in pair], *after)


def finish_kernel(mine_ref, far_ref, *rest):
    out_ref = rest[-1]
    total = mine_ref[...] + far_ref[...].astype(jnp.float32)
    out_ref[...] = total.astype(out_ref.dtype).reshape(out_ref.shape)


def finish_chunk(mine, far, out, at, span, seg_len, width=512):
    rows, ch = mine.shape
    seg = rows // span
    cut = pl.BlockSpec((rows, width), lambda j: (0, j))
    operands, in_specs, aliases = [mine, far], [cut, cut], {}
    if out is not None:
        operands.append(out)
        in_specs.append(ANY)
        aliases = {2: 0}
    return pl.pallas_call(
        finish_kernel,
        grid=(ch // width,),
        in_specs=in_specs,
        out_specs=pl.BlockSpec((seg, span, width), lambda j: (0, at // span, j)),
        out_shape=jax.ShapeDtypeStruct((seg, seg_len, ch), jnp.bfloat16),
        input_output_aliases=aliases,
        compiler_params=pltpu.CompilerParams(vmem_limit_bytes=VMEM_LIMIT),
        cost_estimate=cost(rows * ch, 8 * rows * ch),
        name="finish_chunk",
    )(*operands)


def in_hbm(array):
    return pltpu.with_memory_space_constraint(array, pltpu.HBM)


def shifted(sizes, dim, hop, wrap):
    pairs = []
    total = 1
    for size in sizes:
        total *= size
    inner = 1
    for size in sizes[dim + 1 :]:
        inner *= size
    size = sizes[dim]
    for index in range(total):
        place = index // inner % size
        goal = place + hop
        if goal >= size and not wrap:
            continue
        pairs.append((index, index + (goal % size - place) * inner))
    return pairs


def carried_in(state, sent, rates, length, sizes, held):
    mine = lax.axis_index("seq")
    incoming = None
    reach = float(length)
    levels = []
    for dim in reversed(range(len(sizes))):
        size = sizes[dim]
        place = mine % size
        mine = mine // size
        wrap = dim > 0
        if sent is None:
            sent = state.astype(jnp.bfloat16)
        if dim == 0:
            sent, held = lax.optimization_barrier((sent, held))
        got = [
            lax.ppermute(sent, "seq", shifted(sizes, dim, hop, wrap)).astype(jnp.float32)
            for hop in range(1, size)
        ]
        drop = lambda blocks: jnp.exp(rates * (-reach * blocks))
        prefix = sum(
            jnp.where(hop <= place, drop(float(hop - 1)), 0.0) * part
            for hop, part in enumerate(got, 1)
        )
        sent = None
        levels.append((prefix, drop(place.astype(jnp.float32))))
        if dim > 0:
            state = state * drop((size - 1 - place).astype(jnp.float32)) + sum(
                drop((size - 1 - (place - hop) % size).astype(jnp.float32)) * part
                for hop, part in enumerate(got, 1)
            )
        reach = reach * size
    incoming = levels[-1][0]
    for prefix, fade in reversed(levels[:-1]):
        incoming = prefix + fade * incoming
    return incoming, held


def on_device(sizes, query, key, value, rates, residues, skip_gain, weight):
    tok, ch = query.shape
    seg_len = tok // SEG
    here = lax.axis_index("tp")
    chip, core = here // 2, here % 2
    weight_other = in_hbm(lax.ppermute(weight, "tp", SIBLING))
    weight = in_hbm(weight)
    last, before, sent = end_states(key, value, rates)
    weight_far, weight_near = (
        chip_columns(jnp.stack([block]).astype(jnp.int32), weight, weight_other)
        for block in (2 * (1 - chip) + core, here)
    )
    incoming, weight_far = carried_in(last, sent, rates, tok, sizes, weight_far)
    view = lambda part: part.reshape(SEG, seg_len, ch)
    query, key, value = (in_hbm(view(part)) for part in (query, key, value))
    state, extra = before, incoming
    at = 0
    parts, shares, came = [], [], []
    for i, span in enumerate(SPANS):
        after = ([shares[i - 2], came[max(i - 3, 0)]]) if i >= 2 else []
        gated, state = gate_chunk(
            query, key, value, rates, residues, skip_gain[None],
            state, extra, after, at, span,
        )
        extra = None
        other = lax.ppermute(gated, "tp", SIBLING)
        shares.append(share_chunk(gated, other, weight_far, shares[-1:]))
        came.append(lax.ppermute(shares[-1], "tp", PARTNER))
        parts.append((at, span, gated, other))
        at += span
    own = own_shares(weight_near, [part[2:4] for part in parts], [shares[-1], came[-3]])
    out = None
    for mine, far_share, (at, span, _, _) in zip(own, came, parts):
        out = finish_chunk(mine, far_share, out, at, span, seg_len)
    return out.reshape(tok, ch)


def solution(mesh):
    placed = (
        P("seq", "tp"),
        P("seq", "tp"),
        P("seq", "tp"),
        P(None, "tp"),
        P(None, "tp"),
        P("tp"),
        P("tp", None),
    )
    return jax.shard_map(
        functools.partial(on_device, (4, 4, 4)),
        mesh=mesh,
        in_specs=placed,
        out_specs=P("seq", "tp"),
        check_vma=False,
    )
```

time: 427 us -> 119 us (0.28)
  matrix products: 115 us -> 0 us
  waiting for transfers between devices: 127 us -> 29.1 us
  other arithmetic: 96.3 us -> 1.98 us
  local copies, waits for them, and re-layouts: 69 us -> 2.02 us
  Pallas kernels: 0 us -> 49.5 us
  starting transfers between devices: 0.08 us -> 35.9 us
  between operations: 13.2 us -> 0.29 us
    dot_general x5 -> x0, matrix products: 115 us -> none  [the longest x1 33.9 us: on_device(): jnp.einsum('tnc,mnc->mtc', reach_table, before_total, precision=lax.Preci...]
    reduce_scatter x1 -> x0, waiting for transfers between devices: 80.5 us -> none  [on_device(): lax.psum_scatter(partial_value.astype(jnp.bfloat16), 'tp', scatter_dimens...]
    select_n x63 -> x0, other arithmetic: 57.6 us -> none  [hop(): jnp.where(position < mine, new, old)]
    pallas_call x0 -> x19, Pallas kernels: none -> 49.5 us  [the longest x5 18.2 us: gate_chunk(): pl.pallas_call(functools.partial(gate_kernel, first, at, seg_len), grid=(...]
    all_gather x2 -> x0, waiting for transfers between devices: 46.8 us -> none  [carried_in(): pieces = jax.tree.map(lambda part: lax.all_gather(part, axis), value)]
    ppermute x0 -> x20, starting transfers between devices: none -> 35.9 us  [the longest x9 22 us: carried_in(): lax.ppermute(sent, 'seq', shifted(sizes, dim, hop, wrap))]
    ppermute x0 -> x20, waiting for transfers between devices: none -> 29.1 us  [the longest x5 22.6 us: on_device(): came.append(lax.ppermute(shares[-1], 'tp', PARTNER))]
    dynamic_update_slice x32 -> x0, other arithmetic: 20.5 us -> none  [local_pass(): lax.scan(advance, jnp.zeros_like(decay_rates), end_states)]
  transfers between devices with their start and end apart: 3 -> 20, of which waited for: 2 -> 10; matrix products, arithmetic and copies ran while one was open for 33% -> 2% of each run, Pallas kernels for 0% -> 35%
where the time goes in v1:
time: 119 us
  Pallas kernels  49.5 us (42%)
  starting transfers between devices  35.9 us (30%)
  waiting for transfers between devices  29.1 us (24%)
  local copies, waits for them, and re-layouts  2.02 us (2%)
  other arithmetic  1.98 us (2%)
    ppermute x5, waiting for transfers between devices, on_device(): came.append(lax.ppermute(shares[-1], 'tp', PARTNER))  22.6 us
    ppermute x9, starting transfers between devices, carried_in(): lax.ppermute(sent, 'seq', shifted(sizes, dim, hop, wrap))  22 us
    pallas_call x5, Pallas kernels, gate_chunk(): pl.pallas_call(functools.partial(gate_kernel, first, at, seg_len), grid=(...  18.2 us
    pallas_call x5, Pallas kernels, share_chunk(): pl.pallas_call(share_kernel, grid=(ch // width,), in_specs=[whole, whole,...  7.9 us
    pallas_call x1, Pallas kernels, end_states(): pl.pallas_call(functools.partial(end_kernel, seg_len), grid=(ch // width,...  7.64 us
    ppermute x5, starting transfers between devices, on_device(): other = lax.ppermute(gated, 'tp', SIBLING)  6.83 us
    pallas_call x1, Pallas kernels, own_shares(): pl.pallas_call(functools.partial(own_kernel, len(pairs)), grid=(ch // wid...  6.08 us
    ppermute x9, waiting for transfers between devices, carried_in(): lax.ppermute(sent, 'seq', shifted(sizes, dim, hop, wrap))  5.39 us
  transfers between devices with their start and end apart: 20, of which 10 were waited for; matrix products, arithmetic and copies ran while one was open for 2% of the time, Pallas kernels for 35%

profile of v1, /device:TPU:1, one launch (start us, length us, event | category | flops | bytes accessed | tf_op | source)
XLA Modules:
  0.0 118.8 jit_solution(468140388438882037)
XLA Ops:
  0.0 3.2 %collective-permute-start = (bf16[1024,4096]{1,0:T(8,128)(2,1)}, bf16[1024,4096]{1,0:T(8,128)(2,1)}, u32[]{:S(2)}, u32[]{:S(2)}) collective-permute-start(bf16[1024,4096]{1,0:T(8,128)(2,1)} %w_ref.3), channel_id=1, source_target_pairs={{0,1},{1,0},{2,3},{3,2},{4,5},{5,4},{6,7},{7,6},{8,9},{9,8},{10,11... | collective-permute-start | bytes 25165832 | tf_op jit(solution)/shard_map/ppermute | solution.py:325
  3.2 7.6 %end_states.1 = (f32[16,1024]{1,0:T(8,128)}, f32[128,1024]{1,0:T(8,128)}, bf16[16,1024]{1,0:T(8,128)(2,1)}) custom-call(bf16[1024,1024]{1,0:T(8,128)(2,1)} %k_ref.1, bf16[1024,1024]{1,0:T(8,128)(2,1)} %v_ref.1, f32[16,1024]{1,0:T(8,128)} %lam_ref.11), custom_call_target="tpu_custom_call" | custom-call | flops 1 | bytes 1 | tf_op jit(solution)/shard_map/end_states/pallas_call | solution.py:62
  12.1 5.1 %collective-permute-start.2 = (bf16[16,1024]{1,0:T(8,128)(2,1)}, bf16[16,1024]{1,0:T(8,128)(2,1)S(1)}, u32[]{:S(2)}, u32[]{:S(2)}) collective-permute-start(bf16[16,1024]{1,0:T(8,128)(2,1)} %get-tuple-element.25), channel_id=1, source_target_pairs={{0,8},{4,12},{8,0},{12,4},{16,24},{20,28},{24,16},{28,20},{32,40},... | collective-permute-start | bytes 98312 | tf_op jit(solution)/shard_map/ppermute | solution.py:298
  17.3 2.4 %collective-permute-start.3 = (bf16[16,1024]{1,0:T(8,128)(2,1)}, bf16[16,1024]{1,0:T(8,128)(2,1)S(1)}, u32[]{:S(2)}, u32[]{:S(2)}) collective-permute-start(bf16[16,1024]{1,0:T(8,128)(2,1)} %get-tuple-element.25), channel_id=1, source_target_pairs={{0,12},{4,0},{8,4},{12,8},{16,28},{20,16},{24,20},{28,24},{32,44},... | collective-permute-start | bytes 98312 | tf_op jit(solution)/shard_map/ppermute | solution.py:298
  19.6 2.3 %collective-permute-done.3 = bf16[16,1024]{1,0:T(8,128)(2,1)S(1)} collective-permute-done((bf16[16,1024]{1,0:T(8,128)(2,1)}, bf16[16,1024]{1,0:T(8,128)(2,1)S(1)}, u32[]{:S(2)}, u32[]{:S(2)}) %collective-permute-start.3) | collective-permute-done | bytes 32800 | tf_op jit(solution)/shard_map/ppermute | solution.py:298
  24.1 2.5 %collective-permute-start.5 = (bf16[16,1024]{1,0:T(8,128)(2,1)S(1)}, bf16[16,1024]{1,0:T(8,128)(2,1)S(1)}, u32[]{:S(2)}, u32[]{:S(2)}) collective-permute-start(bf16[16,1024]{1,0:T(8,128)(2,1)S(1)} %fusion.14), channel_id=1, source_target_pairs={{0,32},{4,36},{8,40},{12,44},{16,48},{20,52},{24,56},{28,60},{32,0... | collective-permute-start | bytes 98312 | tf_op jit(solution)/shard_map/ppermute | solution.py:298
  30.9 2.6 %chip_columns.3.w_ref = bf16[2048,1024]{1,0:T(8,128)(2,1)S(1)} custom-call(s32[1]{0:T(128)} %bitcast.5.at_ref, bf16[1024,4096]{1,0:T(8,128)(2,1)} %w_ref.3, bf16[1024,4096]{1,0:T(8,128)(2,1)} %collective-permute-done.wo_ref), custom_call_target="tpu_custom_call" | custom-call | flops 1 | bytes 1 | tf_op jit(solution)/shard_map/chip_columns/pallas_call | solution.py:170
  33.5 2.0 %copy-done = bf16[2048,1024]{1,0:T(8,128)(2,1)} copy-done((bf16[2048,1024]{1,0:T(8,128)(2,1)}, bf16[2048,1024]{1,0:T(8,128)(2,1)S(1)}, u32[]{:S(2)}) %copy-start) | copy-done | bytes 4194328
  35.5 4.6 %collective-permute-start.9 = (bf16[16,1024]{1,0:T(8,128)(2,1)S(1)}, bf16[16,1024]{1,0:T(8,128)(2,1)S(1)}, u32[]{:S(2)}, u32[]{:S(2)}) collective-permute-start(bf16[16,1024]{1,0:T(8,128)(2,1)S(1)} %fusion.13), channel_id=1, source_target_pairs={{0,192},{4,196},{8,200},{12,204},{16,208},{20,212},{24,216},{28,22... | collective-permute-start | bytes 98312 | tf_op jit(solution)/shard_map/ppermute | solution.py:298
  41.4 2.5 %collective-permute-start.7 = (bf16[16,1024]{1,0:T(8,128)(2,1)S(1)}, bf16[16,1024]{1,0:T(8,128)(2,1)S(1)}, u32[]{:S(2)}, u32[]{:S(2)}) collective-permute-start(bf16[16,1024]{1,0:T(8,128)(2,1)S(1)} %fusion.13), channel_id=1, source_target_pairs={{0,64},{4,68},{8,72},{12,76},{16,80},{20,84},{24,88},{28,92},{32,9... | collective-permute-start | bytes 98312 | tf_op jit(solution)/shard_map/ppermute | solution.py:298
  45.1 2.9 %gate_chunk.5 = (bf16[8,16,1024]{2,1,0:T(8,128)(2,1)S(1)}, f32[128,1024]{1,0:T(8,128)S(1)}) custom-call(bf16[8,128,1024]{2,1,0:T(8,128)(2,1)} %bitcast.42, bf16[8,128,1024]{2,1,0:T(8,128)(2,1)} %bitcast.32, bf16[8,128,1024]{2,1,0:T(8,128)(2,1)} %bitcast.37, f32[16,1024]{1,0:T(8,128)S(1)} %copy-done.2, f32[16,1024]{1,0:T(8,128)S(1)} %copy-done.3, ...), custom_call_target="tpu_custom_call" | custom-call | flops 1 | bytes 1 | tf_op jit(solution)/shard_map/gate_chunk/pallas_call | solution.py:143
  48.0 3.4 %collective-permute-start.10 = (bf16[128,1024]{1,0:T(8,128)(2,1)S(1)}, bf16[128,1024]{1,0:T(8,128)(2,1)S(1)}, u32[]{:S(2)}, u32[]{:S(2)}) collective-permute-start(bf16[128,1024]{1,0:T(8,128)(2,1)S(1)} %bitcast.21), channel_id=1, source_target_pairs={{0,1},{1,0},{2,3},{3,2},{4,5},{5,4},{6,7},{7,6},{8,9},{9,8},{10,11... | collective-permute-start | bytes 786440 | tf_op jit(solution)/shard_map/ppermute | solution.py:345
  54.6 2.6 %gate_chunk.6 = (bf16[8,16,1024]{2,1,0:T(8,128)(2,1)S(1)}, f32[128,1024]{1,0:T(8,128)S(1)}) custom-call(bf16[8,128,1024]{2,1,0:T(8,128)(2,1)} %bitcast.43, bf16[8,128,1024]{2,1,0:T(8,128)(2,1)} %bitcast.33, bf16[8,128,1024]{2,1,0:T(8,128)(2,1)} %bitcast.38, f32[16,1024]{1,0:T(8,128)S(1)} %copy-done.2, f32[16,1024]{1,0:T(8,128)S(1)} %copy-done.3, ...), custom_call_target="tpu_custom_call" | custom-call | flops 1 | bytes 1 | tf_op jit(solution)/shard_map/gate_chunk/pallas_call | solution.py:143
  58.0 3.5 %collective-permute-done.12.rest_1_.far_ref = bf16[128,1024]{1,0:T(8,128)(2,1)S(1)} collective-permute-done((bf16[128,1024]{1,0:T(8,128)(2,1)S(1)}, bf16[128,1024]{1,0:T(8,128)(2,1)S(1)}, u32[]{:S(2)}, u32[]{:S(2)}) %collective-permute-start.12) | collective-permute-done | bytes 262176 | tf_op jit(solution)/shard_map/ppermute | solution.py:347
  61.5 4.0 %gate_chunk.7 = (bf16[8,32,1024]{2,1,0:T(8,128)(2,1)S(1)}, f32[128,1024]{1,0:T(8,128)S(1)}) custom-call(bf16[8,128,1024]{2,1,0:T(8,128)(2,1)} %bitcast.44, bf16[8,128,1024]{2,1,0:T(8,128)(2,1)} %bitcast.34, bf16[8,128,1024]{2,1,0:T(8,128)(2,1)} %bitcast.39, f32[16,1024]{1,0:T(8,128)S(1)} %copy-done.2, f32[16,1024]{1,0:T(8,128)S(1)} %copy-done.3, ...), custom_call_target="tpu_custom_call" | custom-call | flops 1 | bytes 1 | tf_op jit(solution)/shard_map/gate_chunk/pallas_call | solution.py:143
  69.0 4.0 %gate_chunk.8 = (bf16[8,32,1024]{2,1,0:T(8,128)(2,1)S(1)}, f32[128,1024]{1,0:T(8,128)S(1)}) custom-call(bf16[8,128,1024]{2,1,0:T(8,128)(2,1)} %bitcast.45, bf16[8,128,1024]{2,1,0:T(8,128)(2,1)} %bitcast.35, bf16[8,128,1024]{2,1,0:T(8,128)(2,1)} %bitcast.40, f32[16,1024]{1,0:T(8,128)S(1)} %copy-done.2, f32[16,1024]{1,0:T(8,128)S(1)} %copy-done.3, ...), custom_call_target="tpu_custom_call" | custom-call | flops 1 | bytes 1 | tf_op jit(solution)/shard_map/gate_chunk/pallas_call | solution.py:143
  73.5 1.8 %share_chunk.7.rest_0_ = bf16[256,1024]{1,0:T(8,128)(2,1)S(1)} custom-call(bf16[256,1024]{1,0:T(8,128)(2,1)S(1)} %bitcast.13, bf16[256,1024]{1,0:T(8,128)(2,1)S(1)} %collective-permute-done.13.other_ref.rest_5_, bf16[2048,1024]{1,0:T(8,128)(2,1)S(1)} %copy-done.1, bf16[128,1024]{1,0:T(8,128)(2,1)S(1)} %share_chunk.6.rest_0_), custom_call_target="tpu_custom_call" | custom-call | flops 1 | bytes 1 | tf_op jit(solution)/shard_map/share_chunk/pallas_call | solution.py:199
  76.3 4.7 %gate_chunk.9 = (bf16[8,32,1024]{2,1,0:T(8,128)(2,1)S(1)}, f32[128,1024]{1,0:T(8,128)}) custom-call(bf16[8,128,1024]{2,1,0:T(8,128)(2,1)} %bitcast.46, bf16[8,128,1024]{2,1,0:T(8,128)(2,1)} %bitcast.36, bf16[8,128,1024]{2,1,0:T(8,128)(2,1)} %bitcast.41, f32[16,1024]{1,0:T(8,128)S(1)} %copy-done.2, f32[16,1024]{1,0:T(8,128)S(1)} %copy-done.3, ...), custom_call_target="tpu_custom_call" | custom-call | flops 1 | bytes 1 | tf_op jit(solution)/shard_map/gate_chunk/pallas_call | solution.py:143
  85.1 1.8 %share_chunk.9.rest_10_ = bf16[256,1024]{1,0:T(8,128)(2,1)S(1)} custom-call(bf16[256,1024]{1,0:T(8,128)(2,1)S(1)} %bitcast.19, bf16[256,1024]{1,0:T(8,128)(2,1)S(1)} %collective-permute-done.16.other_ref.rest_9_, bf16[2048,1024]{1,0:T(8,128)(2,1)S(1)} %copy-done.1, bf16[256,1024]{1,0:T(8,128)(2,1)S(1)} %share_chunk.8.rest_0_), custom_call_target="tpu_custom_call" | custom-call | flops 1 | bytes 1 | tf_op jit(solution)/shard_map/share_chunk/pallas_call | solution.py:199
  87.6 2.5 %chip_columns.2.w_ref = bf16[2048,1024]{1,0:T(8,128)(2,1)S(1)} custom-call(s32[1]{0:T(128)} %bitcast.at_ref, bf16[1024,4096]{1,0:T(8,128)(2,1)} %w_ref.3, bf16[1024,4096]{1,0:T(8,128)(2,1)} %collective-permute-done.wo_ref), custom_call_target="tpu_custom_call" | custom-call | flops 1 | bytes 1 | tf_op jit(solution)/shard_map/chip_columns/pallas_call | solution.py:170
  90.1 5.2 %collective-permute-done.17.rest_11_.far_ref = bf16[256,1024]{1,0:T(8,128)(2,1)S(1)} collective-permute-done((bf16[256,1024]{1,0:T(8,128)(2,1)S(1)}, bf16[256,1024]{1,0:T(8,128)(2,1)S(1)}, u32[]{:S(2)}, u32[]{:S(2)}) %collective-permute-start.17) | collective-permute-done | bytes 524320 | tf_op jit(solution)/shard_map/ppermute | solution.py:347
  95.3 6.1 %own_shares.1 = (f32[128,1024]{1,0:T(8,128)S(1)}, f32[128,1024]{1,0:T(8,128)S(1)}, f32[256,1024]{1,0:T(8,128)S(1)}, f32[256,1024]{1,0:T(8,128)S(1)}, f32[256,1024]{1,0:T(8,128)S(1)}) custom-call(bf16[2048,1024]{1,0:T(8,128)(2,1)S(1)} %chip_columns.2.w_ref, bf16[128,1024]{1,0:T(8,128)(2,1)S(1)} %bitcast.23, ...), custom_call_target="tpu_custom_call" | custom-call | flops 1 | bytes 1 | tf_op jit(solution)/shard_map/own_shares/pallas_call | solution.py:221
  104.0 2.6 %collective-permute-done.19.far_ref = bf16[256,1024]{1,0:T(8,128)(2,1)S(1)} collective-permute-done((bf16[256,1024]{1,0:T(8,128)(2,1)S(1)}, bf16[256,1024]{1,0:T(8,128)(2,1)S(1)}, u32[]{:S(2)}, u32[]{:S(2)}) %collective-permute-start.19) | collective-permute-done | bytes 524320 | tf_op jit(solution)/shard_map/ppermute | solution.py:347
  107.5 10.3 %collective-permute-done.18.far_ref = bf16[256,1024]{1,0:T(8,128)(2,1)S(1)} collective-permute-done((bf16[256,1024]{1,0:T(8,128)(2,1)S(1)}, bf16[256,1024]{1,0:T(8,128)(2,1)S(1)}, u32[]{:S(2)}, u32[]{:S(2)}) %collective-permute-start.18) | collective-permute-done | bytes 524320 | tf_op jit(solution)/shard_map/ppermute | solution.py:347
  (50 shorter events, 28.3 us)
Async XLA Ops:
  0.0 21.9 %copy-start.2 = (f32[16,1024]{1,0:T(8,128)S(1)}, f32[16,1024]{1,0:T(8,128)}, u32[]{:S(2)}) copy-start(f32[16,1024]{1,0:T(8,128)} %lam_ref.11) | copy-start | bytes 196612
  0.0 30.8 %collective-permute-start = (bf16[1024,4096]{1,0:T(8,128)(2,1)}, bf16[1024,4096]{1,0:T(8,128)(2,1)}, u32[]{:S(2)}, u32[]{:S(2)}) collective-permute-start(bf16[1024,4096]{1,0:T(8,128)(2,1)} %w_ref.3), channel_id=1, source_target_pairs={{0,1},{1,0},{2,3},{3,2},{4,5},{5,4},{6,7},{7,6},{8,9},{9,8},{10,11... | collective-permute-start | bytes 25165832 | tf_op jit(solution)/shard_map/ppermute | solution.py:325
  10.9 8.8 %collective-permute-start.1 = (bf16[16,1024]{1,0:T(8,128)(2,1)}, bf16[16,1024]{1,0:T(8,128)(2,1)S(1)}, u32[]{:S(2)}, u32[]{:S(2)}) collective-permute-start(bf16[16,1024]{1,0:T(8,128)(2,1)} %get-tuple-element.25), channel_id=1, source_target_pairs={{0,4},{4,8},{8,12},{12,0},{16,20},{20,24},{24,28},{28,16},{32,36},... | collective-permute-start | bytes 98312 | tf_op jit(solution)/shard_map/ppermute | solution.py:298
  12.1 7.5 %collective-permute-start.2 = (bf16[16,1024]{1,0:T(8,128)(2,1)}, bf16[16,1024]{1,0:T(8,128)(2,1)S(1)}, u32[]{:S(2)}, u32[]{:S(2)}) collective-permute-start(bf16[16,1024]{1,0:T(8,128)(2,1)} %get-tuple-element.25), channel_id=1, source_target_pairs={{0,8},{4,12},{8,0},{12,4},{16,24},{20,28},{24,16},{28,20},{32,40},... | collective-permute-start | bytes 98312 | tf_op jit(solution)/shard_map/ppermute | solution.py:298
  17.3 4.7 %collective-permute-start.3 = (bf16[16,1024]{1,0:T(8,128)(2,1)}, bf16[16,1024]{1,0:T(8,128)(2,1)S(1)}, u32[]{:S(2)}, u32[]{:S(2)}) collective-permute-start(bf16[16,1024]{1,0:T(8,128)(2,1)} %get-tuple-element.25), channel_id=1, source_target_pairs={{0,12},{4,0},{8,4},{12,8},{16,28},{20,16},{24,20},{28,24},{32,44},... | collective-permute-start | bytes 98312 | tf_op jit(solution)/shard_map/ppermute | solution.py:298
  22.8 4.9 %collective-permute-start.4 = (bf16[16,1024]{1,0:T(8,128)(2,1)S(1)}, bf16[16,1024]{1,0:T(8,128)(2,1)S(1)}, u32[]{:S(2)}, u32[]{:S(2)}) collective-permute-start(bf16[16,1024]{1,0:T(8,128)(2,1)S(1)} %fusion.14), channel_id=1, source_target_pairs={{0,16},{4,20},{8,24},{12,28},{16,32},{20,36},{24,40},{28,44},{32,4... | collective-permute-start | bytes 98312 | tf_op jit(solution)/shard_map/ppermute | solution.py:298
  24.1 4.4 %collective-permute-start.5 = (bf16[16,1024]{1,0:T(8,128)(2,1)S(1)}, bf16[16,1024]{1,0:T(8,128)(2,1)S(1)}, u32[]{:S(2)}, u32[]{:S(2)}) collective-permute-start(bf16[16,1024]{1,0:T(8,128)(2,1)S(1)} %fusion.14), channel_id=1, source_target_pairs={{0,32},{4,36},{8,40},{12,44},{16,48},{20,52},{24,56},{28,60},{32,0... | collective-permute-start | bytes 98312 | tf_op jit(solution)/shard_map/ppermute | solution.py:298
  26.6 3.3 %collective-permute-start.6 = (bf16[16,1024]{1,0:T(8,128)(2,1)S(1)}, bf16[16,1024]{1,0:T(8,128)(2,1)S(1)}, u32[]{:S(2)}, u32[]{:S(2)}) collective-permute-start(bf16[16,1024]{1,0:T(8,128)(2,1)S(1)} %fusion.14), channel_id=1, source_target_pairs={{0,48},{4,52},{8,56},{12,60},{16,0},{20,4},{24,8},{28,12},{32,16},... | collective-permute-start | bytes 98312 | tf_op jit(solution)/shard_map/ppermute | solution.py:298
  30.8 14.2 %copy-start.3 = (f32[16,1024]{1,0:T(8,128)S(1)}, f32[16,1024]{1,0:T(8,128)}, u32[]{:S(2)}) copy-start(f32[16,1024]{1,0:T(8,128)} %res_ref.9) | copy-start | bytes 196612
  30.9 14.2 %copy-start.4 = (f32[128,1024]{1,0:T(8,128)S(1)}, f32[128,1024]{1,0:T(8,128)}, u32[]{:S(2)}) copy-start(f32[128,1024]{1,0:T(8,128)} %get-tuple-element.24.state_ref) | copy-start | bytes 1572868
  30.9 14.2 %copy-start.5 = (f32[1024]{0:T(1024)S(1)}, f32[1024]{0:T(1024)}, u32[]{:S(2)}) copy-start(f32[1024]{0:T(1024)} %param.12) | copy-start | bytes 12292
  35.5 8.5 %collective-permute-start.9 = (bf16[16,1024]{1,0:T(8,128)(2,1)S(1)}, bf16[16,1024]{1,0:T(8,128)(2,1)S(1)}, u32[]{:S(2)}, u32[]{:S(2)}) collective-permute-start(bf16[16,1024]{1,0:T(8,128)(2,1)S(1)} %fusion.13), channel_id=1, source_target_pairs={{0,192},{4,196},{8,200},{12,204},{16,208},{20,212},{24,216},{28,22... | collective-permute-start | bytes 98312 | tf_op jit(solution)/shard_map/ppermute | solution.py:298
  40.1 3.9 %collective-permute-start.8 = (bf16[16,1024]{1,0:T(8,128)(2,1)S(1)}, bf16[16,1024]{1,0:T(8,128)(2,1)S(1)}, u32[]{:S(2)}, u32[]{:S(2)}) collective-permute-start(bf16[16,1024]{1,0:T(8,128)(2,1)S(1)} %fusion.13), channel_id=1, source_target_pairs={{0,128},{4,132},{8,136},{12,140},{16,144},{20,148},{24,152},{28,15... | collective-permute-start | bytes 98312 | tf_op jit(solution)/shard_map/ppermute | solution.py:298
  41.4 3.5 %collective-permute-start.7 = (bf16[16,1024]{1,0:T(8,128)(2,1)S(1)}, bf16[16,1024]{1,0:T(8,128)(2,1)S(1)}, u32[]{:S(2)}, u32[]{:S(2)}) collective-permute-start(bf16[16,1024]{1,0:T(8,128)(2,1)S(1)} %fusion.13), channel_id=1, source_target_pairs={{0,64},{4,68},{8,72},{12,76},{16,80},{20,84},{24,88},{28,92},{32,9... | collective-permute-start | bytes 98312 | tf_op jit(solution)/shard_map/ppermute | solution.py:298
  48.0 4.6 %collective-permute-start.10 = (bf16[128,1024]{1,0:T(8,128)(2,1)S(1)}, bf16[128,1024]{1,0:T(8,128)(2,1)S(1)}, u32[]{:S(2)}, u32[]{:S(2)}) collective-permute-start(bf16[128,1024]{1,0:T(8,128)(2,1)S(1)} %bitcast.21), channel_id=1, source_target_pairs={{0,1},{1,0},{2,3},{3,2},{4,5},{5,4},{6,7},{7,6},{8,9},{9,8},{10,11... | collective-permute-start | bytes 786440 | tf_op jit(solution)/shard_map/ppermute | solution.py:345
  53.9 7.6 %collective-permute-start.12 = (bf16[128,1024]{1,0:T(8,128)(2,1)S(1)}, bf16[128,1024]{1,0:T(8,128)(2,1)S(1)}, u32[]{:S(2)}, u32[]{:S(2)}) collective-permute-start(bf16[128,1024]{1,0:T(8,128)(2,1)S(1)} %share_chunk.5.rest_0_), channel_id=1, source_target_pairs={{0,2},{2,0},{1,3},{3,1},{4,6},{6,4},{5,7},{7,5},{8,10},{10,8},{9,1... | collective-permute-start | bytes 786440 | tf_op jit(solution)/shard_map/ppermute | solution.py:347
  57.2 9.8 %collective-permute-start.11 = (bf16[128,1024]{1,0:T(8,128)(2,1)S(1)}, bf16[128,1024]{1,0:T(8,128)(2,1)S(1)}, u32[]{:S(2)}, u32[]{:S(2)}) collective-permute-start(bf16[128,1024]{1,0:T(8,128)(2,1)S(1)} %bitcast.24), channel_id=1, source_target_pairs={{0,1},{1,0},{2,3},{3,2},{4,5},{5,4},{6,7},{7,6},{8,9},{9,8},{10,11... | collective-permute-start | bytes 786440 | tf_op jit(solution)/shard_map/ppermute | solution.py:345
  65.6 7.9 %collective-permute-start.13 = (bf16[256,1024]{1,0:T(8,128)(2,1)S(1)}, bf16[256,1024]{1,0:T(8,128)(2,1)S(1)}, u32[]{:S(2)}, u32[]{:S(2)}) collective-permute-start(bf16[256,1024]{1,0:T(8,128)(2,1)S(1)} %bitcast.12), channel_id=1, source_target_pairs={{0,1},{1,0},{2,3},{3,2},{4,5},{5,4},{6,7},{7,6},{8,9},{9,8},{10,11... | collective-permute-start | bytes 1572872 | tf_op jit(solution)/shard_map/ppermute | solution.py:345
  68.3 8.0 %collective-permute-start.15 = (bf16[128,1024]{1,0:T(8,128)(2,1)S(1)}, bf16[128,1024]{1,0:T(8,128)(2,1)S(1)}, u32[]{:S(2)}, u32[]{:S(2)}) collective-permute-start(bf16[128,1024]{1,0:T(8,128)(2,1)S(1)} %share_chunk.6.rest_0_), channel_id=1, source_target_pairs={{0,2},{2,0},{1,3},{3,1},{4,6},{6,4},{5,7},{7,5},{8,10},{10,8},{9,1... | collective-permute-start | bytes 786440 | tf_op jit(solution)/shard_map/ppermute | solution.py:347
  73.0 9.4 %collective-permute-start.14 = (bf16[256,1024]{1,0:T(8,128)(2,1)S(1)}, bf16[256,1024]{1,0:T(8,128)(2,1)S(1)}, u32[]{:S(2)}, u32[]{:S(2)}) collective-permute-start(bf16[256,1024]{1,0:T(8,128)(2,1)S(1)} %bitcast.15), channel_id=1, source_target_pairs={{0,1},{1,0},{2,3},{3,2},{4,5},{5,4},{6,7},{7,6},{8,9},{9,8},{10,11... | collective-permute-start | bytes 1572872 | tf_op jit(solution)/shard_map/ppermute | solution.py:345
  81.0 4.1 %collective-permute-start.16 = (bf16[256,1024]{1,0:T(8,128)(2,1)S(1)}, bf16[256,1024]{1,0:T(8,128)(2,1)S(1)}, u32[]{:S(2)}, u32[]{:S(2)}) collective-permute-start(bf16[256,1024]{1,0:T(8,128)(2,1)S(1)} %bitcast.18), channel_id=1, source_target_pairs={{0,1},{1,0},{2,3},{3,2},{4,5},{5,4},{6,7},{7,6},{8,9},{9,8},{10,11... | collective-permute-start | bytes 1572872 | tf_op jit(solution)/shard_map/ppermute | solution.py:345
  81.8 13.6 %collective-permute-start.17 = (bf16[256,1024]{1,0:T(8,128)(2,1)S(1)}, bf16[256,1024]{1,0:T(8,128)(2,1)S(1)}, u32[]{:S(2)}, u32[]{:S(2)}) collective-permute-start(bf16[256,1024]{1,0:T(8,128)(2,1)S(1)} %share_chunk.7.rest_0_), channel_id=1, source_target_pairs={{0,2},{2,0},{1,3},{3,1},{4,6},{6,4},{5,7},{7,5},{8,10},{10,8},{9,1... | collective-permute-start | bytes 1572872 | tf_op jit(solution)/shard_map/ppermute | solution.py:347
  84.2 22.4 %collective-permute-start.19 = (bf16[256,1024]{1,0:T(8,128)(2,1)S(1)}, bf16[256,1024]{1,0:T(8,128)(2,1)S(1)}, u32[]{:S(2)}, u32[]{:S(2)}) collective-permute-start(bf16[256,1024]{1,0:T(8,128)(2,1)S(1)} %share_chunk.8.rest_0_), channel_id=1, source_target_pairs={{0,2},{2,0},{1,3},{3,1},{4,6},{6,4},{5,7},{7,5},{8,10},{10,8},{9,1... | collective-permute-start | bytes 1572872 | tf_op jit(solution)/shard_map/ppermute | solution.py:347
  86.9 30.9 %collective-permute-start.18 = (bf16[256,1024]{1,0:T(8,128)(2,1)S(1)}, bf16[256,1024]{1,0:T(8,128)(2,1)S(1)}, u32[]{:S(2)}, u32[]{:S(2)}) collective-permute-start(bf16[256,1024]{1,0:T(8,128)(2,1)S(1)} %share_chunk.9.rest_10_), channel_id=1, source_target_pairs={{0,2},{2,0},{1,3},{3,1},{4,6},{6,4},{5,7},{7,5},{8,10},{10,8},{9,1... | collective-permute-start | bytes 1572872 | tf_op jit(solution)/shard_map/ppermute | solution.py:347
  (2 other events, 9.5 us)

commit v2 on v1

--- a/solution.py
+++ b/solution.py
@@ -9,9 +9,9 @@
 
 SEG = 8
 LANES = 128
-SPANS = (16, 16, 32, 32, 32)
+SPANS = (32, 32, 32, 32)
+PIECE = 64
 VMEM_LIMIT = 32 * 2**20
-VMEM_ALL = 60 * 2**20
 SIBLING = [(0, 1), (1, 0), (2, 3), (3, 2)]
 PARTNER = [(0, 2), (2, 0), (1, 3), (3, 1)]
 ANY = pl.BlockSpec(memory_space=pl.ANY)
@@ -70,18 +70,20 @@
             jax.ShapeDtypeStruct((order, ch), jnp.bfloat16),
         ],
         scratch_shapes=[pltpu.VMEM((SEG * (seg_len + 1), LANES), jnp.float32)],
-        compiler_params=pltpu.CompilerParams(vmem_limit_bytes=VMEM_ALL),
+        compiler_params=pltpu.CompilerParams(vmem_limit_bytes=VMEM_LIMIT),
         cost_estimate=cost(2 * tok * ch * order, 4 * tok * ch),
         name="end_states",
     )(key, value, rates)
 
 
 def gate_kernel(first, late, seg_len, q_ref, k_ref, v_ref, lam_ref, res_ref, skip_ref, state_ref, *rest):
-    g_ref, next_ref, x_ref, y_ref = rest[-4:]
+    next_ref, x_ref, y_ref = rest[-3:]
     if first:
         inc_ref = rest[0]
     order = lam_ref.shape[0]
     span = q_ref.shape[1]
+    held = PIECE // span
+    g_refs = rest[-3 - SEG // held : -3]
     pitch = span + 1
     for group in range(q_ref.shape[2] // LANES):
         cols = slice(group * LANES, (group + 1) * LANES)
@@ -121,15 +123,16 @@
         for seg in range(SEG):
             rows = pl.ds(seg * pitch, span)
             gate = q_ref[seg, :, cols].astype(jnp.float32) * (y_ref[rows, :] + skip * x_ref[rows, :])
-            g_ref[seg, :, cols] = gate.astype(jnp.bfloat16)
+            g_refs[seg // held][seg % held, :, cols] = gate.astype(jnp.bfloat16)
 
 
 def gate_chunk(
-    query, key, value, rates, residues, skip, state, incoming, after, at, span, width=512
+    query, key, value, rates, residues, skip, state, incoming, after, at, span, width=None
 ):
     seg, seg_len, ch = query.shape
     order = rates.shape[0]
     first = incoming is not None
+    width = width or (512 if span <= 16 else 256)
     part = pl.BlockSpec((seg, span, width), lambda j: (0, at // span, j))
     cut = lambda rows: pl.BlockSpec((rows, width), lambda j: (0, j))
     operands = [query, key, value, rates, residues, skip, state]
@@ -140,13 +143,16 @@
     operands.extend(after)
     in_specs.extend([ANY] * len(after))
     rows = seg * span
-    gated, state = pl.pallas_call(
+    held = PIECE // span
+    count = seg // held
+    *gated, state = pl.pallas_call(
         functools.partial(gate_kernel, first, at, seg_len),
         grid=(ch // width,),
         in_specs=in_specs,
-        out_specs=[pl.BlockSpec((seg, span, width), lambda j: (0, 0, j)), cut(order * seg)],
-        out_shape=[
-            jax.ShapeDtypeStruct((seg, span, ch), jnp.bfloat16),
+        out_specs=[pl.BlockSpec((held, span, width), lambda j: (0, 0, j))] * count
+        + [cut(order * seg)],
+        out_shape=[jax.ShapeDtypeStruct((held, span, ch), jnp.bfloat16)] * count
+        + [
             jax.ShapeDtypeStruct((order * seg, ch), jnp.float32),
         ],
         scratch_shapes=[pltpu.VMEM((seg * (span + 1), LANES), jnp.float32)] * 2,
@@ -154,16 +160,17 @@
         cost_estimate=cost(4 * rows * ch * order, 8 * rows * ch + 8 * order * seg * ch),
         name="gate_chunk",
     )(*operands)
-    return gated.reshape(rows, ch), state
-
-
-def columns_kernel(at_ref, w_ref, wo_ref, out_ref):
+    return [piece.reshape(PIECE, ch) for piece in gated], state
+
+
+def columns_kernel(at_ref, w_ref, wo_ref, out_ref, mark_ref):
+    mark_ref[...] = jnp.zeros_like(mark_ref)
     depth = w_ref.shape[0]
     out_ref[:depth] = w_ref[...]
     out_ref[depth:] = wo_ref[...]
 
 
-def chip_columns(block, weight, weight_other, width=512):
+def chip_columns(block, weight, weight_other, order, width=512):
     ch = weight.shape[0]
     per = ch // width
     part = pl.BlockSpec((ch, width), lambda j, at: (0, at[0] * per + j))
@@ -173,61 +180,87 @@
             num_scalar_prefetch=1,
             grid=(per,),
             in_specs=[part, part],
-            out_specs=pl.BlockSpec((2 * ch, width), lambda j, at: (0, j)),
+            out_specs=[
+                pl.BlockSpec((2 * ch, width), lambda j, at: (0, j)),
+                pl.BlockSpec((order, width), lambda j, at: (0, j)),
+            ],
         ),
-        out_shape=jax.ShapeDtypeStruct((2 * ch, ch), weight.dtype),
+        out_shape=[
+            pltpu.HBM((2 * ch, ch), weight.dtype),
+            jax.ShapeDtypeStruct((order, ch), jnp.float32),
+        ],
         compiler_params=pltpu.CompilerParams(vmem_limit_bytes=VMEM_LIMIT),
         cost_estimate=cost(0, 8 * ch * ch),
         name="chip_columns",
     )(block, weight, weight_other)
 
 
-def product(mine, other, weight):
-    depth = weight.shape[0] // 2
-    total = jnp.dot(mine, weight[:depth], preferred_element_type=jnp.float32)
-    return total + jnp.dot(other, weight[depth:], preferred_element_type=jnp.float32)
-
-
-def share_kernel(mine_ref, other_ref, w_ref, *rest):
+def gathered(pieces):
+    return jnp.concatenate([piece[...] for piece in pieces], axis=0)
+
+
+def product(mine, other, weight, weight_other):
+    total = jnp.dot(gathered(mine), weight, preferred_element_type=jnp.float32)
+    return total + jnp.dot(gathered(other), weight_other, preferred_element_type=jnp.float32)
+
+
+def share_kernel(count, w_ref, *rest):
     out_ref = rest[-1]
-    out_ref[...] = product(mine_ref[...], other_ref[...], w_ref[...]).astype(out_ref.dtype)
+    depth = w_ref.shape[0] // 2
+    total = product(rest[:count], rest[count : 2 * count], w_ref[:depth], w_ref[depth:])
+    out_ref[...] = total.astype(out_ref.dtype)
 
 
 def share_chunk(mine, other, weight, after, width=512):
-    rows, ch = mine.shape
-    whole = pl.BlockSpec((rows, ch), lambda j: (0, 0))
+    count = len(mine)
+    ch = weight.shape[1]
+    rows = count * PIECE
     return pl.pallas_call(
-        share_kernel,
+        functools.partial(share_kernel, count),
         grid=(ch // width,),
-        in_specs=[whole, whole, pl.BlockSpec((2 * ch, width), lambda j: (0, j))] + [ANY] * len(after),
+        in_specs=[pl.BlockSpec((2 * ch, width), lambda j: (0, j))]
+        + [pl.BlockSpec((PIECE, ch), lambda j: (0, 0))] * (2 * count)
+        + [ANY] * len(after),
         out_specs=pl.BlockSpec((rows, width), lambda j: (0, j)),
         out_shape=jax.ShapeDtypeStruct((rows, ch), jnp.bfloat16),
         compiler_params=pltpu.CompilerParams(vmem_limit_bytes=VMEM_LIMIT),
         cost_estimate=cost(4 * rows * ch * ch, 4 * ch * ch + 6 * rows * ch),
         name="share_chunk",
-    )(mine, other, weight, *after)
-
-
-def own_kernel(count, w_ref, *rest):
-    parts, outs = rest[: 2 * count], rest[-count:]
-    for i in range(count):
-        outs[i][...] = product(parts[2 * i][...], parts[2 * i + 1][...], w_ref[...])
-
-
-def own_shares(weight, pairs, after, width=256):
-    ch = weight.shape[1]
-    rows = [mine.shape[0] for mine, _ in pairs]
-    whole = [pl.BlockSpec((r, ch), lambda j: (0, 0)) for r in rows for _ in range(2)]
+    )(weight, *mine, *other, *after)
+
+
+def own_kernel(counts, at_ref, w_ref, wo_ref, *rest):
+    outs = rest[-len(counts) :]
+    at = 0
+    for count, out_ref in zip(counts, outs):
+        out_ref[...] = product(
+            rest[at : at + count], rest[at + count : at + 2 * count], w_ref[...], wo_ref[...]
+        )
+        at += 2 * count
+
+
+def own_shares(block, weight, weight_other, pairs, after, width=256):
+    ch = weight.shape[0]
+    per = ch // width
+    counts = [len(mine) for mine, _ in pairs]
+    pieces = [piece for mine, other in pairs for piece in [*mine, *other]]
+    rows = [count * PIECE for count in counts]
+    columns = pl.BlockSpec((ch, width), lambda j, at: (0, at[0] * per + j))
     return pl.pallas_call(
-        functools.partial(own_kernel, len(pairs)),
-        grid=(ch // width,),
-        in_specs=[pl.BlockSpec((2 * ch, width), lambda j: (0, j)), *whole] + [ANY] * len(after),
-        out_specs=[pl.BlockSpec((r, width), lambda j: (0, j)) for r in rows],
+        functools.partial(own_kernel, counts),
+        grid_spec=pltpu.PrefetchScalarGridSpec(
+            num_scalar_prefetch=1,
+            grid=(per,),
+            in_specs=[columns, columns]
+            + [pl.BlockSpec((PIECE, ch), lambda j, at: (0, 0))] * len(pieces)
+            + [ANY] * len(after),
+            out_specs=[pl.BlockSpec((r, width), lambda j, at: (0, j)) for r in rows],
+        ),
         out_shape=[jax.ShapeDtypeStruct((r, ch), jnp.float32) for r in rows],
         compiler_params=pltpu.CompilerParams(vmem_limit_bytes=VMEM_LIMIT),
         cost_estimate=cost(4 * sum(rows) * ch * ch, 4 * ch * ch + 8 * sum(rows) * ch),
         name="own_shares",
-    )(weight, *[part for pair in pairs for part in pair], *after)
+    )(block, weight, weight_other, *pieces, *after)
 
 
 def finish_kernel(mine_ref, far_ref, *rest):
@@ -280,41 +313,43 @@
     return pairs
 
 
-def carried_in(state, sent, rates, length, sizes, held):
+def carried_in(state, sent, rates, length, sizes, marks):
     mine = lax.axis_index("seq")
-    incoming = None
-    reach = float(length)
+    fade = jnp.exp(rates * (-float(length)))
     levels = []
     for dim in reversed(range(len(sizes))):
         size = sizes[dim]
         place = mine % size
         mine = mine // size
-        wrap = dim > 0
-        if sent is None:
-            sent = state.astype(jnp.bfloat16)
-        if dim == 0:
-            sent, held = lax.optimization_barrier((sent, held))
         got = [
-            lax.ppermute(sent, "seq", shifted(sizes, dim, hop, wrap)).astype(jnp.float32)
+            lax.ppermute(sent, "seq", shifted(sizes, dim, hop, True))
             for hop in range(1, size)
         ]
-        drop = lambda blocks: jnp.exp(rates * (-reach * blocks))
+        got = [part.astype(jnp.float32) for part in got]
+        if dim in marks:
+            got = [part + marks[dim] for part in got]
+        powers = [jnp.ones_like(fade), fade]
+        while len(powers) <= size:
+            powers.append(powers[-1] * fade)
+
+        def power(exponent):
+            return sum(jnp.where(exponent == i, powers[i], 0.0) for i in range(size))
+
         prefix = sum(
-            jnp.where(hop <= place, drop(float(hop - 1)), 0.0) * part
+            jnp.where(hop <= place, powers[hop - 1], 0.0) * part
             for hop, part in enumerate(got, 1)
         )
-        sent = None
-        levels.append((prefix, drop(place.astype(jnp.float32))))
+        levels.append((prefix, power(place)))
         if dim > 0:
-            state = state * drop((size - 1 - place).astype(jnp.float32)) + sum(
-                drop((size - 1 - (place - hop) % size).astype(jnp.float32)) * part
-                for hop, part in enumerate(got, 1)
+            state = state * power(size - 1 - place) + sum(
+                power(size - 1 - (place - hop) % size) * part for hop, part in enumerate(got, 1)
             )
-        reach = reach * size
+            sent = state.astype(jnp.bfloat16)
+        fade = powers[size]
     incoming = levels[-1][0]
-    for prefix, fade in reversed(levels[:-1]):
-        incoming = prefix + fade * incoming
-    return incoming, held
+    for prefix, drop in reversed(levels[:-1]):
+        incoming = prefix + drop * incoming
+    return incoming
 
 
 def on_device(sizes, query, key, value, rates, residues, skip_gain, weight):
@@ -324,32 +359,47 @@
     chip, core = here // 2, here % 2
     weight_other = in_hbm(lax.ppermute(weight, "tp", SIBLING))
     weight = in_hbm(weight)
-    last, before, sent = end_states(key, value, rates)
-    weight_far, weight_near = (
-        chip_columns(jnp.stack([block]).astype(jnp.int32), weight, weight_other)
-        for block in (2 * (1 - chip) + core, here)
-    )
-    incoming, weight_far = carried_in(last, sent, rates, tok, sizes, weight_far)
+    last, before, sent = end_states(in_hbm(key), in_hbm(value), rates)
+    block = jnp.stack([2 * (1 - chip) + core]).astype(jnp.int32)
+    weight_far, far_mark = chip_columns(block, weight, weight_other, rates.shape[0])
+    incoming = carried_in(last, sent, rates, tok, sizes, {1: far_mark})
     view = lambda part: part.reshape(SEG, seg_len, ch)
     query, key, value = (in_hbm(view(part)) for part in (query, key, value))
     state, extra = before, incoming
     at = 0
     parts, shares, came = [], [], []
-    for i, span in enumerate(SPANS):
-        after = ([shares[i - 2], came[max(i - 3, 0)]]) if i >= 2 else []
+    gates, others = [], []
+
+    def gate(i, after):
+        nonlocal state, extra, at
         gated, state = gate_chunk(
             query, key, value, rates, residues, skip_gain[None],
-            state, extra, after, at, span,
+            state, extra, after, at, SPANS[i],
         )
         extra = None
-        other = lax.ppermute(gated, "tp", SIBLING)
-        shares.append(share_chunk(gated, other, weight_far, shares[-1:]))
+        gates.append(gated)
+        others.append([lax.ppermute(piece, "tp", SIBLING) for piece in gated])
+        parts.append((at, SPANS[i]))
+        at += SPANS[i]
+
+    def share(i, after):
+        shares.append(share_chunk(gates[i], others[i], weight_far, after))
         came.append(lax.ppermute(shares[-1], "tp", PARTNER))
-        parts.append((at, span, gated, other))
-        at += span
-    own = own_shares(weight_near, [part[2:4] for part in parts], [shares[-1], came[-3]])
+
+    gate(0, [])
+    share(0, [])
+    gate(1, [shares[0]])
+    share(1, [shares[0]])
+    gate(2, [shares[1]])
+    gate(3, [came[0]])
+    share(2, [shares[1], gates[3][0]])
+    share(3, [shares[2], came[1]])
+    own = own_shares(
+        jnp.stack([here]).astype(jnp.int32), weight, weight_other,
+        list(zip(gates, others)), [shares[-1], came[-2]],
+    )
     out = None
-    for mine, far_share, (at, span, _, _) in zip(own, came, parts):
+    for mine, far_share, (at, span) in zip(own, came, parts):
         out = finish_chunk(mine, far_share, out, at, span, seg_len)
     return out.reshape(tok, ch)
 

time: 119 us -> 99.3 us (0.83)
  waiting for transfers between devices: 29.1 us -> 18.3 us
  starting transfers between devices: 35.9 us -> 32.6 us
  Pallas kernels: 49.5 us -> 46.6 us
  other arithmetic: 1.98 us -> 0.37 us
    ppermute x19 -> x29, waiting for transfers between devices: 29.1 us -> 18.3 us  [the longest x4 11.7 us: share(): came.append(lax.ppermute(shares[-1], 'tp', PARTNER))]
    ppermute x19 -> x29, starting transfers between devices: 32.6 us -> 29.4 us  [the longest x9 18.8 us: carried_in(): lax.ppermute(sent, 'seq', shifted(sizes, dim, hop, True))]
    convert_element_type x2, other arithmetic: 1.84 us -> 0.23 us  [carried_in(): sent = state.astype(jnp.bfloat16)]
    pallas_call x2 -> x1, Pallas kernels: 5.13 us -> 3.74 us  [chip_columns(): pl.pallas_call(columns_kernel, grid_spec=pltpu.PrefetchScalarGridSpec(num...]
    pallas_call x5 -> x4, Pallas kernels: 4.52 us -> 3.87 us  [finish_chunk(): pl.pallas_call(finish_kernel, grid=(ch // width,), in_specs=in_specs, out...]
    pallas_call x6 -> x5, Pallas kernels: 14 us -> 13.6 us  [the longest x4 6.98 us: share_chunk(): pl.pallas_call(functools.partial(share_kernel, count), grid=(ch // width,...]
    pallas_call x5 -> x4, Pallas kernels: 18.2 us -> 18.3 us  [gate_chunk(): pl.pallas_call(functools.partial(gate_kernel, first, at, seg_len), grid=(...]
  transfers between devices with their start and end apart: 20 -> 30, of which waited for: 10 -> 14; matrix products, arithmetic and copies ran while one was open for 2% -> 0% of each run, Pallas kernels for 35% -> 40%
where the time goes in v2:
time: 99.3 us; the launch traced here: 98.9 us
  Pallas kernels  46.6 us (47%)
  starting transfers between devices  32.6 us (33%)
  waiting for transfers between devices  18.3 us (18%)
    ppermute x9, starting transfers between devices, carried_in(): lax.ppermute(sent, 'seq', shifted(sizes, dim, hop, True))  18.8 us
    pallas_call x4, Pallas kernels, gate_chunk(): pl.pallas_call(functools.partial(gate_kernel, first, at, seg_len), grid=(...  18.3 us
    ppermute x4, waiting for transfers between devices, share(): came.append(lax.ppermute(shares[-1], 'tp', PARTNER))  11.7 us
    ppermute x16, starting transfers between devices, gate(): others.append([lax.ppermute(piece, 'tp', SIBLING) for piece in gated])  7.34 us
    pallas_call x1, Pallas kernels, end_states(): pl.pallas_call(functools.partial(end_kernel, seg_len), grid=(ch // width,...  7.08 us
    pallas_call x4, Pallas kernels, share_chunk(): pl.pallas_call(functools.partial(share_kernel, count), grid=(ch // width,...  6.98 us
    pallas_call x1, Pallas kernels, own_shares(): pl.pallas_call(functools.partial(own_kernel, counts), grid_spec=pltpu.Pre...  6.61 us
    ppermute x9, waiting for transfers between devices, carried_in(): lax.ppermute(sent, 'seq', shifted(sizes, dim, hop, True))  4.07 us
  transfers between devices with their start and end apart: 30, of which 14 were waited for; matrix products, arithmetic and copies ran while one was open for 0% of the time, Pallas kernels for 40%

profile of v2, /device:TPU:1, one launch (start us, length us, event | category | flops | bytes accessed | tf_op | source)
XLA Modules:
  0.0 98.9 jit_solution(3331129489541640379)
XLA Ops:
  0.0 3.2 %collective-permute-start = (bf16[1024,4096]{1,0:T(8,128)(2,1)}, bf16[1024,4096]{1,0:T(8,128)(2,1)}, u32[]{:S(2)}, u32[]{:S(2)}) collective-permute-start(bf16[1024,4096]{1,0:T(8,128)(2,1)} %w_ref.3), channel_id=1, source_target_pairs={{0,1},{1,0},{2,3},{3,2},{4,5},{5,4},{6,7},{7,6},{8,9},{9,8},{10,11... | collective-permute-start | bytes 25165832 | tf_op jit(solution)/shard_map/ppermute | solution.py:360
  4.1 7.1 %end_states.1 = (f32[16,1024]{1,0:T(8,128)S(1)}, f32[128,1024]{1,0:T(8,128)S(1)}, bf16[16,1024]{1,0:T(8,128)(2,1)S(1)}) custom-call(bf16[1024,1024]{1,0:T(8,128)(2,1)} %k_ref.1, bf16[1024,1024]{1,0:T(8,128)(2,1)} %v_ref.1, f32[16,1024]{1,0:T(8,128)S(1)} %copy-done.1), custom_call_target="tpu_custom_call" | custom-call | flops 1 | bytes 1 | tf_op jit(solution)/shard_map/end_states/pallas_call | solution.py:62
  11.2 1.3 %collective-permute-start.1 = (bf16[16,1024]{1,0:T(8,128)(2,1)S(1)}, bf16[16,1024]{1,0:T(8,128)(2,1)S(1)}, u32[]{:S(2)}, u32[]{:S(2)}) collective-permute-start(bf16[16,1024]{1,0:T(8,128)(2,1)S(1)} %get-tuple-element.34), channel_id=1, source_target_pairs={{0,4},{4,8},{8,12},{12,0},{16,20},{20,24},{24,28},{28,16},{32,36},... | collective-permute-start | bytes 98312 | tf_op jit(solution)/shard_map/ppermute | solution.py:325
  12.5 5.1 %collective-permute-start.2 = (bf16[16,1024]{1,0:T(8,128)(2,1)S(1)}, bf16[16,1024]{1,0:T(8,128)(2,1)S(1)}, u32[]{:S(2)}, u32[]{:S(2)}) collective-permute-start(bf16[16,1024]{1,0:T(8,128)(2,1)S(1)} %get-tuple-element.34), channel_id=1, source_target_pairs={{0,8},{4,12},{8,0},{12,4},{16,24},{20,28},{24,16},{28,20},{32,40},... | collective-permute-start | bytes 98312 | tf_op jit(solution)/shard_map/ppermute | solution.py:325
  17.6 2.4 %collective-permute-start.3 = (bf16[16,1024]{1,0:T(8,128)(2,1)S(1)}, bf16[16,1024]{1,0:T(8,128)(2,1)S(1)}, u32[]{:S(2)}, u32[]{:S(2)}) collective-permute-start(bf16[16,1024]{1,0:T(8,128)(2,1)S(1)} %get-tuple-element.34), channel_id=1, source_target_pairs={{0,12},{4,0},{8,4},{12,8},{16,28},{20,16},{24,20},{28,24},{32,44},... | collective-permute-start | bytes 98312 | tf_op jit(solution)/shard_map/ppermute | solution.py:325
  20.0 2.3 %collective-permute-done.3 = bf16[16,1024]{1,0:T(8,128)(2,1)S(1)} collective-permute-done((bf16[16,1024]{1,0:T(8,128)(2,1)S(1)}, bf16[16,1024]{1,0:T(8,128)(2,1)S(1)}, u32[]{:S(2)}, u32[]{:S(2)}) %collective-permute-start.3) | collective-permute-done | bytes 32800 | tf_op jit(solution)/shard_map/ppermute | solution.py:325
  22.4 1.3 %collective-permute-start.4 = (bf16[16,1024]{1,0:T(8,128)(2,1)S(1)}, bf16[16,1024]{1,0:T(8,128)(2,1)S(1)}, u32[]{:S(2)}, u32[]{:S(2)}) collective-permute-start(bf16[16,1024]{1,0:T(8,128)(2,1)S(1)} %get-tuple-element.61), channel_id=1, source_target_pairs={{0,16},{4,20},{8,24},{12,28},{16,32},{20,36},{24,40},{28,44},{32,4... | collective-permute-start | bytes 98312 | tf_op jit(solution)/shard_map/ppermute | solution.py:325
  23.7 2.5 %collective-permute-start.5 = (bf16[16,1024]{1,0:T(8,128)(2,1)S(1)}, bf16[16,1024]{1,0:T(8,128)(2,1)S(1)}, u32[]{:S(2)}, u32[]{:S(2)}) collective-permute-start(bf16[16,1024]{1,0:T(8,128)(2,1)S(1)} %get-tuple-element.61), channel_id=1, source_target_pairs={{0,32},{4,36},{8,40},{12,44},{16,48},{20,52},{24,56},{28,60},{32,0... | collective-permute-start | bytes 98312 | tf_op jit(solution)/shard_map/ppermute | solution.py:325
  27.3 3.7 %chip_columns.1 = (bf16[2048,1024]{1,0:T(8,128)(2,1)}, f32[16,1024]{1,0:T(8,128)S(1)}) custom-call(s32[1]{0:T(128)} %bitcast.5.at_ref, bf16[1024,4096]{1,0:T(8,128)(2,1)} %w_ref.3, bf16[1024,4096]{1,0:T(8,128)(2,1)} %collective-permute-done.wo_ref), custom_call_target="tpu_custom_call" | custom-call | flops 1 | bytes 1 | tf_op jit(solution)/shard_map/chip_columns/pallas_call | solution.py:177
  31.2 1.4 %collective-permute-start.7 = (bf16[16,1024]{1,0:T(8,128)(2,1)S(1)}, bf16[16,1024]{1,0:T(8,128)(2,1)S(1)}, u32[]{:S(2)}, u32[]{:S(2)}) collective-permute-start(bf16[16,1024]{1,0:T(8,128)(2,1)S(1)} %fusion.24), channel_id=1, source_target_pairs={{0,64},{4,68},{8,72},{12,76},{16,80},{20,84},{24,88},{28,92},{32,9... | collective-permute-start | bytes 98312 | tf_op jit(solution)/shard_map/ppermute | solution.py:325
  32.6 2.6 %collective-permute-start.8 = (bf16[16,1024]{1,0:T(8,128)(2,1)S(1)}, bf16[16,1024]{1,0:T(8,128)(2,1)S(1)}, u32[]{:S(2)}, u32[]{:S(2)}) collective-permute-start(bf16[16,1024]{1,0:T(8,128)(2,1)S(1)} %fusion.24), channel_id=1, source_target_pairs={{0,128},{4,132},{8,136},{12,140},{16,144},{20,148},{24,152},{28,15... | collective-permute-start | bytes 98312 | tf_op jit(solution)/shard_map/ppermute | solution.py:325
  36.8 1.2 %collective-permute-done.9 = bf16[16,1024]{1,0:T(8,128)(2,1)S(1)} collective-permute-done((bf16[16,1024]{1,0:T(8,128)(2,1)S(1)}, bf16[16,1024]{1,0:T(8,128)(2,1)S(1)}, u32[]{:S(2)}, u32[]{:S(2)}) %collective-permute-start.9) | collective-permute-done | bytes 32800 | tf_op jit(solution)/shard_map/ppermute | solution.py:325
  38.2 4.6 %gate_chunk.4 = (bf16[2,32,1024]{2,1,0:T(8,128)(2,1)S(1)}, bf16[2,32,1024]{2,1,0:T(8,128)(2,1)S(1)}, bf16[2,32,1024]{2,1,0:T(8,128)(2,1)S(1)}, bf16[2,32,1024]{2,1,0:T(8,128)(2,1)S(1)}, f32[128,1024]{1,0:T(8,128)S(1)}) custom-call(bf16[8,128,1024]{2,1,0:T(8,128)(2,1)} %bitcast.84, bf16[8,128,1024]{2,1,0:T(8,128)(2,1)} %bitcast.76, ...), custom_call_target="tpu_custom_call" | custom-call | flops 1 | bytes 1 | tf_op jit(solution)/shard_map/gate_chunk/pallas_call | solution.py:148
  42.8 3.4 %collective-permute-start.10 = (bf16[64,1024]{1,0:T(8,128)(2,1)S(1)}, bf16[64,1024]{1,0:T(8,128)(2,1)S(1)}, u32[]{:S(2)}, u32[]{:S(2)}) collective-permute-start(bf16[64,1024]{1,0:T(8,128)(2,1)S(1)} %bitcast.27), channel_id=1, source_target_pairs={{0,1},{1,0},{2,3},{3,2},{4,5},{5,4},{6,7},{7,6},{8,9},{9,8},{10,11... | collective-permute-start | bytes 393224 | tf_op jit(solution)/shard_map/ppermute | solution.py:381
  48.1 1.7 %share_chunk.4.rest_0_.rest_8_ = bf16[256,1024]{1,0:T(8,128)(2,1)S(1)} custom-call(bf16[2048,1024]{1,0:T(8,128)(2,1)S(1)} %copy-done, bf16[64,1024]{1,0:T(8,128)(2,1)S(1)} %bitcast.28, bf16[64,1024]{1,0:T(8,128)(2,1)S(1)} %bitcast.31, bf16[64,1024]{1,0:T(8,128)(2,1)S(1)} %bitcast.34, bf16[64,1024]{1,0:T(8,128)(2,1)S(1)} %bitcast.37, ...), custom_call_target="tpu_custom_call" | custom-call | flops 1 | bytes 1 | tf_op jit(solution)/shard_map/share_chunk/pallas_call | solution.py:218
  50.7 4.4 %gate_chunk.5 = (bf16[2,32,1024]{2,1,0:T(8,128)(2,1)S(1)}, bf16[2,32,1024]{2,1,0:T(8,128)(2,1)S(1)}, bf16[2,32,1024]{2,1,0:T(8,128)(2,1)S(1)}, bf16[2,32,1024]{2,1,0:T(8,128)(2,1)S(1)}, f32[128,1024]{1,0:T(8,128)S(1)}) custom-call(bf16[8,128,1024]{2,1,0:T(8,128)(2,1)} %bitcast.85, bf16[8,128,1024]{2,1,0:T(8,128)(2,1)} %bitcast.77, ...), custom_call_target="tpu_custom_call" | custom-call | flops 1 | bytes 1 | tf_op jit(solution)/shard_map/gate_chunk/pallas_call | solution.py:148
  57.5 1.7 %share_chunk.5.rest_0_.rest_8_ = bf16[256,1024]{1,0:T(8,128)(2,1)S(1)} custom-call(bf16[2048,1024]{1,0:T(8,128)(2,1)S(1)} %copy-done, bf16[64,1024]{1,0:T(8,128)(2,1)S(1)} %bitcast.40, bf16[64,1024]{1,0:T(8,128)(2,1)S(1)} %bitcast.43, bf16[64,1024]{1,0:T(8,128)(2,1)S(1)} %bitcast.46, bf16[64,1024]{1,0:T(8,128)(2,1)S(1)} %bitcast.49, ...), custom_call_target="tpu_custom_call" | custom-call | flops 1 | bytes 1 | tf_op jit(solution)/shard_map/share_chunk/pallas_call | solution.py:218
  60.2 4.4 %gate_chunk.6 = (bf16[2,32,1024]{2,1,0:T(8,128)(2,1)S(1)}, bf16[2,32,1024]{2,1,0:T(8,128)(2,1)S(1)}, bf16[2,32,1024]{2,1,0:T(8,128)(2,1)S(1)}, bf16[2,32,1024]{2,1,0:T(8,128)(2,1)S(1)}, f32[128,1024]{1,0:T(8,128)S(1)}) custom-call(bf16[8,128,1024]{2,1,0:T(8,128)(2,1)} %bitcast.86, bf16[8,128,1024]{2,1,0:T(8,128)(2,1)} %bitcast.78, ...), custom_call_target="tpu_custom_call" | custom-call | flops 1 | bytes 1 | tf_op jit(solution)/shard_map/gate_chunk/pallas_call | solution.py:148
  65.7 5.0 %gate_chunk.7 = (bf16[2,32,1024]{2,1,0:T(8,128)(2,1)S(1)}, bf16[2,32,1024]{2,1,0:T(8,128)(2,1)S(1)}, bf16[2,32,1024]{2,1,0:T(8,128)(2,1)S(1)}, bf16[2,32,1024]{2,1,0:T(8,128)(2,1)S(1)}, f32[128,1024]{1,0:T(8,128)}) custom-call(bf16[8,128,1024]{2,1,0:T(8,128)(2,1)} %bitcast.87, bf16[8,128,1024]{2,1,0:T(8,128)(2,1)} %bitcast.79, ...), custom_call_target="tpu_custom_call" | custom-call | flops 1 | bytes 1 | tf_op jit(solution)/shard_map/gate_chunk/pallas_call | solution.py:148
  71.8 1.7 %share_chunk.6.rest_8_ = bf16[256,1024]{1,0:T(8,128)(2,1)S(1)} custom-call(bf16[2048,1024]{1,0:T(8,128)(2,1)S(1)} %copy-done, bf16[64,1024]{1,0:T(8,128)(2,1)S(1)} %bitcast.52, bf16[64,1024]{1,0:T(8,128)(2,1)S(1)} %bitcast.55, bf16[64,1024]{1,0:T(8,128)(2,1)S(1)} %bitcast.58, bf16[64,1024]{1,0:T(8,128)(2,1)S(1)} %bitcast.61, ...), custom_call_target="tpu_custom_call" | custom-call | flops 1 | bytes 1 | tf_op jit(solution)/shard_map/share_chunk/pallas_call | solution.py:218
  74.7 1.8 %share_chunk.7.rest_32_ = bf16[256,1024]{1,0:T(8,128)(2,1)S(1)} custom-call(bf16[2048,1024]{1,0:T(8,128)(2,1)S(1)} %copy-done, bf16[64,1024]{1,0:T(8,128)(2,1)S(1)} %bitcast.25, bf16[64,1024]{1,0:T(8,128)(2,1)S(1)} %bitcast.64, bf16[64,1024]{1,0:T(8,128)(2,1)S(1)} %bitcast.67, bf16[64,1024]{1,0:T(8,128)(2,1)S(1)} %bitcast.70, ...), custom_call_target="tpu_custom_call" | custom-call | flops 1 | bytes 1 | tf_op jit(solution)/shard_map/share_chunk/pallas_call | solution.py:218
  77.1 9.6 %collective-permute-done.28.rest_33_.far_ref = bf16[256,1024]{1,0:T(8,128)(2,1)S(1)} collective-permute-done((bf16[256,1024]{1,0:T(8,128)(2,1)S(1)}, bf16[256,1024]{1,0:T(8,128)(2,1)S(1)}, u32[]{:S(2)}, u32[]{:S(2)}) %collective-permute-start.28) | collective-permute-done | bytes 524320 | tf_op jit(solution)/shard_map/ppermute | solution.py:387
  86.7 6.6 %own_shares.1 = (f32[256,1024]{1,0:T(8,128)S(1)}, f32[256,1024]{1,0:T(8,128)S(1)}, f32[256,1024]{1,0:T(8,128)S(1)}, f32[256,1024]{1,0:T(8,128)S(1)}) custom-call(s32[1]{0:T(128)} %bitcast.at_ref, bf16[1024,4096]{1,0:T(8,128)(2,1)} %w_ref.3, bf16[1024,4096]{1,0:T(8,128)(2,1)} %collective-permute-done.wo_ref, bf16[64,1024]{1,0:T(8,128)(2,1)S(1)} %bitcast.29, ...), custom_call_target="tpu_custom_call" | custom-call | flops 1 | bytes 1 | tf_op jit(solution)/shard_map/own_shares/pallas_call | solution.py:249
  96.2 1.7 %collective-permute-done.29.far_ref = bf16[256,1024]{1,0:T(8,128)(2,1)S(1)} collective-permute-done((bf16[256,1024]{1,0:T(8,128)(2,1)S(1)}, bf16[256,1024]{1,0:T(8,128)(2,1)S(1)}, u32[]{:S(2)}, u32[]{:S(2)}) %collective-permute-start.29) | collective-permute-done | bytes 524320 | tf_op jit(solution)/shard_map/ppermute | solution.py:387
  (64 shorter events, 18.0 us)
Async XLA Ops:
  0.0 27.3 %collective-permute-start = (bf16[1024,4096]{1,0:T(8,128)(2,1)}, bf16[1024,4096]{1,0:T(8,128)(2,1)}, u32[]{:S(2)}, u32[]{:S(2)}) collective-permute-start(bf16[1024,4096]{1,0:T(8,128)(2,1)} %w_ref.3), channel_id=1, source_target_pairs={{0,1},{1,0},{2,3},{3,2},{4,5},{5,4},{6,7},{7,6},{8,9},{9,8},{10,11... | collective-permute-start | bytes 25165832 | tf_op jit(solution)/shard_map/ppermute | solution.py:360
  11.2 8.8 %collective-permute-start.1 = (bf16[16,1024]{1,0:T(8,128)(2,1)S(1)}, bf16[16,1024]{1,0:T(8,128)(2,1)S(1)}, u32[]{:S(2)}, u32[]{:S(2)}) collective-permute-start(bf16[16,1024]{1,0:T(8,128)(2,1)S(1)} %get-tuple-element.34), channel_id=1, source_target_pairs={{0,4},{4,8},{8,12},{12,0},{16,20},{20,24},{24,28},{28,16},{32,36},... | collective-permute-start | bytes 98312 | tf_op jit(solution)/shard_map/ppermute | solution.py:325
  12.5 7.5 %collective-permute-start.2 = (bf16[16,1024]{1,0:T(8,128)(2,1)S(1)}, bf16[16,1024]{1,0:T(8,128)(2,1)S(1)}, u32[]{:S(2)}, u32[]{:S(2)}) collective-permute-start(bf16[16,1024]{1,0:T(8,128)(2,1)S(1)} %get-tuple-element.34), channel_id=1, source_target_pairs={{0,8},{4,12},{8,0},{12,4},{16,24},{20,28},{24,16},{28,20},{32,40},... | collective-permute-start | bytes 98312 | tf_op jit(solution)/shard_map/ppermute | solution.py:325
  17.6 4.7 %collective-permute-start.3 = (bf16[16,1024]{1,0:T(8,128)(2,1)S(1)}, bf16[16,1024]{1,0:T(8,128)(2,1)S(1)}, u32[]{:S(2)}, u32[]{:S(2)}) collective-permute-start(bf16[16,1024]{1,0:T(8,128)(2,1)S(1)} %get-tuple-element.34), channel_id=1, source_target_pairs={{0,12},{4,0},{8,4},{12,8},{16,28},{20,16},{24,20},{28,24},{32,44},... | collective-permute-start | bytes 98312 | tf_op jit(solution)/shard_map/ppermute | solution.py:325
  22.4 8.6 %collective-permute-start.4 = (bf16[16,1024]{1,0:T(8,128)(2,1)S(1)}, bf16[16,1024]{1,0:T(8,128)(2,1)S(1)}, u32[]{:S(2)}, u32[]{:S(2)}) collective-permute-start(bf16[16,1024]{1,0:T(8,128)(2,1)S(1)} %get-tuple-element.61), channel_id=1, source_target_pairs={{0,16},{4,20},{8,24},{12,28},{16,32},{20,36},{24,40},{28,44},{32,4... | collective-permute-start | bytes 98312 | tf_op jit(solution)/shard_map/ppermute | solution.py:325
  23.7 7.4 %collective-permute-start.5 = (bf16[16,1024]{1,0:T(8,128)(2,1)S(1)}, bf16[16,1024]{1,0:T(8,128)(2,1)S(1)}, u32[]{:S(2)}, u32[]{:S(2)}) collective-permute-start(bf16[16,1024]{1,0:T(8,128)(2,1)S(1)} %get-tuple-element.61), channel_id=1, source_target_pairs={{0,32},{4,36},{8,40},{12,44},{16,48},{20,52},{24,56},{28,60},{32,0... | collective-permute-start | bytes 98312 | tf_op jit(solution)/shard_map/ppermute | solution.py:325
  26.1 4.9 %collective-permute-start.6 = (bf16[16,1024]{1,0:T(8,128)(2,1)S(1)}, bf16[16,1024]{1,0:T(8,128)(2,1)S(1)}, u32[]{:S(2)}, u32[]{:S(2)}) collective-permute-start(bf16[16,1024]{1,0:T(8,128)(2,1)S(1)} %get-tuple-element.61), channel_id=1, source_target_pairs={{0,48},{4,52},{8,56},{12,60},{16,0},{20,4},{24,8},{28,12},{32,16},... | collective-permute-start | bytes 98312 | tf_op jit(solution)/shard_map/ppermute | solution.py:325
  31.2 5.1 %collective-permute-start.7 = (bf16[16,1024]{1,0:T(8,128)(2,1)S(1)}, bf16[16,1024]{1,0:T(8,128)(2,1)S(1)}, u32[]{:S(2)}, u32[]{:S(2)}) collective-permute-start(bf16[16,1024]{1,0:T(8,128)(2,1)S(1)} %fusion.24), channel_id=1, source_target_pairs={{0,64},{4,68},{8,72},{12,76},{16,80},{20,84},{24,88},{28,92},{32,9... | collective-permute-start | bytes 98312 | tf_op jit(solution)/shard_map/ppermute | solution.py:325
  32.6 4.3 %collective-permute-start.8 = (bf16[16,1024]{1,0:T(8,128)(2,1)S(1)}, bf16[16,1024]{1,0:T(8,128)(2,1)S(1)}, u32[]{:S(2)}, u32[]{:S(2)}) collective-permute-start(bf16[16,1024]{1,0:T(8,128)(2,1)S(1)} %fusion.24), channel_id=1, source_target_pairs={{0,128},{4,132},{8,136},{12,140},{16,144},{20,148},{24,152},{28,15... | collective-permute-start | bytes 98312 | tf_op jit(solution)/shard_map/ppermute | solution.py:325
  35.2 2.8 %collective-permute-start.9 = (bf16[16,1024]{1,0:T(8,128)(2,1)S(1)}, bf16[16,1024]{1,0:T(8,128)(2,1)S(1)}, u32[]{:S(2)}, u32[]{:S(2)}) collective-permute-start(bf16[16,1024]{1,0:T(8,128)(2,1)S(1)} %fusion.24), channel_id=1, source_target_pairs={{0,192},{4,196},{8,200},{12,204},{16,208},{20,212},{24,216},{28,22... | collective-permute-start | bytes 98312 | tf_op jit(solution)/shard_map/ppermute | solution.py:325
  42.8 4.4 %collective-permute-start.10 = (bf16[64,1024]{1,0:T(8,128)(2,1)S(1)}, bf16[64,1024]{1,0:T(8,128)(2,1)S(1)}, u32[]{:S(2)}, u32[]{:S(2)}) collective-permute-start(bf16[64,1024]{1,0:T(8,128)(2,1)S(1)} %bitcast.27), channel_id=1, source_target_pairs={{0,1},{1,0},{2,3},{3,2},{4,5},{5,4},{6,7},{7,6},{8,9},{9,8},{10,11... | collective-permute-start | bytes 393224 | tf_op jit(solution)/shard_map/ppermute | solution.py:381
  49.8 15.8 %collective-permute-start.22 = (bf16[256,1024]{1,0:T(8,128)(2,1)S(1)}, bf16[256,1024]{1,0:T(8,128)(2,1)S(1)}, u32[]{:S(2)}, u32[]{:S(2)}) collective-permute-start(bf16[256,1024]{1,0:T(8,128)(2,1)S(1)} %share_chunk.4.rest_0_.rest_8_), channel_id=1, source_target_pairs={{0,2},{2,0},{1,3},{3,1},{4,6},{6,4},{5,7},{7,5},{8,10},{10,8},{9,1... | collective-permute-start | bytes 1572872 | tf_op jit(solution)/shard_map/ppermute | solution.py:387
  55.1 1.5 %collective-permute-start.14 = (bf16[64,1024]{1,0:T(8,128)(2,1)S(1)}, bf16[64,1024]{1,0:T(8,128)(2,1)S(1)}, u32[]{:S(2)}, u32[]{:S(2)}) collective-permute-start(bf16[64,1024]{1,0:T(8,128)(2,1)S(1)} %bitcast.39), channel_id=1, source_target_pairs={{0,1},{1,0},{2,3},{3,2},{4,5},{5,4},{6,7},{7,6},{8,9},{9,8},{10,11... | collective-permute-start | bytes 393224 | tf_op jit(solution)/shard_map/ppermute | solution.py:381
  59.2 15.4 %collective-permute-start.27 = (bf16[256,1024]{1,0:T(8,128)(2,1)S(1)}, bf16[256,1024]{1,0:T(8,128)(2,1)S(1)}, u32[]{:S(2)}, u32[]{:S(2)}) collective-permute-start(bf16[256,1024]{1,0:T(8,128)(2,1)S(1)} %share_chunk.5.rest_0_.rest_8_), channel_id=1, source_target_pairs={{0,2},{2,0},{1,3},{3,1},{4,6},{6,4},{5,7},{7,5},{8,10},{10,8},{9,1... | collective-permute-start | bytes 1572872 | tf_op jit(solution)/shard_map/ppermute | solution.py:387
  64.5 6.2 %collective-permute-start.18 = (bf16[64,1024]{1,0:T(8,128)(2,1)S(1)}, bf16[64,1024]{1,0:T(8,128)(2,1)S(1)}, u32[]{:S(2)}, u32[]{:S(2)}) collective-permute-start(bf16[64,1024]{1,0:T(8,128)(2,1)S(1)} %bitcast.51), channel_id=1, source_target_pairs={{0,1},{1,0},{2,3},{3,2},{4,5},{5,4},{6,7},{7,6},{8,9},{9,8},{10,11... | collective-permute-start | bytes 393224 | tf_op jit(solution)/shard_map/ppermute | solution.py:381
  65.1 6.0 %collective-permute-start.19 = (bf16[64,1024]{1,0:T(8,128)(2,1)S(1)}, bf16[64,1024]{1,0:T(8,128)(2,1)S(1)}, u32[]{:S(2)}, u32[]{:S(2)}) collective-permute-start(bf16[64,1024]{1,0:T(8,128)(2,1)S(1)} %bitcast.54), channel_id=1, source_target_pairs={{0,1},{1,0},{2,3},{3,2},{4,5},{5,4},{6,7},{7,6},{8,9},{9,8},{10,11... | collective-permute-start | bytes 393224 | tf_op jit(solution)/shard_map/ppermute | solution.py:381
  65.2 6.0 %collective-permute-start.20 = (bf16[64,1024]{1,0:T(8,128)(2,1)S(1)}, bf16[64,1024]{1,0:T(8,128)(2,1)S(1)}, u32[]{:S(2)}, u32[]{:S(2)}) collective-permute-start(bf16[64,1024]{1,0:T(8,128)(2,1)S(1)} %bitcast.57), channel_id=1, source_target_pairs={{0,1},{1,0},{2,3},{3,2},{4,5},{5,4},{6,7},{7,6},{8,9},{9,8},{10,11... | collective-permute-start | bytes 393224 | tf_op jit(solution)/shard_map/ppermute | solution.py:381
  65.6 6.0 %collective-permute-start.21 = (bf16[64,1024]{1,0:T(8,128)(2,1)S(1)}, bf16[64,1024]{1,0:T(8,128)(2,1)S(1)}, u32[]{:S(2)}, u32[]{:S(2)}) collective-permute-start(bf16[64,1024]{1,0:T(8,128)(2,1)S(1)} %bitcast.60), channel_id=1, source_target_pairs={{0,1},{1,0},{2,3},{3,2},{4,5},{5,4},{6,7},{7,6},{8,9},{9,8},{10,11... | collective-permute-start | bytes 393224 | tf_op jit(solution)/shard_map/ppermute | solution.py:381
  70.7 2.8 %collective-permute-start.23 = (bf16[64,1024]{1,0:T(8,128)(2,1)S(1)}, bf16[64,1024]{1,0:T(8,128)(2,1)S(1)}, u32[]{:S(2)}, u32[]{:S(2)}) collective-permute-start(bf16[64,1024]{1,0:T(8,128)(2,1)S(1)} %bitcast.23), channel_id=1, source_target_pairs={{0,1},{1,0},{2,3},{3,2},{4,5},{5,4},{6,7},{7,6},{8,9},{9,8},{10,11... | collective-permute-start | bytes 393224 | tf_op jit(solution)/shard_map/ppermute | solution.py:381
  71.1 3.1 %collective-permute-start.24 = (bf16[64,1024]{1,0:T(8,128)(2,1)S(1)}, bf16[64,1024]{1,0:T(8,128)(2,1)S(1)}, u32[]{:S(2)}, u32[]{:S(2)}) collective-permute-start(bf16[64,1024]{1,0:T(8,128)(2,1)S(1)} %bitcast.63), channel_id=1, source_target_pairs={{0,1},{1,0},{2,3},{3,2},{4,5},{5,4},{6,7},{7,6},{8,9},{9,8},{10,11... | collective-permute-start | bytes 393224 | tf_op jit(solution)/shard_map/ppermute | solution.py:381
  71.2 3.0 %collective-permute-start.25 = (bf16[64,1024]{1,0:T(8,128)(2,1)S(1)}, bf16[64,1024]{1,0:T(8,128)(2,1)S(1)}, u32[]{:S(2)}, u32[]{:S(2)}) collective-permute-start(bf16[64,1024]{1,0:T(8,128)(2,1)S(1)} %bitcast.66), channel_id=1, source_target_pairs={{0,1},{1,0},{2,3},{3,2},{4,5},{5,4},{6,7},{7,6},{8,9},{9,8},{10,11... | collective-permute-start | bytes 393224 | tf_op jit(solution)/shard_map/ppermute | solution.py:381
  71.7 2.6 %collective-permute-start.26 = (bf16[64,1024]{1,0:T(8,128)(2,1)S(1)}, bf16[64,1024]{1,0:T(8,128)(2,1)S(1)}, u32[]{:S(2)}, u32[]{:S(2)}) collective-permute-start(bf16[64,1024]{1,0:T(8,128)(2,1)S(1)} %bitcast.69), channel_id=1, source_target_pairs={{0,1},{1,0},{2,3},{3,2},{4,5},{5,4},{6,7},{7,6},{8,9},{9,8},{10,11... | collective-permute-start | bytes 393224 | tf_op jit(solution)/shard_map/ppermute | solution.py:381
  73.5 13.2 %collective-permute-start.28 = (bf16[256,1024]{1,0:T(8,128)(2,1)S(1)}, bf16[256,1024]{1,0:T(8,128)(2,1)S(1)}, u32[]{:S(2)}, u32[]{:S(2)}) collective-permute-start(bf16[256,1024]{1,0:T(8,128)(2,1)S(1)} %share_chunk.6.rest_8_), channel_id=1, source_target_pairs={{0,2},{2,0},{1,3},{3,1},{4,6},{6,4},{5,7},{7,5},{8,10},{10,8},{9,1... | collective-permute-start | bytes 1572872 | tf_op jit(solution)/shard_map/ppermute | solution.py:387
  76.4 21.5 %collective-permute-start.29 = (bf16[256,1024]{1,0:T(8,128)(2,1)S(1)}, bf16[256,1024]{1,0:T(8,128)(2,1)S(1)}, u32[]{:S(2)}, u32[]{:S(2)}) collective-permute-start(bf16[256,1024]{1,0:T(8,128)(2,1)S(1)} %share_chunk.7.rest_32_), channel_id=1, source_target_pairs={{0,2},{2,0},{1,3},{3,1},{4,6},{6,4},{5,7},{7,5},{8,10},{10,8},{9,1... | collective-permute-start | bytes 1572872 | tf_op jit(solution)/shard_map/ppermute | solution.py:387
  (11 other events, 59.0 us)

commit v3 on v2

--- a/solution.py
+++ b/solution.py
@@ -10,7 +10,7 @@
 SEG = 8
 LANES = 128
 SPANS = (32, 32, 32, 32)
-PIECE = 64
+PIECE = 128
 VMEM_LIMIT = 32 * 2**20
 SIBLING = [(0, 1), (1, 0), (2, 3), (3, 2)]
 PARTNER = [(0, 2), (2, 0), (1, 3), (3, 1)]
@@ -19,6 +19,10 @@
 
 def cost(flops, moved):
     return pl.CostEstimate(flops=1, bytes_accessed=1, transcendentals=0)
+
+
+def spread(table):
+    return [jnp.broadcast_to(table[n : n + 1], (SEG, LANES)) for n in range(table.shape[0])]
 
 
 def end_kernel(seg_len, k_ref, v_ref, lam_ref, last_ref, before_ref, sent_ref, x_ref):
@@ -30,8 +34,8 @@
             rows = pl.ds(seg * seg_len, seg_len)
             x = k_ref[rows, cols].astype(jnp.float32) * v_ref[rows, cols].astype(jnp.float32)
             x_ref[pl.ds(seg * pitch, seg_len), :] = x
-        lam = [jnp.broadcast_to(lam_ref[n : n + 1, cols], (SEG, LANES)) for n in range(order)]
-        decay = [jnp.exp(-rate) for rate in lam]
+        lam = lam_ref[:, cols]
+        decay = spread(jnp.exp(-lam))
 
         def body(it, state):
             for u in range(16):
@@ -42,11 +46,11 @@
         zero = jnp.zeros((SEG, LANES), jnp.float32)
         state = lax.fori_loop(0, seg_len // 16, body, (zero,) * order)
         row = lax.broadcasted_iota(jnp.int32, (SEG, LANES), 0)
+        hops = {step: spread(jnp.exp(lam * (-float(seg_len * step)))) for step in (1, 2, 4)}
         for n in range(order):
             run = state[n]
-            for step in (1, 2, 4):
-                hop = jnp.exp(lam[n] * (-float(seg_len * step)))
-                run = run + jnp.where(row >= step, hop * pltpu.roll(run, step, 0), 0.0)
+            for step, hop in hops.items():
+                run = run + jnp.where(row >= step, hop[n] * pltpu.roll(run, step, 0), 0.0)
             last_ref[n : n + 1, cols] = run[SEG - 1 : SEG]
             sent_ref[n : n + 1, cols] = run[SEG - 1 : SEG].astype(jnp.bfloat16)
             before_ref[n * SEG : (n + 1) * SEG, cols] = jnp.where(
@@ -87,20 +91,22 @@
     pitch = span + 1
     for group in range(q_ref.shape[2] // LANES):
         cols = slice(group * LANES, (group + 1) * LANES)
-        for seg in range(SEG):
-            x = k_ref[seg, :, cols].astype(jnp.float32) * v_ref[seg, :, cols].astype(jnp.float32)
-            x_ref[pl.ds(seg * pitch, span), :] = x
-        lam = [jnp.broadcast_to(lam_ref[n : n + 1, cols], (SEG, LANES)) for n in range(order)]
-        decay = [jnp.exp(-rate) for rate in lam]
-        weight = [res_ref[n : n + 1, cols] * jnp.sqrt(lam[n]) for n in range(order)]
+        lam = lam_ref[:, cols]
+        decay = spread(jnp.exp(-lam))
+        weight = spread(res_ref[:, cols] * jnp.sqrt(lam))
         state = [state_ref[n * SEG : (n + 1) * SEG, cols] for n in range(order)]
         if first:
             row = lax.broadcasted_iota(jnp.int32, (SEG, LANES), 0).astype(jnp.float32)
             reach = row * (-float(seg_len)) - float(late)
             state = [
-                h + jnp.exp(lam[n] * reach) * inc_ref[n : n + 1, cols]
+                h + jnp.exp(lam[n : n + 1] * reach) * inc_ref[n : n + 1, cols]
                 for n, h in enumerate(state)
             ]
+
+        skip = skip_ref[:, cols]
+        for seg in range(SEG):
+            x = k_ref[seg, :, cols].astype(jnp.float32) * v_ref[seg, :, cols].astype(jnp.float32)
+            x_ref[pl.ds(seg * pitch, span), :] = x
 
         def body(it, state):
             for u in range(16):
@@ -110,7 +116,7 @@
                 terms = [w * h for w, h in zip(weight, state)]
                 while len(terms) > 1:
                     terms = [a + b for a, b in zip(terms[::2], terms[1::2])]
-                y_ref[where, :] = terms[0]
+                y_ref[where, :] = terms[0] + skip * x
             return state
 
         if span == 16:
@@ -119,10 +125,8 @@
             state = lax.fori_loop(0, span // 16, body, tuple(state))
         for n in range(order):
             next_ref[n * SEG : (n + 1) * SEG, cols] = state[n]
-        skip = skip_ref[:, cols]
         for seg in range(SEG):
-            rows = pl.ds(seg * pitch, span)
-            gate = q_ref[seg, :, cols].astype(jnp.float32) * (y_ref[rows, :] + skip * x_ref[rows, :])
+            gate = q_ref[seg, :, cols].astype(jnp.float32) * y_ref[pl.ds(seg * pitch, span), :]
             g_refs[seg // held][seg % held, :, cols] = gate.astype(jnp.bfloat16)
 
 
@@ -164,35 +168,34 @@
 
 
 def columns_kernel(at_ref, w_ref, wo_ref, out_ref, mark_ref):
+    depth = w_ref.shape[0]
     mark_ref[...] = jnp.zeros_like(mark_ref)
-    depth = w_ref.shape[0]
     out_ref[:depth] = w_ref[...]
     out_ref[depth:] = wo_ref[...]
 
 
-def chip_columns(block, weight, weight_other, order, width=512):
+def chip_columns(start, count, weight, weight_other, order, width=256):
     ch = weight.shape[0]
-    per = ch // width
-    part = pl.BlockSpec((ch, width), lambda j, at: (0, at[0] * per + j))
+    part = pl.BlockSpec((ch, width), lambda j, at: (0, at[0] + j))
     return pl.pallas_call(
         columns_kernel,
         grid_spec=pltpu.PrefetchScalarGridSpec(
             num_scalar_prefetch=1,
-            grid=(per,),
+            grid=(count // width,),
             in_specs=[part, part],
             out_specs=[
                 pl.BlockSpec((2 * ch, width), lambda j, at: (0, j)),
-                pl.BlockSpec((order, width), lambda j, at: (0, j)),
+                pl.BlockSpec((order, ch), lambda j, at: (0, 0)),
             ],
         ),
         out_shape=[
-            pltpu.HBM((2 * ch, ch), weight.dtype),
+            pltpu.HBM((2 * ch, count), weight.dtype),
             jax.ShapeDtypeStruct((order, ch), jnp.float32),
         ],
         compiler_params=pltpu.CompilerParams(vmem_limit_bytes=VMEM_LIMIT),
-        cost_estimate=cost(0, 8 * ch * ch),
+        cost_estimate=cost(0, 8 * ch * count),
         name="chip_columns",
-    )(block, weight, weight_other)
+    )((start // width)[None].astype(jnp.int32), weight, weight_other)
 
 
 def gathered(pieces):
@@ -204,29 +207,29 @@
     return total + jnp.dot(gathered(other), weight_other, preferred_element_type=jnp.float32)
 
 
-def share_kernel(count, w_ref, *rest):
+def share_kernel(count, w_ref, wx_ref, *rest):
     out_ref = rest[-1]
     depth = w_ref.shape[0] // 2
-    total = product(rest[:count], rest[count : 2 * count], w_ref[:depth], w_ref[depth:])
-    out_ref[...] = total.astype(out_ref.dtype)
-
-
-def share_chunk(mine, other, weight, after, width=512):
+    width = w_ref.shape[1]
+    for part, ref in enumerate((w_ref, wx_ref)):
+        total = product(rest[:count], rest[count : 2 * count], ref[:depth], ref[depth:])
+        out_ref[:, part * width : (part + 1) * width] = total.astype(out_ref.dtype)
+
+
+def share_chunk(mine, other, weights, after):
     count = len(mine)
-    ch = weight.shape[1]
-    rows = count * PIECE
+    depth, half = weights[0].shape
+    rows, ch = count * PIECE, depth // 2
+    whole = lambda *shape: pl.BlockSpec(shape, lambda: (0, 0))
     return pl.pallas_call(
         functools.partial(share_kernel, count),
-        grid=(ch // width,),
-        in_specs=[pl.BlockSpec((2 * ch, width), lambda j: (0, j))]
-        + [pl.BlockSpec((PIECE, ch), lambda j: (0, 0))] * (2 * count)
-        + [ANY] * len(after),
-        out_specs=pl.BlockSpec((rows, width), lambda j: (0, j)),
-        out_shape=jax.ShapeDtypeStruct((rows, ch), jnp.bfloat16),
-        compiler_params=pltpu.CompilerParams(vmem_limit_bytes=VMEM_LIMIT),
-        cost_estimate=cost(4 * rows * ch * ch, 4 * ch * ch + 6 * rows * ch),
+        in_specs=[whole(depth, half)] * 2 + [whole(PIECE, ch)] * (2 * count) + [ANY] * len(after),
+        out_specs=whole(rows, 2 * half),
+        out_shape=jax.ShapeDtypeStruct((rows, 2 * half), jnp.bfloat16),
+        compiler_params=pltpu.CompilerParams(vmem_limit_bytes=VMEM_LIMIT),
+        cost_estimate=cost(4 * rows * ch * half, 4 * ch * half + 6 * rows * ch),
         name="share_chunk",
-    )(weight, *mine, *other, *after)
+    )(*weights, *mine, *other, *after)
 
 
 def own_kernel(counts, at_ref, w_ref, wo_ref, *rest):
@@ -359,10 +362,16 @@
     chip, core = here // 2, here % 2
     weight_other = in_hbm(lax.ppermute(weight, "tp", SIBLING))
     weight = in_hbm(weight)
-    last, before, sent = end_states(in_hbm(key), in_hbm(value), rates)
-    block = jnp.stack([2 * (1 - chip) + core]).astype(jnp.int32)
-    weight_far, far_mark = chip_columns(block, weight, weight_other, rates.shape[0])
-    incoming = carried_in(last, sent, rates, tok, sizes, {1: far_mark})
+    last, before, sent = end_states(in_hbm(key), in_hbm(value), in_hbm(rates))
+    half = ch // 2
+    begin = (2 * (1 - chip) + core) * ch
+    weight_far, marks = zip(
+        *(
+            chip_columns(begin + part * half, half, weight, weight_other, rates.shape[0])
+            for part in range(2)
+        )
+    )
+    incoming = carried_in(last, sent, rates, tok, sizes, {2: marks[0], 1: marks[1]})
     view = lambda part: part.reshape(SEG, seg_len, ch)
     query, key, value = (in_hbm(view(part)) for part in (query, key, value))
     state, extra = before, incoming

time: 99.3 us -> 95.6 us (0.963)
  starting transfers between devices: 32.6 us -> 31.2 us
    ppermute x9, waiting for transfers between devices: 4.07 us -> 1.76 us  [carried_in(): lax.ppermute(sent, 'seq', shifted(sizes, dim, hop, True))]
    pallas_call x4, Pallas kernels: 6.98 us -> 5.02 us  [share_chunk(): pl.pallas_call(functools.partial(share_kernel, count), in_specs=[whole(de...]
    pallas_call x1 -> x2, Pallas kernels: 3.74 us -> 5.33 us  [chip_columns(): pl.pallas_call(columns_kernel, grid_spec=pltpu.PrefetchScalarGridSpec(num...]
    ppermute x16 -> x8, starting transfers between devices: 7.34 us -> 5.91 us  [gate(): others.append([lax.ppermute(piece, 'tp', SIBLING) for piece in gated])]
    ppermute x4, waiting for transfers between devices: 11.7 us -> 13 us  [share(): came.append(lax.ppermute(shares[-1], 'tp', PARTNER))]
    ppermute x16 -> x8, waiting for transfers between devices: 2.51 us -> 2.88 us  [gate(): others.append([lax.ppermute(piece, 'tp', SIBLING) for piece in gated])]
  transfers between devices with their start and end apart: 30 -> 22, of which waited for: 14 -> 9; matrix products, arithmetic and copies ran while one was open for 0% -> 0% of each run, Pallas kernels for 40% -> 41%
where the time goes in v3:
time: 95.6 us; the launch traced here: 95.2 us
  Pallas kernels  45.8 us (48%)
  starting transfers between devices  31.2 us (33%)
  waiting for transfers between devices  17.6 us (18%)
    ppermute x9, starting transfers between devices, carried_in(): lax.ppermute(sent, 'seq', shifted(sizes, dim, hop, True))  18.8 us
    pallas_call x4, Pallas kernels, gate_chunk(): pl.pallas_call(functools.partial(gate_kernel, first, at, seg_len), grid=(...  18 us
    ppermute x4, waiting for transfers between devices, share(): came.append(lax.ppermute(shares[-1], 'tp', PARTNER))  13 us
    pallas_call x1, Pallas kernels, end_states(): pl.pallas_call(functools.partial(end_kernel, seg_len), grid=(ch // width,...  6.92 us
    pallas_call x1, Pallas kernels, own_shares(): pl.pallas_call(functools.partial(own_kernel, counts), grid_spec=pltpu.Pre...  6.62 us
    ppermute x8, starting transfers between devices, gate(): others.append([lax.ppermute(piece, 'tp', SIBLING) for piece in gated])  5.91 us
    pallas_call x2, Pallas kernels, chip_columns(): pl.pallas_call(columns_kernel, grid_spec=pltpu.PrefetchScalarGridSpec(num...  5.33 us
    pallas_call x4, Pallas kernels, share_chunk(): pl.pallas_call(functools.partial(share_kernel, count), in_specs=[whole(de...  5.02 us
  transfers between devices with their start and end apart: 22, of which 9 were waited for; matrix products, arithmetic and copies ran while one was open for 0% of the time, Pallas kernels for 41%

profile of v3, /device:TPU:1, one launch (start us, length us, event | category | flops | bytes accessed | tf_op | source)
XLA Modules:
  0.0 95.2 jit_solution(2967632209474222462)
XLA Ops:
  0.0 3.2 %collective-permute-start = (bf16[1024,4096]{1,0:T(8,128)(2,1)}, bf16[1024,4096]{1,0:T(8,128)(2,1)}, u32[]{:S(2)}, u32[]{:S(2)}) collective-permute-start(bf16[1024,4096]{1,0:T(8,128)(2,1)} %w_ref.5), channel_id=1, source_target_pairs={{0,1},{1,0},{2,3},{3,2},{4,5},{5,4},{6,7},{7,6},{8,9},{9,8},{10,11... | collective-permute-start | bytes 25165832 | tf_op jit(solution)/shard_map/ppermute | solution.py:363
  3.2 6.9 %end_states.1 = (f32[16,1024]{1,0:T(8,128)S(1)}, f32[128,1024]{1,0:T(8,128)S(1)}, bf16[16,1024]{1,0:T(8,128)(2,1)S(1)}) custom-call(bf16[1024,1024]{1,0:T(8,128)(2,1)} %k_ref.1, bf16[1024,1024]{1,0:T(8,128)(2,1)} %v_ref.1, f32[16,1024]{1,0:T(8,128)} %lam_ref.9), custom_call_target="tpu_custom_call" | custom-call | flops 1 | bytes 1 | tf_op jit(solution)/shard_map/end_states/pallas_call | solution.py:66
  10.2 1.3 %collective-permute-start.1 = (bf16[16,1024]{1,0:T(8,128)(2,1)S(1)}, bf16[16,1024]{1,0:T(8,128)(2,1)S(1)}, u32[]{:S(2)}, u32[]{:S(2)}) collective-permute-start(bf16[16,1024]{1,0:T(8,128)(2,1)S(1)} %get-tuple-element.28), channel_id=1, source_target_pairs={{0,4},{4,8},{8,12},{12,0},{16,20},{20,24},{24,28},{28,16},{32,36},... | collective-permute-start | bytes 98312 | tf_op jit(solution)/shard_map/ppermute | solution.py:328
  11.5 5.1 %collective-permute-start.2 = (bf16[16,1024]{1,0:T(8,128)(2,1)S(1)}, bf16[16,1024]{1,0:T(8,128)(2,1)S(1)}, u32[]{:S(2)}, u32[]{:S(2)}) collective-permute-start(bf16[16,1024]{1,0:T(8,128)(2,1)S(1)} %get-tuple-element.28), channel_id=1, source_target_pairs={{0,8},{4,12},{8,0},{12,4},{16,24},{20,28},{24,16},{28,20},{32,40},... | collective-permute-start | bytes 98312 | tf_op jit(solution)/shard_map/ppermute | solution.py:328
  16.6 2.4 %collective-permute-start.3 = (bf16[16,1024]{1,0:T(8,128)(2,1)S(1)}, bf16[16,1024]{1,0:T(8,128)(2,1)S(1)}, u32[]{:S(2)}, u32[]{:S(2)}) collective-permute-start(bf16[16,1024]{1,0:T(8,128)(2,1)S(1)} %get-tuple-element.28), channel_id=1, source_target_pairs={{0,12},{4,0},{8,4},{12,8},{16,28},{20,16},{24,20},{28,24},{32,44},... | collective-permute-start | bytes 98312 | tf_op jit(solution)/shard_map/ppermute | solution.py:328
  19.0 2.6 %chip_columns.2 = (bf16[2048,512]{1,0:T(8,128)(2,1)}, f32[16,1024]{1,0:T(8,128)S(1)}) custom-call(s32[1]{0:T(128)} %bitcast.5.at_ref, bf16[1024,4096]{1,0:T(8,128)(2,1)} %w_ref.5, bf16[1024,4096]{1,0:T(8,128)(2,1)} %collective-permute-done.wo_ref), custom_call_target="tpu_custom_call" | custom-call | flops 1 | bytes 1 | tf_op jit(solution)/shard_map/chip_columns/pallas_call | solution.py:180
  21.8 1.3 %collective-permute-start.4 = (bf16[16,1024]{1,0:T(8,128)(2,1)S(1)}, bf16[16,1024]{1,0:T(8,128)(2,1)S(1)}, u32[]{:S(2)}, u32[]{:S(2)}) collective-permute-start(bf16[16,1024]{1,0:T(8,128)(2,1)S(1)} %get-tuple-element.49), channel_id=1, source_target_pairs={{0,16},{4,20},{8,24},{12,28},{16,32},{20,36},{24,40},{28,44},{32,4... | collective-permute-start | bytes 98312 | tf_op jit(solution)/shard_map/ppermute | solution.py:328
  23.1 2.5 %collective-permute-start.5 = (bf16[16,1024]{1,0:T(8,128)(2,1)S(1)}, bf16[16,1024]{1,0:T(8,128)(2,1)S(1)}, u32[]{:S(2)}, u32[]{:S(2)}) collective-permute-start(bf16[16,1024]{1,0:T(8,128)(2,1)S(1)} %get-tuple-element.49), channel_id=1, source_target_pairs={{0,32},{4,36},{8,40},{12,44},{16,48},{20,52},{24,56},{28,60},{32,0... | collective-permute-start | bytes 98312 | tf_op jit(solution)/shard_map/ppermute | solution.py:328
  26.7 2.7 %chip_columns.3 = (bf16[2048,512]{1,0:T(8,128)(2,1)}, f32[16,1024]{1,0:T(8,128)S(1)}) custom-call(s32[1]{0:T(128)} %bitcast.6.at_ref, bf16[1024,4096]{1,0:T(8,128)(2,1)} %w_ref.5, bf16[1024,4096]{1,0:T(8,128)(2,1)} %collective-permute-done.wo_ref), custom_call_target="tpu_custom_call" | custom-call | flops 1 | bytes 1 | tf_op jit(solution)/shard_map/chip_columns/pallas_call | solution.py:180
  29.5 1.4 %collective-permute-start.7 = (bf16[16,1024]{1,0:T(8,128)(2,1)S(1)}, bf16[16,1024]{1,0:T(8,128)(2,1)S(1)}, u32[]{:S(2)}, u32[]{:S(2)}) collective-permute-start(bf16[16,1024]{1,0:T(8,128)(2,1)S(1)} %fusion.31), channel_id=1, source_target_pairs={{0,64},{4,68},{8,72},{12,76},{16,80},{20,84},{24,88},{28,92},{32,9... | collective-permute-start | bytes 98312 | tf_op jit(solution)/shard_map/ppermute | solution.py:328
  30.9 2.6 %collective-permute-start.8 = (bf16[16,1024]{1,0:T(8,128)(2,1)S(1)}, bf16[16,1024]{1,0:T(8,128)(2,1)S(1)}, u32[]{:S(2)}, u32[]{:S(2)}) collective-permute-start(bf16[16,1024]{1,0:T(8,128)(2,1)S(1)} %fusion.31), channel_id=1, source_target_pairs={{0,128},{4,132},{8,136},{12,140},{16,144},{20,148},{24,152},{28,15... | collective-permute-start | bytes 98312 | tf_op jit(solution)/shard_map/ppermute | solution.py:328
  36.5 4.5 %gate_chunk.4 = (bf16[4,32,1024]{2,1,0:T(8,128)(2,1)S(1)}, bf16[4,32,1024]{2,1,0:T(8,128)(2,1)S(1)}, f32[128,1024]{1,0:T(8,128)S(1)}) custom-call(bf16[8,128,1024]{2,1,0:T(8,128)(2,1)} %bitcast.53, bf16[8,128,1024]{2,1,0:T(8,128)(2,1)} %bitcast.45, bf16[8,128,1024]{2,1,0:T(8,128)(2,1)} %bitcast.49, f32[16,1024]{1,0:T(8,128)S(1)} %copy-done.2, ...), custom_call_target="tpu_custom_call" | custom-call | flops 1 | bytes 1 | tf_op jit(solution)/shard_map/gate_chunk/pallas_call | solution.py:152
  41.1 3.4 %collective-permute-start.10 = (bf16[128,1024]{1,0:T(8,128)(2,1)S(1)}, bf16[128,1024]{1,0:T(8,128)(2,1)S(1)}, u32[]{:S(2)}, u32[]{:S(2)}) collective-permute-start(bf16[128,1024]{1,0:T(8,128)(2,1)S(1)} %bitcast.20), channel_id=1, source_target_pairs={{0,1},{1,0},{2,3},{3,2},{4,5},{5,4},{6,7},{7,6},{8,9},{9,8},{10,11... | collective-permute-start | bytes 786440 | tf_op jit(solution)/shard_map/ppermute | solution.py:390
  46.1 1.2 %share_chunk.4.rest_0_.rest_4_ = bf16[256,1024]{1,0:T(8,128)(2,1)S(1)} custom-call(bf16[2048,512]{1,0:T(8,128)(2,1)S(1)} %copy-done, bf16[2048,512]{1,0:T(8,128)(2,1)S(1)} %copy-done.1, bf16[128,1024]{1,0:T(8,128)(2,1)S(1)} %bitcast.21, bf16[128,1024]{1,0:T(8,128)(2,1)S(1)} %bitcast.24, bf16[128,1024]{1,0:T(8,128)(2,1)S(1)} %collective-permute-done.10.rest_2_, ...), custom_call_target="tpu_custom_call" | custom-call | flops 1 | bytes 1 | tf_op jit(solution)/shard_map/share_chunk/pallas_call | solution.py:224
  48.1 4.3 %gate_chunk.5 = (bf16[4,32,1024]{2,1,0:T(8,128)(2,1)S(1)}, bf16[4,32,1024]{2,1,0:T(8,128)(2,1)S(1)}, f32[128,1024]{1,0:T(8,128)S(1)}) custom-call(bf16[8,128,1024]{2,1,0:T(8,128)(2,1)} %bitcast.54, bf16[8,128,1024]{2,1,0:T(8,128)(2,1)} %bitcast.46, bf16[8,128,1024]{2,1,0:T(8,128)(2,1)} %bitcast.50, f32[16,1024]{1,0:T(8,128)S(1)} %copy-done.2, ...), custom_call_target="tpu_custom_call" | custom-call | flops 1 | bytes 1 | tf_op jit(solution)/shard_map/gate_chunk/pallas_call | solution.py:152
  54.9 1.3 %share_chunk.5.rest_0_.rest_4_ = bf16[256,1024]{1,0:T(8,128)(2,1)S(1)} custom-call(bf16[2048,512]{1,0:T(8,128)(2,1)S(1)} %copy-done, bf16[2048,512]{1,0:T(8,128)(2,1)S(1)} %copy-done.1, bf16[128,1024]{1,0:T(8,128)(2,1)S(1)} %bitcast.27, bf16[128,1024]{1,0:T(8,128)(2,1)S(1)} %bitcast.30, bf16[128,1024]{1,0:T(8,128)(2,1)S(1)} %collective-permute-done.12.rest_2_.rest_6_, ...), custom_call_target="tpu_custom_call" | custom-call | flops 1 | bytes 1 | tf_op jit(solution)/shard_map/share_chunk/pallas_call | solution.py:224
  57.0 4.3 %gate_chunk.6 = (bf16[4,32,1024]{2,1,0:T(8,128)(2,1)S(1)}, bf16[4,32,1024]{2,1,0:T(8,128)(2,1)S(1)}, f32[128,1024]{1,0:T(8,128)S(1)}) custom-call(bf16[8,128,1024]{2,1,0:T(8,128)(2,1)} %bitcast.55, bf16[8,128,1024]{2,1,0:T(8,128)(2,1)} %bitcast.47, bf16[8,128,1024]{2,1,0:T(8,128)(2,1)} %bitcast.51, f32[16,1024]{1,0:T(8,128)S(1)} %copy-done.2, ...), custom_call_target="tpu_custom_call" | custom-call | flops 1 | bytes 1 | tf_op jit(solution)/shard_map/gate_chunk/pallas_call | solution.py:152
  62.1 4.9 %gate_chunk.7 = (bf16[4,32,1024]{2,1,0:T(8,128)(2,1)S(1)}, bf16[4,32,1024]{2,1,0:T(8,128)(2,1)S(1)}, f32[128,1024]{1,0:T(8,128)}) custom-call(bf16[8,128,1024]{2,1,0:T(8,128)(2,1)} %bitcast.56, bf16[8,128,1024]{2,1,0:T(8,128)(2,1)} %bitcast.48, bf16[8,128,1024]{2,1,0:T(8,128)(2,1)} %bitcast.52, f32[16,1024]{1,0:T(8,128)S(1)} %copy-done.2, ...), custom_call_target="tpu_custom_call" | custom-call | flops 1 | bytes 1 | tf_op jit(solution)/shard_map/gate_chunk/pallas_call | solution.py:152
  67.5 1.3 %share_chunk.6.rest_4_ = bf16[256,1024]{1,0:T(8,128)(2,1)S(1)} custom-call(bf16[2048,512]{1,0:T(8,128)(2,1)S(1)} %copy-done, bf16[2048,512]{1,0:T(8,128)(2,1)S(1)} %copy-done.1, bf16[128,1024]{1,0:T(8,128)(2,1)S(1)} %bitcast.33, bf16[128,1024]{1,0:T(8,128)(2,1)S(1)} %bitcast.36, bf16[128,1024]{1,0:T(8,128)(2,1)S(1)} %collective-permute-done.14.rest_2_.rest_10_, ...), custom_call_target="tpu_custom_call" | custom-call | flops 1 | bytes 1 | tf_op jit(solution)/shard_map/share_chunk/pallas_call | solution.py:224
  69.6 2.1 %collective-permute-done.19.rest_5_.far_ref = bf16[256,1024]{1,0:T(8,128)(2,1)S(1)} collective-permute-done((bf16[256,1024]{1,0:T(8,128)(2,1)S(1)}, bf16[256,1024]{1,0:T(8,128)(2,1)S(1)}, u32[]{:S(2)}, u32[]{:S(2)}) %collective-permute-start.19) | collective-permute-done | bytes 524320 | tf_op jit(solution)/shard_map/ppermute | solution.py:396
  71.8 1.2 %share_chunk.7.rest_16_ = bf16[256,1024]{1,0:T(8,128)(2,1)S(1)} custom-call(bf16[2048,512]{1,0:T(8,128)(2,1)S(1)} %copy-done, bf16[2048,512]{1,0:T(8,128)(2,1)S(1)} %copy-done.1, bf16[128,1024]{1,0:T(8,128)(2,1)S(1)} %bitcast.18, bf16[128,1024]{1,0:T(8,128)(2,1)S(1)} %bitcast.39, bf16[128,1024]{1,0:T(8,128)(2,1)S(1)} %collective-permute-done.17.rest_2_.rest_14_, ...), custom_call_target="tpu_custom_call" | custom-call | flops 1 | bytes 1 | tf_op jit(solution)/shard_map/share_chunk/pallas_call | solution.py:224
  73.8 9.1 %collective-permute-done.20.rest_17_.far_ref = bf16[256,1024]{1,0:T(8,128)(2,1)S(1)} collective-permute-done((bf16[256,1024]{1,0:T(8,128)(2,1)S(1)}, bf16[256,1024]{1,0:T(8,128)(2,1)S(1)}, u32[]{:S(2)}, u32[]{:S(2)}) %collective-permute-start.20) | collective-permute-done | bytes 524320 | tf_op jit(solution)/shard_map/ppermute | solution.py:396
  83.0 6.6 %own_shares.1 = (f32[256,1024]{1,0:T(8,128)S(1)}, f32[256,1024]{1,0:T(8,128)S(1)}, f32[256,1024]{1,0:T(8,128)S(1)}, f32[256,1024]{1,0:T(8,128)S(1)}) custom-call(s32[1]{0:T(128)} %bitcast.at_ref, bf16[1024,4096]{1,0:T(8,128)(2,1)} %w_ref.5, bf16[1024,4096]{1,0:T(8,128)(2,1)} %collective-permute-done.wo_ref, bf16[128,1024]{1,0:T(8,128)(2,1)S(1)} %bitcast.22, ...), custom_call_target="tpu_custom_call" | custom-call | flops 1 | bytes 1 | tf_op jit(solution)/shard_map/own_shares/pallas_call | solution.py:252
  92.5 1.7 %collective-permute-done.21.far_ref = bf16[256,1024]{1,0:T(8,128)(2,1)S(1)} collective-permute-done((bf16[256,1024]{1,0:T(8,128)(2,1)S(1)}, bf16[256,1024]{1,0:T(8,128)(2,1)S(1)}, u32[]{:S(2)}, u32[]{:S(2)}) %collective-permute-start.21) | collective-permute-done | bytes 524320 | tf_op jit(solution)/shard_map/ppermute | solution.py:396
  (49 shorter events, 16.9 us)
Async XLA Ops:
  0.0 19.0 %collective-permute-start = (bf16[1024,4096]{1,0:T(8,128)(2,1)}, bf16[1024,4096]{1,0:T(8,128)(2,1)}, u32[]{:S(2)}, u32[]{:S(2)}) collective-permute-start(bf16[1024,4096]{1,0:T(8,128)(2,1)} %w_ref.5), channel_id=1, source_target_pairs={{0,1},{1,0},{2,3},{3,2},{4,5},{5,4},{6,7},{7,6},{8,9},{9,8},{10,11... | collective-permute-start | bytes 25165832 | tf_op jit(solution)/shard_map/ppermute | solution.py:363
  10.2 11.5 %collective-permute-start.1 = (bf16[16,1024]{1,0:T(8,128)(2,1)S(1)}, bf16[16,1024]{1,0:T(8,128)(2,1)S(1)}, u32[]{:S(2)}, u32[]{:S(2)}) collective-permute-start(bf16[16,1024]{1,0:T(8,128)(2,1)S(1)} %get-tuple-element.28), channel_id=1, source_target_pairs={{0,4},{4,8},{8,12},{12,0},{16,20},{20,24},{24,28},{28,16},{32,36},... | collective-permute-start | bytes 98312 | tf_op jit(solution)/shard_map/ppermute | solution.py:328
  11.5 10.1 %collective-permute-start.2 = (bf16[16,1024]{1,0:T(8,128)(2,1)S(1)}, bf16[16,1024]{1,0:T(8,128)(2,1)S(1)}, u32[]{:S(2)}, u32[]{:S(2)}) collective-permute-start(bf16[16,1024]{1,0:T(8,128)(2,1)S(1)} %get-tuple-element.28), channel_id=1, source_target_pairs={{0,8},{4,12},{8,0},{12,4},{16,24},{20,28},{24,16},{28,20},{32,40},... | collective-permute-start | bytes 98312 | tf_op jit(solution)/shard_map/ppermute | solution.py:328
  16.6 5.0 %collective-permute-start.3 = (bf16[16,1024]{1,0:T(8,128)(2,1)S(1)}, bf16[16,1024]{1,0:T(8,128)(2,1)S(1)}, u32[]{:S(2)}, u32[]{:S(2)}) collective-permute-start(bf16[16,1024]{1,0:T(8,128)(2,1)S(1)} %get-tuple-element.28), channel_id=1, source_target_pairs={{0,12},{4,0},{8,4},{12,8},{16,28},{20,16},{24,20},{28,24},{32,44},... | collective-permute-start | bytes 98312 | tf_op jit(solution)/shard_map/ppermute | solution.py:328
  21.8 7.6 %collective-permute-start.4 = (bf16[16,1024]{1,0:T(8,128)(2,1)S(1)}, bf16[16,1024]{1,0:T(8,128)(2,1)S(1)}, u32[]{:S(2)}, u32[]{:S(2)}) collective-permute-start(bf16[16,1024]{1,0:T(8,128)(2,1)S(1)} %get-tuple-element.49), channel_id=1, source_target_pairs={{0,16},{4,20},{8,24},{12,28},{16,32},{20,36},{24,40},{28,44},{32,4... | collective-permute-start | bytes 98312 | tf_op jit(solution)/shard_map/ppermute | solution.py:328
  23.1 6.3 %collective-permute-start.5 = (bf16[16,1024]{1,0:T(8,128)(2,1)S(1)}, bf16[16,1024]{1,0:T(8,128)(2,1)S(1)}, u32[]{:S(2)}, u32[]{:S(2)}) collective-permute-start(bf16[16,1024]{1,0:T(8,128)(2,1)S(1)} %get-tuple-element.49), channel_id=1, source_target_pairs={{0,32},{4,36},{8,40},{12,44},{16,48},{20,52},{24,56},{28,60},{32,0... | collective-permute-start | bytes 98312 | tf_op jit(solution)/shard_map/ppermute | solution.py:328
  25.5 3.9 %collective-permute-start.6 = (bf16[16,1024]{1,0:T(8,128)(2,1)S(1)}, bf16[16,1024]{1,0:T(8,128)(2,1)S(1)}, u32[]{:S(2)}, u32[]{:S(2)}) collective-permute-start(bf16[16,1024]{1,0:T(8,128)(2,1)S(1)} %get-tuple-element.49), channel_id=1, source_target_pairs={{0,48},{4,52},{8,56},{12,60},{16,0},{20,4},{24,8},{28,12},{32,16},... | collective-permute-start | bytes 98312 | tf_op jit(solution)/shard_map/ppermute | solution.py:328
  26.7 9.8 %copy-start.3 = (f32[16,1024]{1,0:T(8,128)S(1)}, f32[16,1024]{1,0:T(8,128)}, u32[]{:S(2)}) copy-start(f32[16,1024]{1,0:T(8,128)} %res_ref.7) | copy-start | bytes 196612
  26.7 9.8 %copy-start.4 = (f32[1024]{0:T(1024)S(1)}, f32[1024]{0:T(1024)}, u32[]{:S(2)}) copy-start(f32[1024]{0:T(1024)} %param.12) | copy-start | bytes 12292
  29.5 5.1 %collective-permute-start.7 = (bf16[16,1024]{1,0:T(8,128)(2,1)S(1)}, bf16[16,1024]{1,0:T(8,128)(2,1)S(1)}, u32[]{:S(2)}, u32[]{:S(2)}) collective-permute-start(bf16[16,1024]{1,0:T(8,128)(2,1)S(1)} %fusion.31), channel_id=1, source_target_pairs={{0,64},{4,68},{8,72},{12,76},{16,80},{20,84},{24,88},{28,92},{32,9... | collective-permute-start | bytes 98312 | tf_op jit(solution)/shard_map/ppermute | solution.py:328
  30.9 4.3 %collective-permute-start.8 = (bf16[16,1024]{1,0:T(8,128)(2,1)S(1)}, bf16[16,1024]{1,0:T(8,128)(2,1)S(1)}, u32[]{:S(2)}, u32[]{:S(2)}) collective-permute-start(bf16[16,1024]{1,0:T(8,128)(2,1)S(1)} %fusion.31), channel_id=1, source_target_pairs={{0,128},{4,132},{8,136},{12,140},{16,144},{20,148},{24,152},{28,15... | collective-permute-start | bytes 98312 | tf_op jit(solution)/shard_map/ppermute | solution.py:328
  33.5 2.8 %collective-permute-start.9 = (bf16[16,1024]{1,0:T(8,128)(2,1)S(1)}, bf16[16,1024]{1,0:T(8,128)(2,1)S(1)}, u32[]{:S(2)}, u32[]{:S(2)}) collective-permute-start(bf16[16,1024]{1,0:T(8,128)(2,1)S(1)} %fusion.31), channel_id=1, source_target_pairs={{0,192},{4,196},{8,200},{12,204},{16,208},{20,212},{24,216},{28,22... | collective-permute-start | bytes 98312 | tf_op jit(solution)/shard_map/ppermute | solution.py:328
  41.1 4.6 %collective-permute-start.10 = (bf16[128,1024]{1,0:T(8,128)(2,1)S(1)}, bf16[128,1024]{1,0:T(8,128)(2,1)S(1)}, u32[]{:S(2)}, u32[]{:S(2)}) collective-permute-start(bf16[128,1024]{1,0:T(8,128)(2,1)S(1)} %bitcast.20), channel_id=1, source_target_pairs={{0,1},{1,0},{2,3},{3,2},{4,5},{5,4},{6,7},{7,6},{8,9},{9,8},{10,11... | collective-permute-start | bytes 786440 | tf_op jit(solution)/shard_map/ppermute | solution.py:390
  44.5 1.5 %collective-permute-start.11 = (bf16[128,1024]{1,0:T(8,128)(2,1)S(1)}, bf16[128,1024]{1,0:T(8,128)(2,1)S(1)}, u32[]{:S(2)}, u32[]{:S(2)}) collective-permute-start(bf16[128,1024]{1,0:T(8,128)(2,1)S(1)} %bitcast.23), channel_id=1, source_target_pairs={{0,1},{1,0},{2,3},{3,2},{4,5},{5,4},{6,7},{7,6},{8,9},{9,8},{10,11... | collective-permute-start | bytes 786440 | tf_op jit(solution)/shard_map/ppermute | solution.py:390
  47.3 14.8 %collective-permute-start.16 = (bf16[256,1024]{1,0:T(8,128)(2,1)S(1)}, bf16[256,1024]{1,0:T(8,128)(2,1)S(1)}, u32[]{:S(2)}, u32[]{:S(2)}) collective-permute-start(bf16[256,1024]{1,0:T(8,128)(2,1)S(1)} %share_chunk.4.rest_0_.rest_4_), channel_id=1, source_target_pairs={{0,2},{2,0},{1,3},{3,1},{4,6},{6,4},{5,7},{7,5},{8,10},{10,8},{9,1... | collective-permute-start | bytes 1572872 | tf_op jit(solution)/shard_map/ppermute | solution.py:396
  52.4 2.1 %collective-permute-start.12 = (bf16[128,1024]{1,0:T(8,128)(2,1)S(1)}, bf16[128,1024]{1,0:T(8,128)(2,1)S(1)}, u32[]{:S(2)}, u32[]{:S(2)}) collective-permute-start(bf16[128,1024]{1,0:T(8,128)(2,1)S(1)} %bitcast.26), channel_id=1, source_target_pairs={{0,1},{1,0},{2,3},{3,2},{4,5},{5,4},{6,7},{7,6},{8,9},{9,8},{10,11... | collective-permute-start | bytes 786440 | tf_op jit(solution)/shard_map/ppermute | solution.py:390
  53.3 1.5 %collective-permute-start.13 = (bf16[128,1024]{1,0:T(8,128)(2,1)S(1)}, bf16[128,1024]{1,0:T(8,128)(2,1)S(1)}, u32[]{:S(2)}, u32[]{:S(2)}) collective-permute-start(bf16[128,1024]{1,0:T(8,128)(2,1)S(1)} %bitcast.29), channel_id=1, source_target_pairs={{0,1},{1,0},{2,3},{3,2},{4,5},{5,4},{6,7},{7,6},{8,9},{9,8},{10,11... | collective-permute-start | bytes 786440 | tf_op jit(solution)/shard_map/ppermute | solution.py:390
  56.1 15.6 %collective-permute-start.19 = (bf16[256,1024]{1,0:T(8,128)(2,1)S(1)}, bf16[256,1024]{1,0:T(8,128)(2,1)S(1)}, u32[]{:S(2)}, u32[]{:S(2)}) collective-permute-start(bf16[256,1024]{1,0:T(8,128)(2,1)S(1)} %share_chunk.5.rest_0_.rest_4_), channel_id=1, source_target_pairs={{0,2},{2,0},{1,3},{3,1},{4,6},{6,4},{5,7},{7,5},{8,10},{10,8},{9,1... | collective-permute-start | bytes 1572872 | tf_op jit(solution)/shard_map/ppermute | solution.py:396
  61.2 6.3 %collective-permute-start.14 = (bf16[128,1024]{1,0:T(8,128)(2,1)S(1)}, bf16[128,1024]{1,0:T(8,128)(2,1)S(1)}, u32[]{:S(2)}, u32[]{:S(2)}) collective-permute-start(bf16[128,1024]{1,0:T(8,128)(2,1)S(1)} %bitcast.32), channel_id=1, source_target_pairs={{0,1},{1,0},{2,3},{3,2},{4,5},{5,4},{6,7},{7,6},{8,9},{9,8},{10,11... | collective-permute-start | bytes 786440 | tf_op jit(solution)/shard_map/ppermute | solution.py:390
  62.0 5.6 %collective-permute-start.15 = (bf16[128,1024]{1,0:T(8,128)(2,1)S(1)}, bf16[128,1024]{1,0:T(8,128)(2,1)S(1)}, u32[]{:S(2)}, u32[]{:S(2)}) collective-permute-start(bf16[128,1024]{1,0:T(8,128)(2,1)S(1)} %bitcast.35), channel_id=1, source_target_pairs={{0,1},{1,0},{2,3},{3,2},{4,5},{5,4},{6,7},{7,6},{8,9},{9,8},{10,11... | collective-permute-start | bytes 786440 | tf_op jit(solution)/shard_map/ppermute | solution.py:390
  67.0 2.6 %collective-permute-start.17 = (bf16[128,1024]{1,0:T(8,128)(2,1)S(1)}, bf16[128,1024]{1,0:T(8,128)(2,1)S(1)}, u32[]{:S(2)}, u32[]{:S(2)}) collective-permute-start(bf16[128,1024]{1,0:T(8,128)(2,1)S(1)} %bitcast.16), channel_id=1, source_target_pairs={{0,1},{1,0},{2,3},{3,2},{4,5},{5,4},{6,7},{7,6},{8,9},{9,8},{10,11... | collective-permute-start | bytes 786440 | tf_op jit(solution)/shard_map/ppermute | solution.py:390
  67.5 2.2 %collective-permute-start.18 = (bf16[128,1024]{1,0:T(8,128)(2,1)S(1)}, bf16[128,1024]{1,0:T(8,128)(2,1)S(1)}, u32[]{:S(2)}, u32[]{:S(2)}) collective-permute-start(bf16[128,1024]{1,0:T(8,128)(2,1)S(1)} %bitcast.38), channel_id=1, source_target_pairs={{0,1},{1,0},{2,3},{3,2},{4,5},{5,4},{6,7},{7,6},{8,9},{9,8},{10,11... | collective-permute-start | bytes 786440 | tf_op jit(solution)/shard_map/ppermute | solution.py:390
  68.8 14.2 %collective-permute-start.20 = (bf16[256,1024]{1,0:T(8,128)(2,1)S(1)}, bf16[256,1024]{1,0:T(8,128)(2,1)S(1)}, u32[]{:S(2)}, u32[]{:S(2)}) collective-permute-start(bf16[256,1024]{1,0:T(8,128)(2,1)S(1)} %share_chunk.6.rest_4_), channel_id=1, source_target_pairs={{0,2},{2,0},{1,3},{3,1},{4,6},{6,4},{5,7},{7,5},{8,10},{10,8},{9,1... | collective-permute-start | bytes 1572872 | tf_op jit(solution)/shard_map/ppermute | solution.py:396
  73.0 21.2 %collective-permute-start.21 = (bf16[256,1024]{1,0:T(8,128)(2,1)S(1)}, bf16[256,1024]{1,0:T(8,128)(2,1)S(1)}, u32[]{:S(2)}, u32[]{:S(2)}) collective-permute-start(bf16[256,1024]{1,0:T(8,128)(2,1)S(1)} %share_chunk.7.rest_16_), channel_id=1, source_target_pairs={{0,2},{2,0},{1,3},{3,1},{4,6},{6,4},{5,7},{7,5},{8,10},{10,8},{9,1... | collective-permute-start | bytes 1572872 | tf_op jit(solution)/shard_map/ppermute | solution.py:396
  (3 other events, 21.7 us)

commit v4 on v3

--- a/solution.py
+++ b/solution.py
@@ -10,7 +10,7 @@
 SEG = 8
 LANES = 128
 SPANS = (32, 32, 32, 32)
-PIECE = 128
+PIECES = (2, 2, 2, 2)
 VMEM_LIMIT = 32 * 2**20
 SIBLING = [(0, 1), (1, 0), (2, 3), (3, 2)]
 PARTNER = [(0, 2), (2, 0), (1, 3), (3, 1)]
@@ -80,14 +80,50 @@
     )(key, value, rates)
 
 
-def gate_kernel(first, late, seg_len, q_ref, k_ref, v_ref, lam_ref, res_ref, skip_ref, state_ref, *rest):
+def ahead_kernel(q_ref, k_ref, v_ref, after_ref, q_out, x_out, mark_ref, x_ref):
+    span, pitch = q_ref.shape[1], q_ref.shape[1] + 1
+    mark_ref[...] = jnp.zeros_like(mark_ref)
+    q_out[...] = q_ref[...]
+    for group in range(q_ref.shape[2] // LANES):
+        cols = slice(group * LANES, (group + 1) * LANES)
+        for seg in range(SEG):
+            x = k_ref[seg, :, cols].astype(jnp.float32) * v_ref[seg, :, cols].astype(jnp.float32)
+            x_ref[pl.ds(seg * pitch, span), :] = x
+        for u in range(span):
+            x_out[u * SEG : (u + 1) * SEG, cols] = x_ref[pl.ds(u, SEG, stride=pitch), :]
+
+
+def ahead(query, key, value, after, span, order, width=512):
+    seg, seg_len, ch = query.shape
+    part = pl.BlockSpec((seg, span, width), lambda j: (0, 0, j))
+    cut = lambda rows: pl.BlockSpec((rows, width), lambda j: (0, j))
+    return pl.pallas_call(
+        ahead_kernel,
+        grid=(ch // width,),
+        in_specs=[part, part, part, ANY],
+        out_specs=[part, cut(seg * span), cut(order)],
+        out_shape=[
+            jax.ShapeDtypeStruct((seg, span, ch), query.dtype),
+            jax.ShapeDtypeStruct((seg * span, ch), jnp.float32),
+            jax.ShapeDtypeStruct((order, ch), jnp.float32),
+        ],
+        scratch_shapes=[pltpu.VMEM((seg * (span + 1), LANES), jnp.float32)],
+        compiler_params=pltpu.CompilerParams(vmem_limit_bytes=VMEM_LIMIT),
+        cost_estimate=cost(seg * span * ch, 12 * seg * span * ch),
+        name="ahead",
+    )(query, key, value, after)
+
+
+def gate_kernel(first, count, late, seg_len, q_ref, *rest):
     next_ref, x_ref, y_ref = rest[-3:]
     if first:
-        inc_ref = rest[0]
+        x_ref, lam_ref, res_ref, skip_ref, state_ref, inc_ref = rest[:6]
+    else:
+        k_ref, v_ref, lam_ref, res_ref, skip_ref, state_ref = rest[:6]
     order = lam_ref.shape[0]
     span = q_ref.shape[1]
-    held = PIECE // span
-    g_refs = rest[-3 - SEG // held : -3]
+    held = SEG // count
+    g_refs = rest[-3 - count : -3]
     pitch = span + 1
     for group in range(q_ref.shape[2] // LANES):
         cols = slice(group * LANES, (group + 1) * LANES)
@@ -104,14 +140,17 @@
             ]
 
         skip = skip_ref[:, cols]
-        for seg in range(SEG):
+        for seg in range(0 if first else SEG):
             x = k_ref[seg, :, cols].astype(jnp.float32) * v_ref[seg, :, cols].astype(jnp.float32)
             x_ref[pl.ds(seg * pitch, span), :] = x
 
         def body(it, state):
             for u in range(16):
                 where = pl.ds(it * 16 + u, SEG, stride=pitch)
-                x = x_ref[where, :]
+                if first:
+                    x = x_ref[pl.ds(pl.multiple_of((it * 16 + u) * SEG, SEG), SEG), cols]
+                else:
+                    x = x_ref[where, :]
                 state = tuple(h * d + x for h, d in zip(state, decay))
                 terms = [w * h for w, h in zip(weight, state)]
                 while len(terms) > 1:
@@ -131,26 +170,26 @@
 
 
 def gate_chunk(
-    query, key, value, rates, residues, skip, state, incoming, after, at, span, width=None
+    query, inputs, rates, residues, skip, state, incoming, after, at, span, count, seg_len
 ):
-    seg, seg_len, ch = query.shape
+    seg, _, ch = query.shape
     order = rates.shape[0]
     first = incoming is not None
-    width = width or (512 if span <= 16 else 256)
+    width = 512 if first else 256
     part = pl.BlockSpec((seg, span, width), lambda j: (0, at // span, j))
     cut = lambda rows: pl.BlockSpec((rows, width), lambda j: (0, j))
-    operands = [query, key, value, rates, residues, skip, state]
-    in_specs = [part, part, part, cut(order), cut(order), cut(1), cut(order * seg)]
+    operands = [query, *inputs, rates, residues, skip, state]
+    taken = [cut(seg * span)] if first else [part, part]
+    in_specs = [part, *taken, cut(order), cut(order), cut(1), cut(order * seg)]
     if first:
         operands.append(incoming)
         in_specs.append(cut(order))
     operands.extend(after)
     in_specs.extend([ANY] * len(after))
     rows = seg * span
-    held = PIECE // span
-    count = seg // held
+    held = seg // count
     *gated, state = pl.pallas_call(
-        functools.partial(gate_kernel, first, at, seg_len),
+        functools.partial(gate_kernel, first, count, at, seg_len),
         grid=(ch // width,),
         in_specs=in_specs,
         out_specs=[pl.BlockSpec((held, span, width), lambda j: (0, 0, j))] * count
@@ -164,7 +203,7 @@
         cost_estimate=cost(4 * rows * ch * order, 8 * rows * ch + 8 * order * seg * ch),
         name="gate_chunk",
     )(*operands)
-    return [piece.reshape(PIECE, ch) for piece in gated], state
+    return [piece.reshape(held * span, ch) for piece in gated], state
 
 
 def columns_kernel(at_ref, w_ref, wo_ref, out_ref, mark_ref):
@@ -174,7 +213,7 @@
     out_ref[depth:] = wo_ref[...]
 
 
-def chip_columns(start, count, weight, weight_other, order, width=256):
+def chip_columns(start, count, weight, weight_other, order, pinned, width=256):
     ch = weight.shape[0]
     part = pl.BlockSpec((ch, width), lambda j, at: (0, at[0] + j))
     return pl.pallas_call(
@@ -189,7 +228,7 @@
             ],
         ),
         out_shape=[
-            pltpu.HBM((2 * ch, count), weight.dtype),
+            (pltpu.HBM if pinned else jax.ShapeDtypeStruct)((2 * ch, count), weight.dtype),
             jax.ShapeDtypeStruct((order, ch), jnp.float32),
         ],
         compiler_params=pltpu.CompilerParams(vmem_limit_bytes=VMEM_LIMIT),
@@ -219,11 +258,13 @@
 def share_chunk(mine, other, weights, after):
     count = len(mine)
     depth, half = weights[0].shape
-    rows, ch = count * PIECE, depth // 2
+    ch = depth // 2
+    rows = sum(piece.shape[0] for piece in mine)
+    pieces = [*mine, *other]
     whole = lambda *shape: pl.BlockSpec(shape, lambda: (0, 0))
     return pl.pallas_call(
         functools.partial(share_kernel, count),
-        in_specs=[whole(depth, half)] * 2 + [whole(PIECE, ch)] * (2 * count) + [ANY] * len(after),
+        in_specs=[whole(depth, half)] * 2 + [whole(*piece.shape) for piece in pieces] + [ANY] * len(after),
         out_specs=whole(rows, 2 * half),
         out_shape=jax.ShapeDtypeStruct((rows, 2 * half), jnp.bfloat16),
         compiler_params=pltpu.CompilerParams(vmem_limit_bytes=VMEM_LIMIT),
@@ -247,7 +288,7 @@
     per = ch // width
     counts = [len(mine) for mine, _ in pairs]
     pieces = [piece for mine, other in pairs for piece in [*mine, *other]]
-    rows = [count * PIECE for count in counts]
+    rows = [sum(piece.shape[0] for piece in mine) for mine, _ in pairs]
     columns = pl.BlockSpec((ch, width), lambda j, at: (0, at[0] * per + j))
     return pl.pallas_call(
         functools.partial(own_kernel, counts),
@@ -255,7 +296,7 @@
             num_scalar_prefetch=1,
             grid=(per,),
             in_specs=[columns, columns]
-            + [pl.BlockSpec((PIECE, ch), lambda j, at: (0, 0))] * len(pieces)
+            + [pl.BlockSpec(piece.shape, lambda j, at: (0, 0)) for piece in pieces]
             + [ANY] * len(after),
             out_specs=[pl.BlockSpec((r, width), lambda j, at: (0, j)) for r in rows],
         ),
@@ -367,13 +408,17 @@
     begin = (2 * (1 - chip) + core) * ch
     weight_far, marks = zip(
         *(
-            chip_columns(begin + part * half, half, weight, weight_other, rates.shape[0])
+            chip_columns(
+                begin + part * half, half, weight, weight_other, rates.shape[0], part == 0
+            )
             for part in range(2)
         )
     )
-    incoming = carried_in(last, sent, rates, tok, sizes, {2: marks[0], 1: marks[1]})
     view = lambda part: part.reshape(SEG, seg_len, ch)
     query, key, value = (in_hbm(view(part)) for part in (query, key, value))
+    query_ahead, steps, mark = ahead(query, key, value, sent, SPANS[0], rates.shape[0])
+    marks = {2: mark, 1: marks[0], 0: marks[1]}
+    incoming = carried_in(last, sent, rates, tok, sizes, marks)
     state, extra = before, incoming
     at = 0
     parts, shares, came = [], [], []
@@ -381,9 +426,10 @@
 
     def gate(i, after):
         nonlocal state, extra, at
+        first = [query_ahead, [steps]]
         gated, state = gate_chunk(
-            query, key, value, rates, residues, skip_gain[None],
-            state, extra, after, at, SPANS[i],
+            *([query, [key, value]] if i else first), rates, residues, skip_gain[None],
+            state, extra, after, at, SPANS[i], PIECES[i], seg_len,
         )
         extra = None
         gates.append(gated)

time: 95.6 us -> 93.7 us (0.980)
    ppermute x9, waiting for transfers between devices: 1.76 us -> 0.57 us  [carried_in(): lax.ppermute(sent, 'seq', shifted(sizes, dim, hop, True))]
    pallas_call x2, Pallas kernels: 5.33 us -> 4.35 us  [chip_columns(): pl.pallas_call(columns_kernel, grid_spec=pltpu.PrefetchScalarGridSpec(num...]
    pallas_call x4 -> x5, Pallas kernels: 18 us -> 18.1 us  [the longest x4 16.5 us: gate_chunk(): pl.pallas_call(functools.partial(gate_kernel, first, count, at, seg_len),...]
  transfers between devices with their start and end apart: 22 -> 22, of which waited for: 9 -> 8; matrix products, arithmetic and copies ran while one was open for 0% -> 0% of each run, Pallas kernels for 41% -> 43%
where the time goes in v4:
time: 93.7 us; the launch traced here: 93.3 us
  Pallas kernels  44.9 us (48%)
  starting transfers between devices  31 us (33%)
  waiting for transfers between devices  16.7 us (18%)
    ppermute x9, starting transfers between devices, carried_in(): lax.ppermute(sent, 'seq', shifted(sizes, dim, hop, True))  18.8 us
    pallas_call x4, Pallas kernels, gate_chunk(): pl.pallas_call(functools.partial(gate_kernel, first, count, at, seg_len),...  16.5 us
    ppermute x4, waiting for transfers between devices, share(): came.append(lax.ppermute(shares[-1], 'tp', PARTNER))  13.3 us
    pallas_call x1, Pallas kernels, end_states(): pl.pallas_call(functools.partial(end_kernel, seg_len), grid=(ch // width,...  6.92 us
    pallas_call x1, Pallas kernels, own_shares(): pl.pallas_call(functools.partial(own_kernel, counts), grid_spec=pltpu.Pre...  6.62 us
    ppermute x8, starting transfers between devices, gate(): others.append([lax.ppermute(piece, 'tp', SIBLING) for piece in gated])  5.73 us
    pallas_call x4, Pallas kernels, share_chunk(): pl.pallas_call(functools.partial(share_kernel, count), in_specs=[whole(de...  5.02 us
    pallas_call x2, Pallas kernels, chip_columns(): pl.pallas_call(columns_kernel, grid_spec=pltpu.PrefetchScalarGridSpec(num...  4.35 us
  transfers between devices with their start and end apart: 22, of which 8 were waited for; matrix products, arithmetic and copies ran while one was open for 0% of the time, Pallas kernels for 43%

profile of v4, /device:TPU:1, one launch (start us, length us, event | category | flops | bytes accessed | tf_op | source)
XLA Modules:
  0.0 93.3 jit_solution(6492999224743096206)
XLA Ops:
  0.0 3.2 %collective-permute-start = (bf16[1024,4096]{1,0:T(8,128)(2,1)}, bf16[1024,4096]{1,0:T(8,128)(2,1)}, u32[]{:S(2)}, u32[]{:S(2)}) collective-permute-start(bf16[1024,4096]{1,0:T(8,128)(2,1)} %w_ref.5), channel_id=1, source_target_pairs={{0,1},{1,0},{2,3},{3,2},{4,5},{5,4},{6,7},{7,6},{8,9},{9,8},{10,11... | collective-permute-start | bytes 25165832 | tf_op jit(solution)/shard_map/ppermute | solution.py:404
  3.2 6.9 %end_states.1 = (f32[16,1024]{1,0:T(8,128)S(1)}, f32[128,1024]{1,0:T(8,128)S(1)}, bf16[16,1024]{1,0:T(8,128)(2,1)S(1)}) custom-call(bf16[1024,1024]{1,0:T(8,128)(2,1)} %k_ref.1, bf16[1024,1024]{1,0:T(8,128)(2,1)} %v_ref.1, f32[16,1024]{1,0:T(8,128)} %rest_2_.7), custom_call_target="tpu_custom_call" | custom-call | flops 1 | bytes 1 | tf_op jit(solution)/shard_map/end_states/pallas_call | solution.py:66
  10.2 1.3 %collective-permute-start.1 = (bf16[16,1024]{1,0:T(8,128)(2,1)S(1)}, bf16[16,1024]{1,0:T(8,128)(2,1)S(1)}, u32[]{:S(2)}, u32[]{:S(2)}) collective-permute-start(bf16[16,1024]{1,0:T(8,128)(2,1)S(1)} %get-tuple-element.30.after_ref), channel_id=1, source_target_pairs={{0,4},{4,8},{8,12},{12,0},{16,20},{20,24},{24,28},{28,16},{32,36},... | collective-permute-start | bytes 98312 | tf_op jit(solution)/shard_map/ppermute | solution.py:369
  11.5 5.1 %collective-permute-start.2 = (bf16[16,1024]{1,0:T(8,128)(2,1)S(1)}, bf16[16,1024]{1,0:T(8,128)(2,1)S(1)}, u32[]{:S(2)}, u32[]{:S(2)}) collective-permute-start(bf16[16,1024]{1,0:T(8,128)(2,1)S(1)} %get-tuple-element.30.after_ref), channel_id=1, source_target_pairs={{0,8},{4,12},{8,0},{12,4},{16,24},{20,28},{24,16},{28,20},{32,40},... | collective-permute-start | bytes 98312 | tf_op jit(solution)/shard_map/ppermute | solution.py:369
  16.6 2.4 %collective-permute-start.3 = (bf16[16,1024]{1,0:T(8,128)(2,1)S(1)}, bf16[16,1024]{1,0:T(8,128)(2,1)S(1)}, u32[]{:S(2)}, u32[]{:S(2)}) collective-permute-start(bf16[16,1024]{1,0:T(8,128)(2,1)S(1)} %get-tuple-element.30.after_ref), channel_id=1, source_target_pairs={{0,12},{4,0},{8,4},{12,8},{16,28},{20,16},{24,20},{28,24},{32,44},... | collective-permute-start | bytes 98312 | tf_op jit(solution)/shard_map/ppermute | solution.py:369
  19.0 1.6 %ahead.1 = (bf16[8,32,1024]{2,1,0:T(8,128)(2,1)S(1)}, f32[256,1024]{1,0:T(8,128)S(1)}, f32[16,1024]{1,0:T(8,128)S(1)}) custom-call(bf16[8,128,1024]{2,1,0:T(8,128)(2,1)} %bitcast.53, bf16[8,128,1024]{2,1,0:T(8,128)(2,1)} %bitcast.45, bf16[8,128,1024]{2,1,0:T(8,128)(2,1)} %bitcast.49, bf16[16,1024]{1,0:T(8,128)(2,1)S(1)} %get-tuple-element.30.after_ref), custom_call_target="tpu_custom_call" | custom-call | flops 1 | bytes 1 | tf_op jit(solution)/shard_map/ahead/pallas_call | solution.py:100
  21.4 1.3 %collective-permute-start.4 = (bf16[16,1024]{1,0:T(8,128)(2,1)S(1)}, bf16[16,1024]{1,0:T(8,128)(2,1)S(1)}, u32[]{:S(2)}, u32[]{:S(2)}) collective-permute-start(bf16[16,1024]{1,0:T(8,128)(2,1)S(1)} %get-tuple-element.55), channel_id=1, source_target_pairs={{0,16},{4,20},{8,24},{12,28},{16,32},{20,36},{24,40},{28,44},{32,4... | collective-permute-start | bytes 98312 | tf_op jit(solution)/shard_map/ppermute | solution.py:369
  22.7 2.5 %collective-permute-start.5 = (bf16[16,1024]{1,0:T(8,128)(2,1)S(1)}, bf16[16,1024]{1,0:T(8,128)(2,1)S(1)}, u32[]{:S(2)}, u32[]{:S(2)}) collective-permute-start(bf16[16,1024]{1,0:T(8,128)(2,1)S(1)} %get-tuple-element.55), channel_id=1, source_target_pairs={{0,32},{4,36},{8,40},{12,44},{16,48},{20,52},{24,56},{28,60},{32,0... | collective-permute-start | bytes 98312 | tf_op jit(solution)/shard_map/ppermute | solution.py:369
  26.3 2.6 %chip_columns.2 = (bf16[2048,512]{1,0:T(8,128)(2,1)}, f32[16,1024]{1,0:T(8,128)S(1)}) custom-call(s32[1]{0:T(128)} %bitcast.5.at_ref, bf16[1024,4096]{1,0:T(8,128)(2,1)} %w_ref.5, bf16[1024,4096]{1,0:T(8,128)(2,1)} %collective-permute-done.wo_ref), custom_call_target="tpu_custom_call" | custom-call | flops 1 | bytes 1 | tf_op jit(solution)/shard_map/chip_columns/pallas_call | solution.py:219
  29.1 1.4 %collective-permute-start.7 = (bf16[16,1024]{1,0:T(8,128)(2,1)S(1)}, bf16[16,1024]{1,0:T(8,128)(2,1)S(1)}, u32[]{:S(2)}, u32[]{:S(2)}) collective-permute-start(bf16[16,1024]{1,0:T(8,128)(2,1)S(1)} %fusion.31), channel_id=1, source_target_pairs={{0,64},{4,68},{8,72},{12,76},{16,80},{20,84},{24,88},{28,92},{32,9... | collective-permute-start | bytes 98312 | tf_op jit(solution)/shard_map/ppermute | solution.py:369
  30.4 2.6 %collective-permute-start.8 = (bf16[16,1024]{1,0:T(8,128)(2,1)S(1)}, bf16[16,1024]{1,0:T(8,128)(2,1)S(1)}, u32[]{:S(2)}, u32[]{:S(2)}) collective-permute-start(bf16[16,1024]{1,0:T(8,128)(2,1)S(1)} %fusion.31), channel_id=1, source_target_pairs={{0,128},{4,132},{8,136},{12,140},{16,144},{20,148},{24,152},{28,15... | collective-permute-start | bytes 98312 | tf_op jit(solution)/shard_map/ppermute | solution.py:369
  34.1 1.8 %chip_columns.3 = (bf16[2048,512]{1,0:T(8,128)(2,1)S(1)}, f32[16,1024]{1,0:T(8,128)S(1)}) custom-call(s32[1]{0:T(128)} %bitcast.6.at_ref, bf16[1024,4096]{1,0:T(8,128)(2,1)} %w_ref.5, bf16[1024,4096]{1,0:T(8,128)(2,1)} %collective-permute-done.wo_ref), custom_call_target="tpu_custom_call" | custom-call | flops 1 | bytes 1 | tf_op jit(solution)/shard_map/chip_columns/pallas_call | solution.py:219
  36.1 3.0 %gate_chunk.4 = (bf16[4,32,1024]{2,1,0:T(8,128)(2,1)S(1)}, bf16[4,32,1024]{2,1,0:T(8,128)(2,1)S(1)}, f32[128,1024]{1,0:T(8,128)S(1)}) custom-call(bf16[8,32,1024]{2,1,0:T(8,128)(2,1)S(1)} %get-tuple-element.31.q_ref, f32[256,1024]{1,0:T(8,128)S(1)} %get-tuple-element.32.rest_0_, f32[16,1024]{1,0:T(8,128)S(1)} %copy-done.1, f32[16,1024]{1,0:T(8,128)S(1)} %copy-done.2, ...), custom_call_target="tpu_custom_call" | custom-call | flops 1 | bytes 1 | tf_op jit(solution)/shard_map/gate_chunk/pallas_call | solution.py:191
  39.1 3.3 %collective-permute-start.10 = (bf16[128,1024]{1,0:T(8,128)(2,1)S(1)}, bf16[128,1024]{1,0:T(8,128)(2,1)S(1)}, u32[]{:S(2)}, u32[]{:S(2)}) collective-permute-start(bf16[128,1024]{1,0:T(8,128)(2,1)S(1)} %bitcast.20), channel_id=1, source_target_pairs={{0,1},{1,0},{2,3},{3,2},{4,5},{5,4},{6,7},{7,6},{8,9},{9,8},{10,11... | collective-permute-start | bytes 786440 | tf_op jit(solution)/shard_map/ppermute | solution.py:436
  46.1 4.3 %gate_chunk.5 = (bf16[4,32,1024]{2,1,0:T(8,128)(2,1)S(1)}, bf16[4,32,1024]{2,1,0:T(8,128)(2,1)S(1)}, f32[128,1024]{1,0:T(8,128)S(1)}) custom-call(bf16[8,128,1024]{2,1,0:T(8,128)(2,1)} %bitcast.54, bf16[8,128,1024]{2,1,0:T(8,128)(2,1)} %bitcast.46, bf16[8,128,1024]{2,1,0:T(8,128)(2,1)} %bitcast.50, f32[16,1024]{1,0:T(8,128)S(1)} %copy-done.1, ...), custom_call_target="tpu_custom_call" | custom-call | flops 1 | bytes 1 | tf_op jit(solution)/shard_map/gate_chunk/pallas_call | solution.py:191
  52.7 1.3 %share_chunk.5.rest_6_.rest_4_ = bf16[256,1024]{1,0:T(8,128)(2,1)S(1)} custom-call(bf16[2048,512]{1,0:T(8,128)(2,1)S(1)} %copy-done, bf16[2048,512]{1,0:T(8,128)(2,1)S(1)} %get-tuple-element.42.wx_ref, bf16[128,1024]{1,0:T(8,128)(2,1)S(1)} %bitcast.27, bf16[128,1024]{1,0:T(8,128)(2,1)S(1)} %bitcast.30, ...), custom_call_target="tpu_custom_call" | custom-call | flops 1 | bytes 1 | tf_op jit(solution)/shard_map/share_chunk/pallas_call | solution.py:265
  54.9 4.3 %gate_chunk.6 = (bf16[4,32,1024]{2,1,0:T(8,128)(2,1)S(1)}, bf16[4,32,1024]{2,1,0:T(8,128)(2,1)S(1)}, f32[128,1024]{1,0:T(8,128)S(1)}) custom-call(bf16[8,128,1024]{2,1,0:T(8,128)(2,1)} %bitcast.55, bf16[8,128,1024]{2,1,0:T(8,128)(2,1)} %bitcast.47, bf16[8,128,1024]{2,1,0:T(8,128)(2,1)} %bitcast.51, f32[16,1024]{1,0:T(8,128)S(1)} %copy-done.1, ...), custom_call_target="tpu_custom_call" | custom-call | flops 1 | bytes 1 | tf_op jit(solution)/shard_map/gate_chunk/pallas_call | solution.py:191
  60.0 4.9 %gate_chunk.7 = (bf16[4,32,1024]{2,1,0:T(8,128)(2,1)S(1)}, bf16[4,32,1024]{2,1,0:T(8,128)(2,1)S(1)}, f32[128,1024]{1,0:T(8,128)}) custom-call(bf16[8,128,1024]{2,1,0:T(8,128)(2,1)} %bitcast.56, bf16[8,128,1024]{2,1,0:T(8,128)(2,1)} %bitcast.48, bf16[8,128,1024]{2,1,0:T(8,128)(2,1)} %bitcast.52, f32[16,1024]{1,0:T(8,128)S(1)} %copy-done.1, ...), custom_call_target="tpu_custom_call" | custom-call | flops 1 | bytes 1 | tf_op jit(solution)/shard_map/gate_chunk/pallas_call | solution.py:191
  65.6 1.3 %share_chunk.6.rest_4_ = bf16[256,1024]{1,0:T(8,128)(2,1)S(1)} custom-call(bf16[2048,512]{1,0:T(8,128)(2,1)S(1)} %copy-done, bf16[2048,512]{1,0:T(8,128)(2,1)S(1)} %get-tuple-element.42.wx_ref, bf16[128,1024]{1,0:T(8,128)(2,1)S(1)} %bitcast.33, bf16[128,1024]{1,0:T(8,128)(2,1)S(1)} %bitcast.36, ...), custom_call_target="tpu_custom_call" | custom-call | flops 1 | bytes 1 | tf_op jit(solution)/shard_map/share_chunk/pallas_call | solution.py:265
  67.6 2.3 %collective-permute-done.19.rest_5_.far_ref = bf16[256,1024]{1,0:T(8,128)(2,1)S(1)} collective-permute-done((bf16[256,1024]{1,0:T(8,128)(2,1)S(1)}, bf16[256,1024]{1,0:T(8,128)(2,1)S(1)}, u32[]{:S(2)}, u32[]{:S(2)}) %collective-permute-start.19) | collective-permute-done | bytes 524320 | tf_op jit(solution)/shard_map/ppermute | solution.py:442
  69.9 1.2 %share_chunk.7.rest_16_ = bf16[256,1024]{1,0:T(8,128)(2,1)S(1)} custom-call(bf16[2048,512]{1,0:T(8,128)(2,1)S(1)} %copy-done, bf16[2048,512]{1,0:T(8,128)(2,1)S(1)} %get-tuple-element.42.wx_ref, bf16[128,1024]{1,0:T(8,128)(2,1)S(1)} %bitcast.18, bf16[128,1024]{1,0:T(8,128)(2,1)S(1)} %bitcast.39, ...), custom_call_target="tpu_custom_call" | custom-call | flops 1 | bytes 1 | tf_op jit(solution)/shard_map/share_chunk/pallas_call | solution.py:265
  71.9 9.3 %collective-permute-done.20.rest_17_.far_ref = bf16[256,1024]{1,0:T(8,128)(2,1)S(1)} collective-permute-done((bf16[256,1024]{1,0:T(8,128)(2,1)S(1)}, bf16[256,1024]{1,0:T(8,128)(2,1)S(1)}, u32[]{:S(2)}, u32[]{:S(2)}) %collective-permute-start.20) | collective-permute-done | bytes 524320 | tf_op jit(solution)/shard_map/ppermute | solution.py:442
  81.1 6.6 %own_shares.1 = (f32[256,1024]{1,0:T(8,128)S(1)}, f32[256,1024]{1,0:T(8,128)S(1)}, f32[256,1024]{1,0:T(8,128)S(1)}, f32[256,1024]{1,0:T(8,128)S(1)}) custom-call(s32[1]{0:T(128)} %bitcast.at_ref, bf16[1024,4096]{1,0:T(8,128)(2,1)} %w_ref.5, bf16[1024,4096]{1,0:T(8,128)(2,1)} %collective-permute-done.wo_ref, bf16[128,1024]{1,0:T(8,128)(2,1)S(1)} %bitcast.22, ...), custom_call_target="tpu_custom_call" | custom-call | flops 1 | bytes 1 | tf_op jit(solution)/shard_map/own_shares/pallas_call | solution.py:293
  90.7 1.7 %collective-permute-done.21.far_ref = bf16[256,1024]{1,0:T(8,128)(2,1)S(1)} collective-permute-done((bf16[256,1024]{1,0:T(8,128)(2,1)S(1)}, bf16[256,1024]{1,0:T(8,128)(2,1)S(1)}, u32[]{:S(2)}, u32[]{:S(2)}) %collective-permute-start.21) | collective-permute-done | bytes 524320 | tf_op jit(solution)/shard_map/ppermute | solution.py:442
  (48 shorter events, 16.9 us)
Async XLA Ops:
  0.0 26.3 %collective-permute-start = (bf16[1024,4096]{1,0:T(8,128)(2,1)}, bf16[1024,4096]{1,0:T(8,128)(2,1)}, u32[]{:S(2)}, u32[]{:S(2)}) collective-permute-start(bf16[1024,4096]{1,0:T(8,128)(2,1)} %w_ref.5), channel_id=1, source_target_pairs={{0,1},{1,0},{2,3},{3,2},{4,5},{5,4},{6,7},{7,6},{8,9},{9,8},{10,11... | collective-permute-start | bytes 25165832 | tf_op jit(solution)/shard_map/ppermute | solution.py:404
  10.2 10.6 %collective-permute-start.1 = (bf16[16,1024]{1,0:T(8,128)(2,1)S(1)}, bf16[16,1024]{1,0:T(8,128)(2,1)S(1)}, u32[]{:S(2)}, u32[]{:S(2)}) collective-permute-start(bf16[16,1024]{1,0:T(8,128)(2,1)S(1)} %get-tuple-element.30.after_ref), channel_id=1, source_target_pairs={{0,4},{4,8},{8,12},{12,0},{16,20},{20,24},{24,28},{28,16},{32,36},... | collective-permute-start | bytes 98312 | tf_op jit(solution)/shard_map/ppermute | solution.py:369
  11.5 9.2 %collective-permute-start.2 = (bf16[16,1024]{1,0:T(8,128)(2,1)S(1)}, bf16[16,1024]{1,0:T(8,128)(2,1)S(1)}, u32[]{:S(2)}, u32[]{:S(2)}) collective-permute-start(bf16[16,1024]{1,0:T(8,128)(2,1)S(1)} %get-tuple-element.30.after_ref), channel_id=1, source_target_pairs={{0,8},{4,12},{8,0},{12,4},{16,24},{20,28},{24,16},{28,20},{32,40},... | collective-permute-start | bytes 98312 | tf_op jit(solution)/shard_map/ppermute | solution.py:369
  16.6 4.7 %collective-permute-start.3 = (bf16[16,1024]{1,0:T(8,128)(2,1)S(1)}, bf16[16,1024]{1,0:T(8,128)(2,1)S(1)}, u32[]{:S(2)}, u32[]{:S(2)}) collective-permute-start(bf16[16,1024]{1,0:T(8,128)(2,1)S(1)} %get-tuple-element.30.after_ref), channel_id=1, source_target_pairs={{0,12},{4,0},{8,4},{12,8},{16,28},{20,16},{24,20},{28,24},{32,44},... | collective-permute-start | bytes 98312 | tf_op jit(solution)/shard_map/ppermute | solution.py:369
  19.0 2.3 %copy-start.1 = (f32[16,1024]{1,0:T(8,128)S(1)}, f32[16,1024]{1,0:T(8,128)}, u32[]{:S(2)}) copy-start(f32[16,1024]{1,0:T(8,128)} %rest_2_.7) | copy-start | bytes 196612
  21.4 7.5 %collective-permute-start.4 = (bf16[16,1024]{1,0:T(8,128)(2,1)S(1)}, bf16[16,1024]{1,0:T(8,128)(2,1)S(1)}, u32[]{:S(2)}, u32[]{:S(2)}) collective-permute-start(bf16[16,1024]{1,0:T(8,128)(2,1)S(1)} %get-tuple-element.55), channel_id=1, source_target_pairs={{0,16},{4,20},{8,24},{12,28},{16,32},{20,36},{24,40},{28,44},{32,4... | collective-permute-start | bytes 98312 | tf_op jit(solution)/shard_map/ppermute | solution.py:369
  22.7 6.2 %collective-permute-start.5 = (bf16[16,1024]{1,0:T(8,128)(2,1)S(1)}, bf16[16,1024]{1,0:T(8,128)(2,1)S(1)}, u32[]{:S(2)}, u32[]{:S(2)}) collective-permute-start(bf16[16,1024]{1,0:T(8,128)(2,1)S(1)} %get-tuple-element.55), channel_id=1, source_target_pairs={{0,32},{4,36},{8,40},{12,44},{16,48},{20,52},{24,56},{28,60},{32,0... | collective-permute-start | bytes 98312 | tf_op jit(solution)/shard_map/ppermute | solution.py:369
  25.1 3.8 %collective-permute-start.6 = (bf16[16,1024]{1,0:T(8,128)(2,1)S(1)}, bf16[16,1024]{1,0:T(8,128)(2,1)S(1)}, u32[]{:S(2)}, u32[]{:S(2)}) collective-permute-start(bf16[16,1024]{1,0:T(8,128)(2,1)S(1)} %get-tuple-element.55), channel_id=1, source_target_pairs={{0,48},{4,52},{8,56},{12,60},{16,0},{20,4},{24,8},{28,12},{32,16},... | collective-permute-start | bytes 98312 | tf_op jit(solution)/shard_map/ppermute | solution.py:369
  29.1 6.8 %collective-permute-start.7 = (bf16[16,1024]{1,0:T(8,128)(2,1)S(1)}, bf16[16,1024]{1,0:T(8,128)(2,1)S(1)}, u32[]{:S(2)}, u32[]{:S(2)}) collective-permute-start(bf16[16,1024]{1,0:T(8,128)(2,1)S(1)} %fusion.31), channel_id=1, source_target_pairs={{0,64},{4,68},{8,72},{12,76},{16,80},{20,84},{24,88},{28,92},{32,9... | collective-permute-start | bytes 98312 | tf_op jit(solution)/shard_map/ppermute | solution.py:369
  30.4 5.5 %collective-permute-start.8 = (bf16[16,1024]{1,0:T(8,128)(2,1)S(1)}, bf16[16,1024]{1,0:T(8,128)(2,1)S(1)}, u32[]{:S(2)}, u32[]{:S(2)}) collective-permute-start(bf16[16,1024]{1,0:T(8,128)(2,1)S(1)} %fusion.31), channel_id=1, source_target_pairs={{0,128},{4,132},{8,136},{12,140},{16,144},{20,148},{24,152},{28,15... | collective-permute-start | bytes 98312 | tf_op jit(solution)/shard_map/ppermute | solution.py:369
  33.0 2.9 %collective-permute-start.9 = (bf16[16,1024]{1,0:T(8,128)(2,1)S(1)}, bf16[16,1024]{1,0:T(8,128)(2,1)S(1)}, u32[]{:S(2)}, u32[]{:S(2)}) collective-permute-start(bf16[16,1024]{1,0:T(8,128)(2,1)S(1)} %fusion.31), channel_id=1, source_target_pairs={{0,192},{4,196},{8,200},{12,204},{16,208},{20,212},{24,216},{28,22... | collective-permute-start | bytes 98312 | tf_op jit(solution)/shard_map/ppermute | solution.py:369
  35.9 8.1 %copy-start = (bf16[2048,512]{1,0:T(8,128)(2,1)S(1)}, bf16[2048,512]{1,0:T(8,128)(2,1)}, u32[]{:S(2)}) copy-start(bf16[2048,512]{1,0:T(8,128)(2,1)} %get-tuple-element.41.w_ref) | copy-start | bytes 6291460
  39.1 4.5 %collective-permute-start.10 = (bf16[128,1024]{1,0:T(8,128)(2,1)S(1)}, bf16[128,1024]{1,0:T(8,128)(2,1)S(1)}, u32[]{:S(2)}, u32[]{:S(2)}) collective-permute-start(bf16[128,1024]{1,0:T(8,128)(2,1)S(1)} %bitcast.20), channel_id=1, source_target_pairs={{0,1},{1,0},{2,3},{3,2},{4,5},{5,4},{6,7},{7,6},{8,9},{9,8},{10,11... | collective-permute-start | bytes 786440 | tf_op jit(solution)/shard_map/ppermute | solution.py:436
  42.5 1.5 %collective-permute-start.11 = (bf16[128,1024]{1,0:T(8,128)(2,1)S(1)}, bf16[128,1024]{1,0:T(8,128)(2,1)S(1)}, u32[]{:S(2)}, u32[]{:S(2)}) collective-permute-start(bf16[128,1024]{1,0:T(8,128)(2,1)S(1)} %bitcast.23), channel_id=1, source_target_pairs={{0,1},{1,0},{2,3},{3,2},{4,5},{5,4},{6,7},{7,6},{8,9},{9,8},{10,11... | collective-permute-start | bytes 786440 | tf_op jit(solution)/shard_map/ppermute | solution.py:436
  45.3 14.8 %collective-permute-start.16 = (bf16[256,1024]{1,0:T(8,128)(2,1)S(1)}, bf16[256,1024]{1,0:T(8,128)(2,1)S(1)}, u32[]{:S(2)}, u32[]{:S(2)}) collective-permute-start(bf16[256,1024]{1,0:T(8,128)(2,1)S(1)} %share_chunk.4.rest_6_.rest_4_), channel_id=1, source_target_pairs={{0,2},{2,0},{1,3},{3,1},{4,6},{6,4},{5,7},{7,5},{8,10},{10,8},{9,1... | collective-permute-start | bytes 1572872 | tf_op jit(solution)/shard_map/ppermute | solution.py:442
  50.4 1.9 %collective-permute-start.12 = (bf16[128,1024]{1,0:T(8,128)(2,1)S(1)}, bf16[128,1024]{1,0:T(8,128)(2,1)S(1)}, u32[]{:S(2)}, u32[]{:S(2)}) collective-permute-start(bf16[128,1024]{1,0:T(8,128)(2,1)S(1)} %bitcast.26), channel_id=1, source_target_pairs={{0,1},{1,0},{2,3},{3,2},{4,5},{5,4},{6,7},{7,6},{8,9},{9,8},{10,11... | collective-permute-start | bytes 786440 | tf_op jit(solution)/shard_map/ppermute | solution.py:436
  51.2 1.5 %collective-permute-start.13 = (bf16[128,1024]{1,0:T(8,128)(2,1)S(1)}, bf16[128,1024]{1,0:T(8,128)(2,1)S(1)}, u32[]{:S(2)}, u32[]{:S(2)}) collective-permute-start(bf16[128,1024]{1,0:T(8,128)(2,1)S(1)} %bitcast.29), channel_id=1, source_target_pairs={{0,1},{1,0},{2,3},{3,2},{4,5},{5,4},{6,7},{7,6},{8,9},{9,8},{10,11... | collective-permute-start | bytes 786440 | tf_op jit(solution)/shard_map/ppermute | solution.py:436
  54.0 15.9 %collective-permute-start.19 = (bf16[256,1024]{1,0:T(8,128)(2,1)S(1)}, bf16[256,1024]{1,0:T(8,128)(2,1)S(1)}, u32[]{:S(2)}, u32[]{:S(2)}) collective-permute-start(bf16[256,1024]{1,0:T(8,128)(2,1)S(1)} %share_chunk.5.rest_6_.rest_4_), channel_id=1, source_target_pairs={{0,2},{2,0},{1,3},{3,1},{4,6},{6,4},{5,7},{7,5},{8,10},{10,8},{9,1... | collective-permute-start | bytes 1572872 | tf_op jit(solution)/shard_map/ppermute | solution.py:442
  59.2 6.4 %collective-permute-start.14 = (bf16[128,1024]{1,0:T(8,128)(2,1)S(1)}, bf16[128,1024]{1,0:T(8,128)(2,1)S(1)}, u32[]{:S(2)}, u32[]{:S(2)}) collective-permute-start(bf16[128,1024]{1,0:T(8,128)(2,1)S(1)} %bitcast.32), channel_id=1, source_target_pairs={{0,1},{1,0},{2,3},{3,2},{4,5},{5,4},{6,7},{7,6},{8,9},{9,8},{10,11... | collective-permute-start | bytes 786440 | tf_op jit(solution)/shard_map/ppermute | solution.py:436
  59.9 5.7 %collective-permute-start.15 = (bf16[128,1024]{1,0:T(8,128)(2,1)S(1)}, bf16[128,1024]{1,0:T(8,128)(2,1)S(1)}, u32[]{:S(2)}, u32[]{:S(2)}) collective-permute-start(bf16[128,1024]{1,0:T(8,128)(2,1)S(1)} %bitcast.35), channel_id=1, source_target_pairs={{0,1},{1,0},{2,3},{3,2},{4,5},{5,4},{6,7},{7,6},{8,9},{9,8},{10,11... | collective-permute-start | bytes 786440 | tf_op jit(solution)/shard_map/ppermute | solution.py:436
  65.0 2.6 %collective-permute-start.17 = (bf16[128,1024]{1,0:T(8,128)(2,1)S(1)}, bf16[128,1024]{1,0:T(8,128)(2,1)S(1)}, u32[]{:S(2)}, u32[]{:S(2)}) collective-permute-start(bf16[128,1024]{1,0:T(8,128)(2,1)S(1)} %bitcast.16), channel_id=1, source_target_pairs={{0,1},{1,0},{2,3},{3,2},{4,5},{5,4},{6,7},{7,6},{8,9},{9,8},{10,11... | collective-permute-start | bytes 786440 | tf_op jit(solution)/shard_map/ppermute | solution.py:436
  65.6 2.0 %collective-permute-start.18 = (bf16[128,1024]{1,0:T(8,128)(2,1)S(1)}, bf16[128,1024]{1,0:T(8,128)(2,1)S(1)}, u32[]{:S(2)}, u32[]{:S(2)}) collective-permute-start(bf16[128,1024]{1,0:T(8,128)(2,1)S(1)} %bitcast.38), channel_id=1, source_target_pairs={{0,1},{1,0},{2,3},{3,2},{4,5},{5,4},{6,7},{7,6},{8,9},{9,8},{10,11... | collective-permute-start | bytes 786440 | tf_op jit(solution)/shard_map/ppermute | solution.py:436
  66.9 14.2 %collective-permute-start.20 = (bf16[256,1024]{1,0:T(8,128)(2,1)S(1)}, bf16[256,1024]{1,0:T(8,128)(2,1)S(1)}, u32[]{:S(2)}, u32[]{:S(2)}) collective-permute-start(bf16[256,1024]{1,0:T(8,128)(2,1)S(1)} %share_chunk.6.rest_4_), channel_id=1, source_target_pairs={{0,2},{2,0},{1,3},{3,1},{4,6},{6,4},{5,7},{7,5},{8,10},{10,8},{9,1... | collective-permute-start | bytes 1572872 | tf_op jit(solution)/shard_map/ppermute | solution.py:442
  71.2 21.2 %collective-permute-start.21 = (bf16[256,1024]{1,0:T(8,128)(2,1)S(1)}, bf16[256,1024]{1,0:T(8,128)(2,1)S(1)}, u32[]{:S(2)}, u32[]{:S(2)}) collective-permute-start(bf16[256,1024]{1,0:T(8,128)(2,1)S(1)} %share_chunk.7.rest_16_), channel_id=1, source_target_pairs={{0,2},{2,0},{1,3},{3,1},{4,6},{6,4},{5,7},{7,5},{8,10},{10,8},{9,1... | collective-permute-start | bytes 1572872 | tf_op jit(solution)/shard_map/ppermute | solution.py:442
  (2 other events, 4.0 us)

commit v5 on v4

--- a/solution.py
+++ b/solution.py
@@ -52,10 +52,10 @@
             for step, hop in hops.items():
                 run = run + jnp.where(row >= step, hop[n] * pltpu.roll(run, step, 0), 0.0)
             last_ref[n : n + 1, cols] = run[SEG - 1 : SEG]
-            sent_ref[n : n + 1, cols] = run[SEG - 1 : SEG].astype(jnp.bfloat16)
             before_ref[n * SEG : (n + 1) * SEG, cols] = jnp.where(
                 row >= 1, pltpu.roll(run, 1, 0), 0.0
             )
+        sent_ref[:, cols] = last_ref[:, cols].astype(jnp.bfloat16)
 
 
 def end_states(key, value, rates, width=256):
@@ -73,7 +73,7 @@
             jax.ShapeDtypeStruct((order * SEG, ch), jnp.float32),
             jax.ShapeDtypeStruct((order, ch), jnp.bfloat16),
         ],
-        scratch_shapes=[pltpu.VMEM((SEG * (seg_len + 1), LANES), jnp.float32)],
+        scratch_shapes=[pltpu.VMEM(((SEG + 1) * (seg_len + 1), LANES), jnp.float32)],
         compiler_params=pltpu.CompilerParams(vmem_limit_bytes=VMEM_LIMIT),
         cost_estimate=cost(2 * tok * ch * order, 4 * tok * ch),
         name="end_states",
@@ -107,7 +107,7 @@
             jax.ShapeDtypeStruct((seg * span, ch), jnp.float32),
             jax.ShapeDtypeStruct((order, ch), jnp.float32),
         ],
-        scratch_shapes=[pltpu.VMEM((seg * (span + 1), LANES), jnp.float32)],
+        scratch_shapes=[pltpu.VMEM(((seg + 1) * (span + 1), LANES), jnp.float32)],
         compiler_params=pltpu.CompilerParams(vmem_limit_bytes=VMEM_LIMIT),
         cost_estimate=cost(seg * span * ch, 12 * seg * span * ch),
         name="ahead",
@@ -175,7 +175,7 @@
     seg, _, ch = query.shape
     order = rates.shape[0]
     first = incoming is not None
-    width = 512 if first else 256
+    width = ch if first else 256
     part = pl.BlockSpec((seg, span, width), lambda j: (0, at // span, j))
     cut = lambda rows: pl.BlockSpec((rows, width), lambda j: (0, j))
     operands = [query, *inputs, rates, residues, skip, state]
@@ -198,7 +198,7 @@
         + [
             jax.ShapeDtypeStruct((order * seg, ch), jnp.float32),
         ],
-        scratch_shapes=[pltpu.VMEM((seg * (span + 1), LANES), jnp.float32)] * 2,
+        scratch_shapes=[pltpu.VMEM(((seg + 1) * (span + 1), LANES), jnp.float32)] * 2,
         compiler_params=pltpu.CompilerParams(vmem_limit_bytes=VMEM_LIMIT),
         cost_estimate=cost(4 * rows * ch * order, 8 * rows * ch + 8 * order * seg * ch),
         name="gate_chunk",

time: 93.7 us -> 93.3 us (level)
  no operation moved by 1% of the time
where the time goes in v5:
time: 93.3 us; the launch traced here: 92.9 us
  Pallas kernels  44.5 us (48%)
  starting transfers between devices  31 us (33%)
  waiting for transfers between devices  16.7 us (18%)
    ppermute x9, starting transfers between devices, carried_in(): lax.ppermute(sent, 'seq', shifted(sizes, dim, hop, True))  18.8 us
    pallas_call x4, Pallas kernels, gate_chunk(): pl.pallas_call(functools.partial(gate_kernel, first, count, at, seg_len),...  16.2 us
    ppermute x4, waiting for transfers between devices, share(): came.append(lax.ppermute(shares[-1], 'tp', PARTNER))  13.3 us
    pallas_call x1, Pallas kernels, end_states(): pl.pallas_call(functools.partial(end_kernel, seg_len), grid=(ch // width,...  6.8 us
    pallas_call x1, Pallas kernels, own_shares(): pl.pallas_call(functools.partial(own_kernel, counts), grid_spec=pltpu.Pre...  6.62 us
    ppermute x8, starting transfers between devices, gate(): others.append([lax.ppermute(piece, 'tp', SIBLING) for piece in gated])  5.73 us
    pallas_call x4, Pallas kernels, share_chunk(): pl.pallas_call(functools.partial(share_kernel, count), in_specs=[whole(de...  5.02 us
    pallas_call x2, Pallas kernels, chip_columns(): pl.pallas_call(columns_kernel, grid_spec=pltpu.PrefetchScalarGridSpec(num...  4.35 us
  transfers between devices with their start and end apart: 22, of which 8 were waited for; matrix products, arithmetic and copies ran while one was open for 0% of the time, Pallas kernels for 43%

profile of v5, /device:TPU:1, one launch (start us, length us, event | category | flops | bytes accessed | tf_op | source)
XLA Modules:
  0.0 92.9 jit_solution(12866057526522690219)
XLA Ops:
  0.0 3.2 %collective-permute-start = (bf16[1024,4096]{1,0:T(8,128)(2,1)}, bf16[1024,4096]{1,0:T(8,128)(2,1)}, u32[]{:S(2)}, u32[]{:S(2)}) collective-permute-start(bf16[1024,4096]{1,0:T(8,128)(2,1)} %w_ref.5), channel_id=1, source_target_pairs={{0,1},{1,0},{2,3},{3,2},{4,5},{5,4},{6,7},{7,6},{8,9},{9,8},{10,11... | collective-permute-start | bytes 25165832 | tf_op jit(solution)/shard_map/ppermute | solution.py:404
  3.2 6.8 %end_states.1 = (f32[16,1024]{1,0:T(8,128)S(1)}, f32[128,1024]{1,0:T(8,128)S(1)}, bf16[16,1024]{1,0:T(8,128)(2,1)S(1)}) custom-call(bf16[1024,1024]{1,0:T(8,128)(2,1)} %k_ref.1, bf16[1024,1024]{1,0:T(8,128)(2,1)} %v_ref.1, f32[16,1024]{1,0:T(8,128)} %rest_2_.7), custom_call_target="tpu_custom_call" | custom-call | flops 1 | bytes 1 | tf_op jit(solution)/shard_map/end_states/pallas_call | solution.py:66
  10.0 1.3 %collective-permute-start.1 = (bf16[16,1024]{1,0:T(8,128)(2,1)S(1)}, bf16[16,1024]{1,0:T(8,128)(2,1)S(1)}, u32[]{:S(2)}, u32[]{:S(2)}) collective-permute-start(bf16[16,1024]{1,0:T(8,128)(2,1)S(1)} %get-tuple-element.30.after_ref), channel_id=1, source_target_pairs={{0,4},{4,8},{8,12},{12,0},{16,20},{20,24},{24,28},{28,16},{32,36},... | collective-permute-start | bytes 98312 | tf_op jit(solution)/shard_map/ppermute | solution.py:369
  11.4 5.1 %collective-permute-start.2 = (bf16[16,1024]{1,0:T(8,128)(2,1)S(1)}, bf16[16,1024]{1,0:T(8,128)(2,1)S(1)}, u32[]{:S(2)}, u32[]{:S(2)}) collective-permute-start(bf16[16,1024]{1,0:T(8,128)(2,1)S(1)} %get-tuple-element.30.after_ref), channel_id=1, source_target_pairs={{0,8},{4,12},{8,0},{12,4},{16,24},{20,28},{24,16},{28,20},{32,40},... | collective-permute-start | bytes 98312 | tf_op jit(solution)/shard_map/ppermute | solution.py:369
  16.5 2.4 %collective-permute-start.3 = (bf16[16,1024]{1,0:T(8,128)(2,1)S(1)}, bf16[16,1024]{1,0:T(8,128)(2,1)S(1)}, u32[]{:S(2)}, u32[]{:S(2)}) collective-permute-start(bf16[16,1024]{1,0:T(8,128)(2,1)S(1)} %get-tuple-element.30.after_ref), channel_id=1, source_target_pairs={{0,12},{4,0},{8,4},{12,8},{16,28},{20,16},{24,20},{28,24},{32,44},... | collective-permute-start | bytes 98312 | tf_op jit(solution)/shard_map/ppermute | solution.py:369
  18.9 1.6 %ahead.1 = (bf16[8,32,1024]{2,1,0:T(8,128)(2,1)S(1)}, f32[256,1024]{1,0:T(8,128)S(1)}, f32[16,1024]{1,0:T(8,128)S(1)}) custom-call(bf16[8,128,1024]{2,1,0:T(8,128)(2,1)} %bitcast.53, bf16[8,128,1024]{2,1,0:T(8,128)(2,1)} %bitcast.45, bf16[8,128,1024]{2,1,0:T(8,128)(2,1)} %bitcast.49, bf16[16,1024]{1,0:T(8,128)(2,1)S(1)} %get-tuple-element.30.after_ref), custom_call_target="tpu_custom_call" | custom-call | flops 1 | bytes 1 | tf_op jit(solution)/shard_map/ahead/pallas_call | solution.py:100
  21.3 1.3 %collective-permute-start.4 = (bf16[16,1024]{1,0:T(8,128)(2,1)S(1)}, bf16[16,1024]{1,0:T(8,128)(2,1)S(1)}, u32[]{:S(2)}, u32[]{:S(2)}) collective-permute-start(bf16[16,1024]{1,0:T(8,128)(2,1)S(1)} %get-tuple-element.55), channel_id=1, source_target_pairs={{0,16},{4,20},{8,24},{12,28},{16,32},{20,36},{24,40},{28,44},{32,4... | collective-permute-start | bytes 98312 | tf_op jit(solution)/shard_map/ppermute | solution.py:369
  22.6 2.5 %collective-permute-start.5 = (bf16[16,1024]{1,0:T(8,128)(2,1)S(1)}, bf16[16,1024]{1,0:T(8,128)(2,1)S(1)}, u32[]{:S(2)}, u32[]{:S(2)}) collective-permute-start(bf16[16,1024]{1,0:T(8,128)(2,1)S(1)} %get-tuple-element.55), channel_id=1, source_target_pairs={{0,32},{4,36},{8,40},{12,44},{16,48},{20,52},{24,56},{28,60},{32,0... | collective-permute-start | bytes 98312 | tf_op jit(solution)/shard_map/ppermute | solution.py:369
  26.2 2.6 %chip_columns.2 = (bf16[2048,512]{1,0:T(8,128)(2,1)}, f32[16,1024]{1,0:T(8,128)S(1)}) custom-call(s32[1]{0:T(128)} %bitcast.5.at_ref, bf16[1024,4096]{1,0:T(8,128)(2,1)} %w_ref.5, bf16[1024,4096]{1,0:T(8,128)(2,1)} %collective-permute-done.wo_ref), custom_call_target="tpu_custom_call" | custom-call | flops 1 | bytes 1 | tf_op jit(solution)/shard_map/chip_columns/pallas_call | solution.py:219
  28.9 1.4 %collective-permute-start.7 = (bf16[16,1024]{1,0:T(8,128)(2,1)S(1)}, bf16[16,1024]{1,0:T(8,128)(2,1)S(1)}, u32[]{:S(2)}, u32[]{:S(2)}) collective-permute-start(bf16[16,1024]{1,0:T(8,128)(2,1)S(1)} %fusion.31), channel_id=1, source_target_pairs={{0,64},{4,68},{8,72},{12,76},{16,80},{20,84},{24,88},{28,92},{32,9... | collective-permute-start | bytes 98312 | tf_op jit(solution)/shard_map/ppermute | solution.py:369
  30.3 2.6 %collective-permute-start.8 = (bf16[16,1024]{1,0:T(8,128)(2,1)S(1)}, bf16[16,1024]{1,0:T(8,128)(2,1)S(1)}, u32[]{:S(2)}, u32[]{:S(2)}) collective-permute-start(bf16[16,1024]{1,0:T(8,128)(2,1)S(1)} %fusion.31), channel_id=1, source_target_pairs={{0,128},{4,132},{8,136},{12,140},{16,144},{20,148},{24,152},{28,15... | collective-permute-start | bytes 98312 | tf_op jit(solution)/shard_map/ppermute | solution.py:369
  34.0 1.8 %chip_columns.3 = (bf16[2048,512]{1,0:T(8,128)(2,1)S(1)}, f32[16,1024]{1,0:T(8,128)S(1)}) custom-call(s32[1]{0:T(128)} %bitcast.6.at_ref, bf16[1024,4096]{1,0:T(8,128)(2,1)} %w_ref.5, bf16[1024,4096]{1,0:T(8,128)(2,1)} %collective-permute-done.wo_ref), custom_call_target="tpu_custom_call" | custom-call | flops 1 | bytes 1 | tf_op jit(solution)/shard_map/chip_columns/pallas_call | solution.py:219
  36.0 2.7 %gate_chunk.4 = (bf16[4,32,1024]{2,1,0:T(8,128)(2,1)S(1)}, bf16[4,32,1024]{2,1,0:T(8,128)(2,1)S(1)}, f32[128,1024]{1,0:T(8,128)S(1)}) custom-call(bf16[8,32,1024]{2,1,0:T(8,128)(2,1)S(1)} %get-tuple-element.31.q_ref, f32[256,1024]{1,0:T(8,128)S(1)} %get-tuple-element.32.rest_0_, f32[16,1024]{1,0:T(8,128)S(1)} %copy-done.1, f32[16,1024]{1,0:T(8,128)S(1)} %copy-done.2, ...), custom_call_target="tpu_custom_call" | custom-call | flops 1 | bytes 1 | tf_op jit(solution)/shard_map/gate_chunk/pallas_call | solution.py:191
  38.7 3.3 %collective-permute-start.10 = (bf16[128,1024]{1,0:T(8,128)(2,1)S(1)}, bf16[128,1024]{1,0:T(8,128)(2,1)S(1)}, u32[]{:S(2)}, u32[]{:S(2)}) collective-permute-start(bf16[128,1024]{1,0:T(8,128)(2,1)S(1)} %bitcast.20), channel_id=1, source_target_pairs={{0,1},{1,0},{2,3},{3,2},{4,5},{5,4},{6,7},{7,6},{8,9},{9,8},{10,11... | collective-permute-start | bytes 786440 | tf_op jit(solution)/shard_map/ppermute | solution.py:436
  45.7 4.3 %gate_chunk.5 = (bf16[4,32,1024]{2,1,0:T(8,128)(2,1)S(1)}, bf16[4,32,1024]{2,1,0:T(8,128)(2,1)S(1)}, f32[128,1024]{1,0:T(8,128)S(1)}) custom-call(bf16[8,128,1024]{2,1,0:T(8,128)(2,1)} %bitcast.54, bf16[8,128,1024]{2,1,0:T(8,128)(2,1)} %bitcast.46, bf16[8,128,1024]{2,1,0:T(8,128)(2,1)} %bitcast.50, f32[16,1024]{1,0:T(8,128)S(1)} %copy-done.1, ...), custom_call_target="tpu_custom_call" | custom-call | flops 1 | bytes 1 | tf_op jit(solution)/shard_map/gate_chunk/pallas_call | solution.py:191
  52.3 1.3 %share_chunk.5.rest_6_.rest_4_ = bf16[256,1024]{1,0:T(8,128)(2,1)S(1)} custom-call(bf16[2048,512]{1,0:T(8,128)(2,1)S(1)} %copy-done, bf16[2048,512]{1,0:T(8,128)(2,1)S(1)} %get-tuple-element.42.wx_ref, bf16[128,1024]{1,0:T(8,128)(2,1)S(1)} %bitcast.27, bf16[128,1024]{1,0:T(8,128)(2,1)S(1)} %bitcast.30, ...), custom_call_target="tpu_custom_call" | custom-call | flops 1 | bytes 1 | tf_op jit(solution)/shard_map/share_chunk/pallas_call | solution.py:265
  54.5 4.3 %gate_chunk.6 = (bf16[4,32,1024]{2,1,0:T(8,128)(2,1)S(1)}, bf16[4,32,1024]{2,1,0:T(8,128)(2,1)S(1)}, f32[128,1024]{1,0:T(8,128)S(1)}) custom-call(bf16[8,128,1024]{2,1,0:T(8,128)(2,1)} %bitcast.55, bf16[8,128,1024]{2,1,0:T(8,128)(2,1)} %bitcast.47, bf16[8,128,1024]{2,1,0:T(8,128)(2,1)} %bitcast.51, f32[16,1024]{1,0:T(8,128)S(1)} %copy-done.1, ...), custom_call_target="tpu_custom_call" | custom-call | flops 1 | bytes 1 | tf_op jit(solution)/shard_map/gate_chunk/pallas_call | solution.py:191
  59.6 4.9 %gate_chunk.7 = (bf16[4,32,1024]{2,1,0:T(8,128)(2,1)S(1)}, bf16[4,32,1024]{2,1,0:T(8,128)(2,1)S(1)}, f32[128,1024]{1,0:T(8,128)}) custom-call(bf16[8,128,1024]{2,1,0:T(8,128)(2,1)} %bitcast.56, bf16[8,128,1024]{2,1,0:T(8,128)(2,1)} %bitcast.48, bf16[8,128,1024]{2,1,0:T(8,128)(2,1)} %bitcast.52, f32[16,1024]{1,0:T(8,128)S(1)} %copy-done.1, ...), custom_call_target="tpu_custom_call" | custom-call | flops 1 | bytes 1 | tf_op jit(solution)/shard_map/gate_chunk/pallas_call | solution.py:191
  65.2 1.3 %share_chunk.6.rest_4_ = bf16[256,1024]{1,0:T(8,128)(2,1)S(1)} custom-call(bf16[2048,512]{1,0:T(8,128)(2,1)S(1)} %copy-done, bf16[2048,512]{1,0:T(8,128)(2,1)S(1)} %get-tuple-element.42.wx_ref, bf16[128,1024]{1,0:T(8,128)(2,1)S(1)} %bitcast.33, bf16[128,1024]{1,0:T(8,128)(2,1)S(1)} %bitcast.36, ...), custom_call_target="tpu_custom_call" | custom-call | flops 1 | bytes 1 | tf_op jit(solution)/shard_map/share_chunk/pallas_call | solution.py:265
  67.2 2.3 %collective-permute-done.19.rest_5_.far_ref = bf16[256,1024]{1,0:T(8,128)(2,1)S(1)} collective-permute-done((bf16[256,1024]{1,0:T(8,128)(2,1)S(1)}, bf16[256,1024]{1,0:T(8,128)(2,1)S(1)}, u32[]{:S(2)}, u32[]{:S(2)}) %collective-permute-start.19) | collective-permute-done | bytes 524320 | tf_op jit(solution)/shard_map/ppermute | solution.py:442
  69.5 1.2 %share_chunk.7.rest_16_ = bf16[256,1024]{1,0:T(8,128)(2,1)S(1)} custom-call(bf16[2048,512]{1,0:T(8,128)(2,1)S(1)} %copy-done, bf16[2048,512]{1,0:T(8,128)(2,1)S(1)} %get-tuple-element.42.wx_ref, bf16[128,1024]{1,0:T(8,128)(2,1)S(1)} %bitcast.18, bf16[128,1024]{1,0:T(8,128)(2,1)S(1)} %bitcast.39, ...), custom_call_target="tpu_custom_call" | custom-call | flops 1 | bytes 1 | tf_op jit(solution)/shard_map/share_chunk/pallas_call | solution.py:265
  71.4 9.3 %collective-permute-done.20.rest_17_.far_ref = bf16[256,1024]{1,0:T(8,128)(2,1)S(1)} collective-permute-done((bf16[256,1024]{1,0:T(8,128)(2,1)S(1)}, bf16[256,1024]{1,0:T(8,128)(2,1)S(1)}, u32[]{:S(2)}, u32[]{:S(2)}) %collective-permute-start.20) | collective-permute-done | bytes 524320 | tf_op jit(solution)/shard_map/ppermute | solution.py:442
  80.7 6.6 %own_shares.1 = (f32[256,1024]{1,0:T(8,128)S(1)}, f32[256,1024]{1,0:T(8,128)S(1)}, f32[256,1024]{1,0:T(8,128)S(1)}, f32[256,1024]{1,0:T(8,128)S(1)}) custom-call(s32[1]{0:T(128)} %bitcast.at_ref, bf16[1024,4096]{1,0:T(8,128)(2,1)} %w_ref.5, bf16[1024,4096]{1,0:T(8,128)(2,1)} %collective-permute-done.wo_ref, bf16[128,1024]{1,0:T(8,128)(2,1)S(1)} %bitcast.22, ...), custom_call_target="tpu_custom_call" | custom-call | flops 1 | bytes 1 | tf_op jit(solution)/shard_map/own_shares/pallas_call | solution.py:293
  90.3 1.7 %collective-permute-done.21.far_ref = bf16[256,1024]{1,0:T(8,128)(2,1)S(1)} collective-permute-done((bf16[256,1024]{1,0:T(8,128)(2,1)S(1)}, bf16[256,1024]{1,0:T(8,128)(2,1)S(1)}, u32[]{:S(2)}, u32[]{:S(2)}) %collective-permute-start.21) | collective-permute-done | bytes 524320 | tf_op jit(solution)/shard_map/ppermute | solution.py:442
  (48 shorter events, 16.9 us)
Async XLA Ops:
  0.0 26.2 %collective-permute-start = (bf16[1024,4096]{1,0:T(8,128)(2,1)}, bf16[1024,4096]{1,0:T(8,128)(2,1)}, u32[]{:S(2)}, u32[]{:S(2)}) collective-permute-start(bf16[1024,4096]{1,0:T(8,128)(2,1)} %w_ref.5), channel_id=1, source_target_pairs={{0,1},{1,0},{2,3},{3,2},{4,5},{5,4},{6,7},{7,6},{8,9},{9,8},{10,11... | collective-permute-start | bytes 25165832 | tf_op jit(solution)/shard_map/ppermute | solution.py:404
  10.0 10.6 %collective-permute-start.1 = (bf16[16,1024]{1,0:T(8,128)(2,1)S(1)}, bf16[16,1024]{1,0:T(8,128)(2,1)S(1)}, u32[]{:S(2)}, u32[]{:S(2)}) collective-permute-start(bf16[16,1024]{1,0:T(8,128)(2,1)S(1)} %get-tuple-element.30.after_ref), channel_id=1, source_target_pairs={{0,4},{4,8},{8,12},{12,0},{16,20},{20,24},{24,28},{28,16},{32,36},... | collective-permute-start | bytes 98312 | tf_op jit(solution)/shard_map/ppermute | solution.py:369
  11.4 9.2 %collective-permute-start.2 = (bf16[16,1024]{1,0:T(8,128)(2,1)S(1)}, bf16[16,1024]{1,0:T(8,128)(2,1)S(1)}, u32[]{:S(2)}, u32[]{:S(2)}) collective-permute-start(bf16[16,1024]{1,0:T(8,128)(2,1)S(1)} %get-tuple-element.30.after_ref), channel_id=1, source_target_pairs={{0,8},{4,12},{8,0},{12,4},{16,24},{20,28},{24,16},{28,20},{32,40},... | collective-permute-start | bytes 98312 | tf_op jit(solution)/shard_map/ppermute | solution.py:369
  16.5 4.7 %collective-permute-start.3 = (bf16[16,1024]{1,0:T(8,128)(2,1)S(1)}, bf16[16,1024]{1,0:T(8,128)(2,1)S(1)}, u32[]{:S(2)}, u32[]{:S(2)}) collective-permute-start(bf16[16,1024]{1,0:T(8,128)(2,1)S(1)} %get-tuple-element.30.after_ref), channel_id=1, source_target_pairs={{0,12},{4,0},{8,4},{12,8},{16,28},{20,16},{24,20},{28,24},{32,44},... | collective-permute-start | bytes 98312 | tf_op jit(solution)/shard_map/ppermute | solution.py:369
  18.9 2.3 %copy-start.1 = (f32[16,1024]{1,0:T(8,128)S(1)}, f32[16,1024]{1,0:T(8,128)}, u32[]{:S(2)}) copy-start(f32[16,1024]{1,0:T(8,128)} %rest_2_.7) | copy-start | bytes 196612
  21.3 7.5 %collective-permute-start.4 = (bf16[16,1024]{1,0:T(8,128)(2,1)S(1)}, bf16[16,1024]{1,0:T(8,128)(2,1)S(1)}, u32[]{:S(2)}, u32[]{:S(2)}) collective-permute-start(bf16[16,1024]{1,0:T(8,128)(2,1)S(1)} %get-tuple-element.55), channel_id=1, source_target_pairs={{0,16},{4,20},{8,24},{12,28},{16,32},{20,36},{24,40},{28,44},{32,4... | collective-permute-start | bytes 98312 | tf_op jit(solution)/shard_map/ppermute | solution.py:369
  22.6 6.2 %collective-permute-start.5 = (bf16[16,1024]{1,0:T(8,128)(2,1)S(1)}, bf16[16,1024]{1,0:T(8,128)(2,1)S(1)}, u32[]{:S(2)}, u32[]{:S(2)}) collective-permute-start(bf16[16,1024]{1,0:T(8,128)(2,1)S(1)} %get-tuple-element.55), channel_id=1, source_target_pairs={{0,32},{4,36},{8,40},{12,44},{16,48},{20,52},{24,56},{28,60},{32,0... | collective-permute-start | bytes 98312 | tf_op jit(solution)/shard_map/ppermute | solution.py:369
  25.0 3.8 %collective-permute-start.6 = (bf16[16,1024]{1,0:T(8,128)(2,1)S(1)}, bf16[16,1024]{1,0:T(8,128)(2,1)S(1)}, u32[]{:S(2)}, u32[]{:S(2)}) collective-permute-start(bf16[16,1024]{1,0:T(8,128)(2,1)S(1)} %get-tuple-element.55), channel_id=1, source_target_pairs={{0,48},{4,52},{8,56},{12,60},{16,0},{20,4},{24,8},{28,12},{32,16},... | collective-permute-start | bytes 98312 | tf_op jit(solution)/shard_map/ppermute | solution.py:369
  28.9 6.8 %collective-permute-start.7 = (bf16[16,1024]{1,0:T(8,128)(2,1)S(1)}, bf16[16,1024]{1,0:T(8,128)(2,1)S(1)}, u32[]{:S(2)}, u32[]{:S(2)}) collective-permute-start(bf16[16,1024]{1,0:T(8,128)(2,1)S(1)} %fusion.31), channel_id=1, source_target_pairs={{0,64},{4,68},{8,72},{12,76},{16,80},{20,84},{24,88},{28,92},{32,9... | collective-permute-start | bytes 98312 | tf_op jit(solution)/shard_map/ppermute | solution.py:369
  30.3 5.5 %collective-permute-start.8 = (bf16[16,1024]{1,0:T(8,128)(2,1)S(1)}, bf16[16,1024]{1,0:T(8,128)(2,1)S(1)}, u32[]{:S(2)}, u32[]{:S(2)}) collective-permute-start(bf16[16,1024]{1,0:T(8,128)(2,1)S(1)} %fusion.31), channel_id=1, source_target_pairs={{0,128},{4,132},{8,136},{12,140},{16,144},{20,148},{24,152},{28,15... | collective-permute-start | bytes 98312 | tf_op jit(solution)/shard_map/ppermute | solution.py:369
  32.9 2.9 %collective-permute-start.9 = (bf16[16,1024]{1,0:T(8,128)(2,1)S(1)}, bf16[16,1024]{1,0:T(8,128)(2,1)S(1)}, u32[]{:S(2)}, u32[]{:S(2)}) collective-permute-start(bf16[16,1024]{1,0:T(8,128)(2,1)S(1)} %fusion.31), channel_id=1, source_target_pairs={{0,192},{4,196},{8,200},{12,204},{16,208},{20,212},{24,216},{28,22... | collective-permute-start | bytes 98312 | tf_op jit(solution)/shard_map/ppermute | solution.py:369
  35.8 7.8 %copy-start = (bf16[2048,512]{1,0:T(8,128)(2,1)S(1)}, bf16[2048,512]{1,0:T(8,128)(2,1)}, u32[]{:S(2)}) copy-start(bf16[2048,512]{1,0:T(8,128)(2,1)} %get-tuple-element.41.w_ref) | copy-start | bytes 6291460
  38.7 4.5 %collective-permute-start.10 = (bf16[128,1024]{1,0:T(8,128)(2,1)S(1)}, bf16[128,1024]{1,0:T(8,128)(2,1)S(1)}, u32[]{:S(2)}, u32[]{:S(2)}) collective-permute-start(bf16[128,1024]{1,0:T(8,128)(2,1)S(1)} %bitcast.20), channel_id=1, source_target_pairs={{0,1},{1,0},{2,3},{3,2},{4,5},{5,4},{6,7},{7,6},{8,9},{9,8},{10,11... | collective-permute-start | bytes 786440 | tf_op jit(solution)/shard_map/ppermute | solution.py:436
  42.1 1.5 %collective-permute-start.11 = (bf16[128,1024]{1,0:T(8,128)(2,1)S(1)}, bf16[128,1024]{1,0:T(8,128)(2,1)S(1)}, u32[]{:S(2)}, u32[]{:S(2)}) collective-permute-start(bf16[128,1024]{1,0:T(8,128)(2,1)S(1)} %bitcast.23), channel_id=1, source_target_pairs={{0,1},{1,0},{2,3},{3,2},{4,5},{5,4},{6,7},{7,6},{8,9},{9,8},{10,11... | collective-permute-start | bytes 786440 | tf_op jit(solution)/shard_map/ppermute | solution.py:436
  44.8 14.8 %collective-permute-start.16 = (bf16[256,1024]{1,0:T(8,128)(2,1)S(1)}, bf16[256,1024]{1,0:T(8,128)(2,1)S(1)}, u32[]{:S(2)}, u32[]{:S(2)}) collective-permute-start(bf16[256,1024]{1,0:T(8,128)(2,1)S(1)} %share_chunk.4.rest_6_.rest_4_), channel_id=1, source_target_pairs={{0,2},{2,0},{1,3},{3,1},{4,6},{6,4},{5,7},{7,5},{8,10},{10,8},{9,1... | collective-permute-start | bytes 1572872 | tf_op jit(solution)/shard_map/ppermute | solution.py:442
  50.0 1.9 %collective-permute-start.12 = (bf16[128,1024]{1,0:T(8,128)(2,1)S(1)}, bf16[128,1024]{1,0:T(8,128)(2,1)S(1)}, u32[]{:S(2)}, u32[]{:S(2)}) collective-permute-start(bf16[128,1024]{1,0:T(8,128)(2,1)S(1)} %bitcast.26), channel_id=1, source_target_pairs={{0,1},{1,0},{2,3},{3,2},{4,5},{5,4},{6,7},{7,6},{8,9},{9,8},{10,11... | collective-permute-start | bytes 786440 | tf_op jit(solution)/shard_map/ppermute | solution.py:436
  50.8 1.5 %collective-permute-start.13 = (bf16[128,1024]{1,0:T(8,128)(2,1)S(1)}, bf16[128,1024]{1,0:T(8,128)(2,1)S(1)}, u32[]{:S(2)}, u32[]{:S(2)}) collective-permute-start(bf16[128,1024]{1,0:T(8,128)(2,1)S(1)} %bitcast.29), channel_id=1, source_target_pairs={{0,1},{1,0},{2,3},{3,2},{4,5},{5,4},{6,7},{7,6},{8,9},{9,8},{10,11... | collective-permute-start | bytes 786440 | tf_op jit(solution)/shard_map/ppermute | solution.py:436
  53.6 15.9 %collective-permute-start.19 = (bf16[256,1024]{1,0:T(8,128)(2,1)S(1)}, bf16[256,1024]{1,0:T(8,128)(2,1)S(1)}, u32[]{:S(2)}, u32[]{:S(2)}) collective-permute-start(bf16[256,1024]{1,0:T(8,128)(2,1)S(1)} %share_chunk.5.rest_6_.rest_4_), channel_id=1, source_target_pairs={{0,2},{2,0},{1,3},{3,1},{4,6},{6,4},{5,7},{7,5},{8,10},{10,8},{9,1... | collective-permute-start | bytes 1572872 | tf_op jit(solution)/shard_map/ppermute | solution.py:442
  58.8 6.4 %collective-permute-start.14 = (bf16[128,1024]{1,0:T(8,128)(2,1)S(1)}, bf16[128,1024]{1,0:T(8,128)(2,1)S(1)}, u32[]{:S(2)}, u32[]{:S(2)}) collective-permute-start(bf16[128,1024]{1,0:T(8,128)(2,1)S(1)} %bitcast.32), channel_id=1, source_target_pairs={{0,1},{1,0},{2,3},{3,2},{4,5},{5,4},{6,7},{7,6},{8,9},{9,8},{10,11... | collective-permute-start | bytes 786440 | tf_op jit(solution)/shard_map/ppermute | solution.py:436
  59.5 5.7 %collective-permute-start.15 = (bf16[128,1024]{1,0:T(8,128)(2,1)S(1)}, bf16[128,1024]{1,0:T(8,128)(2,1)S(1)}, u32[]{:S(2)}, u32[]{:S(2)}) collective-permute-start(bf16[128,1024]{1,0:T(8,128)(2,1)S(1)} %bitcast.35), channel_id=1, source_target_pairs={{0,1},{1,0},{2,3},{3,2},{4,5},{5,4},{6,7},{7,6},{8,9},{9,8},{10,11... | collective-permute-start | bytes 786440 | tf_op jit(solution)/shard_map/ppermute | solution.py:436
  64.6 2.6 %collective-permute-start.17 = (bf16[128,1024]{1,0:T(8,128)(2,1)S(1)}, bf16[128,1024]{1,0:T(8,128)(2,1)S(1)}, u32[]{:S(2)}, u32[]{:S(2)}) collective-permute-start(bf16[128,1024]{1,0:T(8,128)(2,1)S(1)} %bitcast.16), channel_id=1, source_target_pairs={{0,1},{1,0},{2,3},{3,2},{4,5},{5,4},{6,7},{7,6},{8,9},{9,8},{10,11... | collective-permute-start | bytes 786440 | tf_op jit(solution)/shard_map/ppermute | solution.py:436
  65.2 2.0 %collective-permute-start.18 = (bf16[128,1024]{1,0:T(8,128)(2,1)S(1)}, bf16[128,1024]{1,0:T(8,128)(2,1)S(1)}, u32[]{:S(2)}, u32[]{:S(2)}) collective-permute-start(bf16[128,1024]{1,0:T(8,128)(2,1)S(1)} %bitcast.38), channel_id=1, source_target_pairs={{0,1},{1,0},{2,3},{3,2},{4,5},{5,4},{6,7},{7,6},{8,9},{9,8},{10,11... | collective-permute-start | bytes 786440 | tf_op jit(solution)/shard_map/ppermute | solution.py:436
  66.5 14.2 %collective-permute-start.20 = (bf16[256,1024]{1,0:T(8,128)(2,1)S(1)}, bf16[256,1024]{1,0:T(8,128)(2,1)S(1)}, u32[]{:S(2)}, u32[]{:S(2)}) collective-permute-start(bf16[256,1024]{1,0:T(8,128)(2,1)S(1)} %share_chunk.6.rest_4_), channel_id=1, source_target_pairs={{0,2},{2,0},{1,3},{3,1},{4,6},{6,4},{5,7},{7,5},{8,10},{10,8},{9,1... | collective-permute-start | bytes 1572872 | tf_op jit(solution)/shard_map/ppermute | solution.py:442
  70.7 21.2 %collective-permute-start.21 = (bf16[256,1024]{1,0:T(8,128)(2,1)S(1)}, bf16[256,1024]{1,0:T(8,128)(2,1)S(1)}, u32[]{:S(2)}, u32[]{:S(2)}) collective-permute-start(bf16[256,1024]{1,0:T(8,128)(2,1)S(1)} %share_chunk.7.rest_16_), channel_id=1, source_target_pairs={{0,2},{2,0},{1,3},{3,1},{4,6},{6,4},{5,7},{7,5},{8,10},{10,8},{9,1... | collective-permute-start | bytes 1572872 | tf_op jit(solution)/shard_map/ppermute | solution.py:442
  (2 other events, 4.0 us)

commit v6 on v5

--- a/solution.py
+++ b/solution.py
@@ -313,7 +313,7 @@
     out_ref[...] = total.astype(out_ref.dtype).reshape(out_ref.shape)
 
 
-def finish_chunk(mine, far, out, at, span, seg_len, width=512):
+def finish_chunk(mine, far, out, at, span, seg_len, width=1024):
     rows, ch = mine.shape
     seg = rows // span
     cut = pl.BlockSpec((rows, width), lambda j: (0, j))
@@ -401,9 +401,10 @@
     seg_len = tok // SEG
     here = lax.axis_index("tp")
     chip, core = here // 2, here % 2
-    weight_other = in_hbm(lax.ppermute(weight, "tp", SIBLING))
+    last, before, sent = end_states(in_hbm(key), in_hbm(value), in_hbm(rates))
+    late_weight, sent = lax.optimization_barrier((weight, sent))
+    weight_other = in_hbm(lax.ppermute(late_weight, "tp", SIBLING))
     weight = in_hbm(weight)
-    last, before, sent = end_states(in_hbm(key), in_hbm(value), in_hbm(rates))
     half = ch // 2
     begin = (2 * (1 - chip) + core) * ch
     weight_far, marks = zip(

time: 93.3 us -> 93.3 us (level)
  transfers between devices with their start and end apart: 22 -> 22, of which waited for: 8 -> 8; matrix products, arithmetic and copies ran while one was open for 0% -> 0% of each run, Pallas kernels for 43% -> 35%
where the time goes in v6:
time: 93.3 us; the launch traced here: 92.9 us
  Pallas kernels  44.2 us (47%)
  starting transfers between devices  31.4 us (34%)
  waiting for transfers between devices  16.6 us (18%)
    ppermute x9, starting transfers between devices, carried_in(): lax.ppermute(sent, 'seq', shifted(sizes, dim, hop, True))  18.7 us
    pallas_call x4, Pallas kernels, gate_chunk(): pl.pallas_call(functools.partial(gate_kernel, first, count, at, seg_len),...  16.2 us
    ppermute x4, waiting for transfers between devices, share(): came.append(lax.ppermute(shares[-1], 'tp', PARTNER))  13.3 us
    pallas_call x1, Pallas kernels, end_states(): pl.pallas_call(functools.partial(end_kernel, seg_len), grid=(ch // width,...  6.8 us
    pallas_call x1, Pallas kernels, own_shares(): pl.pallas_call(functools.partial(own_kernel, counts), grid_spec=pltpu.Pre...  6.62 us
    ppermute x8, starting transfers between devices, gate(): others.append([lax.ppermute(piece, 'tp', SIBLING) for piece in gated])  5.94 us
    pallas_call x4, Pallas kernels, share_chunk(): pl.pallas_call(functools.partial(share_kernel, count), in_specs=[whole(de...  5.02 us
    pallas_call x2, Pallas kernels, chip_columns(): pl.pallas_call(columns_kernel, grid_spec=pltpu.PrefetchScalarGridSpec(num...  4.35 us
  transfers between devices with their start and end apart: 22, of which 8 were waited for; matrix products, arithmetic and copies ran while one was open for 0% of the time, Pallas kernels for 35%

profile of v6, /device:TPU:1, one launch (start us, length us, event | category | flops | bytes accessed | tf_op | source)
XLA Modules:
  0.0 92.9 jit_solution(6971015308570420910)
XLA Ops:
  0.0 6.8 %end_states.1 = (f32[16,1024]{1,0:T(8,128)S(1)}, f32[128,1024]{1,0:T(8,128)S(1)}, bf16[16,1024]{1,0:T(8,128)(2,1)S(1)}) custom-call(bf16[1024,1024]{1,0:T(8,128)(2,1)} %k_ref.1, bf16[1024,1024]{1,0:T(8,128)(2,1)} %v_ref.1, f32[16,1024]{1,0:T(8,128)} %rest_2_.7), custom_call_target="tpu_custom_call" | custom-call | flops 1 | bytes 1 | tf_op jit(solution)/shard_map/end_states/pallas_call | solution.py:66
  6.8 3.3 %collective-permute-start = (bf16[1024,4096]{1,0:T(8,128)(2,1)}, bf16[1024,4096]{1,0:T(8,128)(2,1)}, u32[]{:S(2)}, u32[]{:S(2)}) collective-permute-start(bf16[1024,4096]{1,0:T(8,128)(2,1)} %w_ref.5), channel_id=1, source_target_pairs={{0,1},{1,0},{2,3},{3,2},{4,5},{5,4},{6,7},{7,6},{8,9},{9,8},{10,11... | collective-permute-start | bytes 25165832 | tf_op jit(solution)/shard_map/ppermute | solution.py:406
  10.1 1.3 %collective-permute-start.1 = (bf16[16,1024]{1,0:T(8,128)(2,1)S(1)}, bf16[16,1024]{1,0:T(8,128)(2,1)S(1)}, u32[]{:S(2)}, u32[]{:S(2)}) collective-permute-start(bf16[16,1024]{1,0:T(8,128)(2,1)S(1)} %get-tuple-element.34.after_ref), channel_id=1, source_target_pairs={{0,4},{4,8},{8,12},{12,0},{16,20},{20,24},{24,28},{28,16},{32,36},... | collective-permute-start | bytes 98312 | tf_op jit(solution)/shard_map/ppermute | solution.py:369
  11.4 5.1 %collective-permute-start.2 = (bf16[16,1024]{1,0:T(8,128)(2,1)S(1)}, bf16[16,1024]{1,0:T(8,128)(2,1)S(1)}, u32[]{:S(2)}, u32[]{:S(2)}) collective-permute-start(bf16[16,1024]{1,0:T(8,128)(2,1)S(1)} %get-tuple-element.34.after_ref), channel_id=1, source_target_pairs={{0,8},{4,12},{8,0},{12,4},{16,24},{20,28},{24,16},{28,20},{32,40},... | collective-permute-start | bytes 98312 | tf_op jit(solution)/shard_map/ppermute | solution.py:369
  16.5 2.4 %collective-permute-start.3 = (bf16[16,1024]{1,0:T(8,128)(2,1)S(1)}, bf16[16,1024]{1,0:T(8,128)(2,1)S(1)}, u32[]{:S(2)}, u32[]{:S(2)}) collective-permute-start(bf16[16,1024]{1,0:T(8,128)(2,1)S(1)} %get-tuple-element.34.after_ref), channel_id=1, source_target_pairs={{0,12},{4,0},{8,4},{12,8},{16,28},{20,16},{24,20},{28,24},{32,44},... | collective-permute-start | bytes 98312 | tf_op jit(solution)/shard_map/ppermute | solution.py:369
  18.9 1.6 %ahead.1 = (bf16[8,32,1024]{2,1,0:T(8,128)(2,1)S(1)}, f32[256,1024]{1,0:T(8,128)S(1)}, f32[16,1024]{1,0:T(8,128)S(1)}) custom-call(bf16[8,128,1024]{2,1,0:T(8,128)(2,1)} %bitcast.53, bf16[8,128,1024]{2,1,0:T(8,128)(2,1)} %bitcast.45, bf16[8,128,1024]{2,1,0:T(8,128)(2,1)} %bitcast.49, bf16[16,1024]{1,0:T(8,128)(2,1)S(1)} %get-tuple-element.34.after_ref), custom_call_target="tpu_custom_call" | custom-call | flops 1 | bytes 1 | tf_op jit(solution)/shard_map/ahead/pallas_call | solution.py:100
  21.1 1.3 %collective-permute-start.4 = (bf16[16,1024]{1,0:T(8,128)(2,1)S(1)}, bf16[16,1024]{1,0:T(8,128)(2,1)S(1)}, u32[]{:S(2)}, u32[]{:S(2)}) collective-permute-start(bf16[16,1024]{1,0:T(8,128)(2,1)S(1)} %get-tuple-element.59), channel_id=1, source_target_pairs={{0,16},{4,20},{8,24},{12,28},{16,32},{20,36},{24,40},{28,44},{32,4... | collective-permute-start | bytes 98312 | tf_op jit(solution)/shard_map/ppermute | solution.py:369
  22.4 2.5 %collective-permute-start.5 = (bf16[16,1024]{1,0:T(8,128)(2,1)S(1)}, bf16[16,1024]{1,0:T(8,128)(2,1)S(1)}, u32[]{:S(2)}, u32[]{:S(2)}) collective-permute-start(bf16[16,1024]{1,0:T(8,128)(2,1)S(1)} %get-tuple-element.59), channel_id=1, source_target_pairs={{0,32},{4,36},{8,40},{12,44},{16,48},{20,52},{24,56},{28,60},{32,0... | collective-permute-start | bytes 98312 | tf_op jit(solution)/shard_map/ppermute | solution.py:369
  26.0 2.6 %chip_columns.2 = (bf16[2048,512]{1,0:T(8,128)(2,1)}, f32[16,1024]{1,0:T(8,128)S(1)}) custom-call(s32[1]{0:T(128)} %bitcast.5.at_ref, bf16[1024,4096]{1,0:T(8,128)(2,1)} %w_ref.5, bf16[1024,4096]{1,0:T(8,128)(2,1)} %collective-permute-done.wo_ref), custom_call_target="tpu_custom_call" | custom-call | flops 1 | bytes 1 | tf_op jit(solution)/shard_map/chip_columns/pallas_call | solution.py:219
  28.7 1.4 %collective-permute-start.7 = (bf16[16,1024]{1,0:T(8,128)(2,1)S(1)}, bf16[16,1024]{1,0:T(8,128)(2,1)S(1)}, u32[]{:S(2)}, u32[]{:S(2)}) collective-permute-start(bf16[16,1024]{1,0:T(8,128)(2,1)S(1)} %fusion.31), channel_id=1, source_target_pairs={{0,64},{4,68},{8,72},{12,76},{16,80},{20,84},{24,88},{28,92},{32,9... | collective-permute-start | bytes 98312 | tf_op jit(solution)/shard_map/ppermute | solution.py:369
  30.1 2.6 %collective-permute-start.8 = (bf16[16,1024]{1,0:T(8,128)(2,1)S(1)}, bf16[16,1024]{1,0:T(8,128)(2,1)S(1)}, u32[]{:S(2)}, u32[]{:S(2)}) collective-permute-start(bf16[16,1024]{1,0:T(8,128)(2,1)S(1)} %fusion.31), channel_id=1, source_target_pairs={{0,128},{4,132},{8,136},{12,140},{16,144},{20,148},{24,152},{28,15... | collective-permute-start | bytes 98312 | tf_op jit(solution)/shard_map/ppermute | solution.py:369
  33.8 1.8 %chip_columns.3 = (bf16[2048,512]{1,0:T(8,128)(2,1)S(1)}, f32[16,1024]{1,0:T(8,128)S(1)}) custom-call(s32[1]{0:T(128)} %bitcast.6.at_ref, bf16[1024,4096]{1,0:T(8,128)(2,1)} %w_ref.5, bf16[1024,4096]{1,0:T(8,128)(2,1)} %collective-permute-done.wo_ref), custom_call_target="tpu_custom_call" | custom-call | flops 1 | bytes 1 | tf_op jit(solution)/shard_map/chip_columns/pallas_call | solution.py:219
  35.8 2.7 %gate_chunk.4 = (bf16[4,32,1024]{2,1,0:T(8,128)(2,1)S(1)}, bf16[4,32,1024]{2,1,0:T(8,128)(2,1)S(1)}, f32[128,1024]{1,0:T(8,128)S(1)}) custom-call(bf16[8,32,1024]{2,1,0:T(8,128)(2,1)S(1)} %get-tuple-element.35.q_ref, f32[256,1024]{1,0:T(8,128)S(1)} %get-tuple-element.36.rest_0_, f32[16,1024]{1,0:T(8,128)S(1)} %copy-done.1, f32[16,1024]{1,0:T(8,128)S(1)} %copy-done.2, ...), custom_call_target="tpu_custom_call" | custom-call | flops 1 | bytes 1 | tf_op jit(solution)/shard_map/gate_chunk/pallas_call | solution.py:191
  38.5 3.5 %collective-permute-start.10 = (bf16[128,1024]{1,0:T(8,128)(2,1)S(1)}, bf16[128,1024]{1,0:T(8,128)(2,1)S(1)}, u32[]{:S(2)}, u32[]{:S(2)}) collective-permute-start(bf16[128,1024]{1,0:T(8,128)(2,1)S(1)} %bitcast.20), channel_id=1, source_target_pairs={{0,1},{1,0},{2,3},{3,2},{4,5},{5,4},{6,7},{7,6},{8,9},{9,8},{10,11... | collective-permute-start | bytes 786440 | tf_op jit(solution)/shard_map/ppermute | solution.py:437
  45.8 4.3 %gate_chunk.5 = (bf16[4,32,1024]{2,1,0:T(8,128)(2,1)S(1)}, bf16[4,32,1024]{2,1,0:T(8,128)(2,1)S(1)}, f32[128,1024]{1,0:T(8,128)S(1)}) custom-call(bf16[8,128,1024]{2,1,0:T(8,128)(2,1)} %bitcast.54, bf16[8,128,1024]{2,1,0:T(8,128)(2,1)} %bitcast.46, bf16[8,128,1024]{2,1,0:T(8,128)(2,1)} %bitcast.50, f32[16,1024]{1,0:T(8,128)S(1)} %copy-done.1, ...), custom_call_target="tpu_custom_call" | custom-call | flops 1 | bytes 1 | tf_op jit(solution)/shard_map/gate_chunk/pallas_call | solution.py:191
  52.4 1.3 %share_chunk.5.rest_6_.rest_4_ = bf16[256,1024]{1,0:T(8,128)(2,1)S(1)} custom-call(bf16[2048,512]{1,0:T(8,128)(2,1)S(1)} %copy-done, bf16[2048,512]{1,0:T(8,128)(2,1)S(1)} %get-tuple-element.46.wx_ref, bf16[128,1024]{1,0:T(8,128)(2,1)S(1)} %bitcast.27, bf16[128,1024]{1,0:T(8,128)(2,1)S(1)} %bitcast.30, ...), custom_call_target="tpu_custom_call" | custom-call | flops 1 | bytes 1 | tf_op jit(solution)/shard_map/share_chunk/pallas_call | solution.py:265
  54.5 4.3 %gate_chunk.6 = (bf16[4,32,1024]{2,1,0:T(8,128)(2,1)S(1)}, bf16[4,32,1024]{2,1,0:T(8,128)(2,1)S(1)}, f32[128,1024]{1,0:T(8,128)S(1)}) custom-call(bf16[8,128,1024]{2,1,0:T(8,128)(2,1)} %bitcast.55, bf16[8,128,1024]{2,1,0:T(8,128)(2,1)} %bitcast.47, bf16[8,128,1024]{2,1,0:T(8,128)(2,1)} %bitcast.51, f32[16,1024]{1,0:T(8,128)S(1)} %copy-done.1, ...), custom_call_target="tpu_custom_call" | custom-call | flops 1 | bytes 1 | tf_op jit(solution)/shard_map/gate_chunk/pallas_call | solution.py:191
  59.6 4.9 %gate_chunk.7 = (bf16[4,32,1024]{2,1,0:T(8,128)(2,1)S(1)}, bf16[4,32,1024]{2,1,0:T(8,128)(2,1)S(1)}, f32[128,1024]{1,0:T(8,128)}) custom-call(bf16[8,128,1024]{2,1,0:T(8,128)(2,1)} %bitcast.56, bf16[8,128,1024]{2,1,0:T(8,128)(2,1)} %bitcast.48, bf16[8,128,1024]{2,1,0:T(8,128)(2,1)} %bitcast.52, f32[16,1024]{1,0:T(8,128)S(1)} %copy-done.1, ...), custom_call_target="tpu_custom_call" | custom-call | flops 1 | bytes 1 | tf_op jit(solution)/shard_map/gate_chunk/pallas_call | solution.py:191
  65.2 1.3 %share_chunk.6.rest_4_ = bf16[256,1024]{1,0:T(8,128)(2,1)S(1)} custom-call(bf16[2048,512]{1,0:T(8,128)(2,1)S(1)} %copy-done, bf16[2048,512]{1,0:T(8,128)(2,1)S(1)} %get-tuple-element.46.wx_ref, bf16[128,1024]{1,0:T(8,128)(2,1)S(1)} %bitcast.33, bf16[128,1024]{1,0:T(8,128)(2,1)S(1)} %bitcast.36, ...), custom_call_target="tpu_custom_call" | custom-call | flops 1 | bytes 1 | tf_op jit(solution)/shard_map/share_chunk/pallas_call | solution.py:265
  67.3 2.2 %collective-permute-done.19.rest_5_.far_ref = bf16[256,1024]{1,0:T(8,128)(2,1)S(1)} collective-permute-done((bf16[256,1024]{1,0:T(8,128)(2,1)S(1)}, bf16[256,1024]{1,0:T(8,128)(2,1)S(1)}, u32[]{:S(2)}, u32[]{:S(2)}) %collective-permute-start.19) | collective-permute-done | bytes 524320 | tf_op jit(solution)/shard_map/ppermute | solution.py:443
  69.5 1.2 %share_chunk.7.rest_16_ = bf16[256,1024]{1,0:T(8,128)(2,1)S(1)} custom-call(bf16[2048,512]{1,0:T(8,128)(2,1)S(1)} %copy-done, bf16[2048,512]{1,0:T(8,128)(2,1)S(1)} %get-tuple-element.46.wx_ref, bf16[128,1024]{1,0:T(8,128)(2,1)S(1)} %bitcast.18, bf16[128,1024]{1,0:T(8,128)(2,1)S(1)} %bitcast.39, ...), custom_call_target="tpu_custom_call" | custom-call | flops 1 | bytes 1 | tf_op jit(solution)/shard_map/share_chunk/pallas_call | solution.py:265
  71.5 9.2 %collective-permute-done.20.rest_17_.far_ref = bf16[256,1024]{1,0:T(8,128)(2,1)S(1)} collective-permute-done((bf16[256,1024]{1,0:T(8,128)(2,1)S(1)}, bf16[256,1024]{1,0:T(8,128)(2,1)S(1)}, u32[]{:S(2)}, u32[]{:S(2)}) %collective-permute-start.20) | collective-permute-done | bytes 524320 | tf_op jit(solution)/shard_map/ppermute | solution.py:443
  80.7 6.6 %own_shares.1 = (f32[256,1024]{1,0:T(8,128)S(1)}, f32[256,1024]{1,0:T(8,128)S(1)}, f32[256,1024]{1,0:T(8,128)S(1)}, f32[256,1024]{1,0:T(8,128)S(1)}) custom-call(s32[1]{0:T(128)} %bitcast.at_ref, bf16[1024,4096]{1,0:T(8,128)(2,1)} %w_ref.5, bf16[1024,4096]{1,0:T(8,128)(2,1)} %collective-permute-done.wo_ref, bf16[128,1024]{1,0:T(8,128)(2,1)S(1)} %bitcast.22, ...), custom_call_target="tpu_custom_call" | custom-call | flops 1 | bytes 1 | tf_op jit(solution)/shard_map/own_shares/pallas_call | solution.py:293
  90.1 1.9 %collective-permute-done.21.far_ref = bf16[256,1024]{1,0:T(8,128)(2,1)S(1)} collective-permute-done((bf16[256,1024]{1,0:T(8,128)(2,1)S(1)}, bf16[256,1024]{1,0:T(8,128)(2,1)S(1)}, u32[]{:S(2)}, u32[]{:S(2)}) %collective-permute-start.21) | collective-permute-done | bytes 524320 | tf_op jit(solution)/shard_map/ppermute | solution.py:443
  (48 shorter events, 16.5 us)
Async XLA Ops:
  6.8 19.2 %collective-permute-start = (bf16[1024,4096]{1,0:T(8,128)(2,1)}, bf16[1024,4096]{1,0:T(8,128)(2,1)}, u32[]{:S(2)}, u32[]{:S(2)}) collective-permute-start(bf16[1024,4096]{1,0:T(8,128)(2,1)} %w_ref.5), channel_id=1, source_target_pairs={{0,1},{1,0},{2,3},{3,2},{4,5},{5,4},{6,7},{7,6},{8,9},{9,8},{10,11... | collective-permute-start | bytes 25165832 | tf_op jit(solution)/shard_map/ppermute | solution.py:406
  10.1 10.5 %collective-permute-start.1 = (bf16[16,1024]{1,0:T(8,128)(2,1)S(1)}, bf16[16,1024]{1,0:T(8,128)(2,1)S(1)}, u32[]{:S(2)}, u32[]{:S(2)}) collective-permute-start(bf16[16,1024]{1,0:T(8,128)(2,1)S(1)} %get-tuple-element.34.after_ref), channel_id=1, source_target_pairs={{0,4},{4,8},{8,12},{12,0},{16,20},{20,24},{24,28},{28,16},{32,36},... | collective-permute-start | bytes 98312 | tf_op jit(solution)/shard_map/ppermute | solution.py:369
  11.4 9.2 %collective-permute-start.2 = (bf16[16,1024]{1,0:T(8,128)(2,1)S(1)}, bf16[16,1024]{1,0:T(8,128)(2,1)S(1)}, u32[]{:S(2)}, u32[]{:S(2)}) collective-permute-start(bf16[16,1024]{1,0:T(8,128)(2,1)S(1)} %get-tuple-element.34.after_ref), channel_id=1, source_target_pairs={{0,8},{4,12},{8,0},{12,4},{16,24},{20,28},{24,16},{28,20},{32,40},... | collective-permute-start | bytes 98312 | tf_op jit(solution)/shard_map/ppermute | solution.py:369
  16.5 4.5 %collective-permute-start.3 = (bf16[16,1024]{1,0:T(8,128)(2,1)S(1)}, bf16[16,1024]{1,0:T(8,128)(2,1)S(1)}, u32[]{:S(2)}, u32[]{:S(2)}) collective-permute-start(bf16[16,1024]{1,0:T(8,128)(2,1)S(1)} %get-tuple-element.34.after_ref), channel_id=1, source_target_pairs={{0,12},{4,0},{8,4},{12,8},{16,28},{20,16},{24,20},{28,24},{32,44},... | collective-permute-start | bytes 98312 | tf_op jit(solution)/shard_map/ppermute | solution.py:369
  18.9 2.1 %copy-start.1 = (f32[16,1024]{1,0:T(8,128)S(1)}, f32[16,1024]{1,0:T(8,128)}, u32[]{:S(2)}) copy-start(f32[16,1024]{1,0:T(8,128)} %rest_2_.7) | copy-start | bytes 196612
  21.1 7.5 %collective-permute-start.4 = (bf16[16,1024]{1,0:T(8,128)(2,1)S(1)}, bf16[16,1024]{1,0:T(8,128)(2,1)S(1)}, u32[]{:S(2)}, u32[]{:S(2)}) collective-permute-start(bf16[16,1024]{1,0:T(8,128)(2,1)S(1)} %get-tuple-element.59), channel_id=1, source_target_pairs={{0,16},{4,20},{8,24},{12,28},{16,32},{20,36},{24,40},{28,44},{32,4... | collective-permute-start | bytes 98312 | tf_op jit(solution)/shard_map/ppermute | solution.py:369
  22.4 6.2 %collective-permute-start.5 = (bf16[16,1024]{1,0:T(8,128)(2,1)S(1)}, bf16[16,1024]{1,0:T(8,128)(2,1)S(1)}, u32[]{:S(2)}, u32[]{:S(2)}) collective-permute-start(bf16[16,1024]{1,0:T(8,128)(2,1)S(1)} %get-tuple-element.59), channel_id=1, source_target_pairs={{0,32},{4,36},{8,40},{12,44},{16,48},{20,52},{24,56},{28,60},{32,0... | collective-permute-start | bytes 98312 | tf_op jit(solution)/shard_map/ppermute | solution.py:369
  24.8 3.8 %collective-permute-start.6 = (bf16[16,1024]{1,0:T(8,128)(2,1)S(1)}, bf16[16,1024]{1,0:T(8,128)(2,1)S(1)}, u32[]{:S(2)}, u32[]{:S(2)}) collective-permute-start(bf16[16,1024]{1,0:T(8,128)(2,1)S(1)} %get-tuple-element.59), channel_id=1, source_target_pairs={{0,48},{4,52},{8,56},{12,60},{16,0},{20,4},{24,8},{28,12},{32,16},... | collective-permute-start | bytes 98312 | tf_op jit(solution)/shard_map/ppermute | solution.py:369
  28.7 6.8 %collective-permute-start.7 = (bf16[16,1024]{1,0:T(8,128)(2,1)S(1)}, bf16[16,1024]{1,0:T(8,128)(2,1)S(1)}, u32[]{:S(2)}, u32[]{:S(2)}) collective-permute-start(bf16[16,1024]{1,0:T(8,128)(2,1)S(1)} %fusion.31), channel_id=1, source_target_pairs={{0,64},{4,68},{8,72},{12,76},{16,80},{20,84},{24,88},{28,92},{32,9... | collective-permute-start | bytes 98312 | tf_op jit(solution)/shard_map/ppermute | solution.py:369
  30.1 5.5 %collective-permute-start.8 = (bf16[16,1024]{1,0:T(8,128)(2,1)S(1)}, bf16[16,1024]{1,0:T(8,128)(2,1)S(1)}, u32[]{:S(2)}, u32[]{:S(2)}) collective-permute-start(bf16[16,1024]{1,0:T(8,128)(2,1)S(1)} %fusion.31), channel_id=1, source_target_pairs={{0,128},{4,132},{8,136},{12,140},{16,144},{20,148},{24,152},{28,15... | collective-permute-start | bytes 98312 | tf_op jit(solution)/shard_map/ppermute | solution.py:369
  32.7 2.9 %collective-permute-start.9 = (bf16[16,1024]{1,0:T(8,128)(2,1)S(1)}, bf16[16,1024]{1,0:T(8,128)(2,1)S(1)}, u32[]{:S(2)}, u32[]{:S(2)}) collective-permute-start(bf16[16,1024]{1,0:T(8,128)(2,1)S(1)} %fusion.31), channel_id=1, source_target_pairs={{0,192},{4,196},{8,200},{12,204},{16,208},{20,212},{24,216},{28,22... | collective-permute-start | bytes 98312 | tf_op jit(solution)/shard_map/ppermute | solution.py:369
  35.6 8.0 %copy-start = (bf16[2048,512]{1,0:T(8,128)(2,1)S(1)}, bf16[2048,512]{1,0:T(8,128)(2,1)}, u32[]{:S(2)}) copy-start(bf16[2048,512]{1,0:T(8,128)(2,1)} %get-tuple-element.45.w_ref) | copy-start | bytes 6291460
  38.5 4.7 %collective-permute-start.10 = (bf16[128,1024]{1,0:T(8,128)(2,1)S(1)}, bf16[128,1024]{1,0:T(8,128)(2,1)S(1)}, u32[]{:S(2)}, u32[]{:S(2)}) collective-permute-start(bf16[128,1024]{1,0:T(8,128)(2,1)S(1)} %bitcast.20), channel_id=1, source_target_pairs={{0,1},{1,0},{2,3},{3,2},{4,5},{5,4},{6,7},{7,6},{8,9},{9,8},{10,11... | collective-permute-start | bytes 786440 | tf_op jit(solution)/shard_map/ppermute | solution.py:437
  42.1 1.5 %collective-permute-start.11 = (bf16[128,1024]{1,0:T(8,128)(2,1)S(1)}, bf16[128,1024]{1,0:T(8,128)(2,1)S(1)}, u32[]{:S(2)}, u32[]{:S(2)}) collective-permute-start(bf16[128,1024]{1,0:T(8,128)(2,1)S(1)} %bitcast.23), channel_id=1, source_target_pairs={{0,1},{1,0},{2,3},{3,2},{4,5},{5,4},{6,7},{7,6},{8,9},{9,8},{10,11... | collective-permute-start | bytes 786440 | tf_op jit(solution)/shard_map/ppermute | solution.py:437
  44.9 14.8 %collective-permute-start.16 = (bf16[256,1024]{1,0:T(8,128)(2,1)S(1)}, bf16[256,1024]{1,0:T(8,128)(2,1)S(1)}, u32[]{:S(2)}, u32[]{:S(2)}) collective-permute-start(bf16[256,1024]{1,0:T(8,128)(2,1)S(1)} %share_chunk.4.rest_6_.rest_4_), channel_id=1, source_target_pairs={{0,2},{2,0},{1,3},{3,1},{4,6},{6,4},{5,7},{7,5},{8,10},{10,8},{9,1... | collective-permute-start | bytes 1572872 | tf_op jit(solution)/shard_map/ppermute | solution.py:443
  50.1 1.9 %collective-permute-start.12 = (bf16[128,1024]{1,0:T(8,128)(2,1)S(1)}, bf16[128,1024]{1,0:T(8,128)(2,1)S(1)}, u32[]{:S(2)}, u32[]{:S(2)}) collective-permute-start(bf16[128,1024]{1,0:T(8,128)(2,1)S(1)} %bitcast.26), channel_id=1, source_target_pairs={{0,1},{1,0},{2,3},{3,2},{4,5},{5,4},{6,7},{7,6},{8,9},{9,8},{10,11... | collective-permute-start | bytes 786440 | tf_op jit(solution)/shard_map/ppermute | solution.py:437
  50.9 1.5 %collective-permute-start.13 = (bf16[128,1024]{1,0:T(8,128)(2,1)S(1)}, bf16[128,1024]{1,0:T(8,128)(2,1)S(1)}, u32[]{:S(2)}, u32[]{:S(2)}) collective-permute-start(bf16[128,1024]{1,0:T(8,128)(2,1)S(1)} %bitcast.29), channel_id=1, source_target_pairs={{0,1},{1,0},{2,3},{3,2},{4,5},{5,4},{6,7},{7,6},{8,9},{9,8},{10,11... | collective-permute-start | bytes 786440 | tf_op jit(solution)/shard_map/ppermute | solution.py:437
  53.7 15.9 %collective-permute-start.19 = (bf16[256,1024]{1,0:T(8,128)(2,1)S(1)}, bf16[256,1024]{1,0:T(8,128)(2,1)S(1)}, u32[]{:S(2)}, u32[]{:S(2)}) collective-permute-start(bf16[256,1024]{1,0:T(8,128)(2,1)S(1)} %share_chunk.5.rest_6_.rest_4_), channel_id=1, source_target_pairs={{0,2},{2,0},{1,3},{3,1},{4,6},{6,4},{5,7},{7,5},{8,10},{10,8},{9,1... | collective-permute-start | bytes 1572872 | tf_op jit(solution)/shard_map/ppermute | solution.py:443
  58.8 6.4 %collective-permute-start.14 = (bf16[128,1024]{1,0:T(8,128)(2,1)S(1)}, bf16[128,1024]{1,0:T(8,128)(2,1)S(1)}, u32[]{:S(2)}, u32[]{:S(2)}) collective-permute-start(bf16[128,1024]{1,0:T(8,128)(2,1)S(1)} %bitcast.32), channel_id=1, source_target_pairs={{0,1},{1,0},{2,3},{3,2},{4,5},{5,4},{6,7},{7,6},{8,9},{9,8},{10,11... | collective-permute-start | bytes 786440 | tf_op jit(solution)/shard_map/ppermute | solution.py:437
  59.5 5.7 %collective-permute-start.15 = (bf16[128,1024]{1,0:T(8,128)(2,1)S(1)}, bf16[128,1024]{1,0:T(8,128)(2,1)S(1)}, u32[]{:S(2)}, u32[]{:S(2)}) collective-permute-start(bf16[128,1024]{1,0:T(8,128)(2,1)S(1)} %bitcast.35), channel_id=1, source_target_pairs={{0,1},{1,0},{2,3},{3,2},{4,5},{5,4},{6,7},{7,6},{8,9},{9,8},{10,11... | collective-permute-start | bytes 786440 | tf_op jit(solution)/shard_map/ppermute | solution.py:437
  64.6 2.7 %collective-permute-start.17 = (bf16[128,1024]{1,0:T(8,128)(2,1)S(1)}, bf16[128,1024]{1,0:T(8,128)(2,1)S(1)}, u32[]{:S(2)}, u32[]{:S(2)}) collective-permute-start(bf16[128,1024]{1,0:T(8,128)(2,1)S(1)} %bitcast.16), channel_id=1, source_target_pairs={{0,1},{1,0},{2,3},{3,2},{4,5},{5,4},{6,7},{7,6},{8,9},{9,8},{10,11... | collective-permute-start | bytes 786440 | tf_op jit(solution)/shard_map/ppermute | solution.py:437
  65.2 2.1 %collective-permute-start.18 = (bf16[128,1024]{1,0:T(8,128)(2,1)S(1)}, bf16[128,1024]{1,0:T(8,128)(2,1)S(1)}, u32[]{:S(2)}, u32[]{:S(2)}) collective-permute-start(bf16[128,1024]{1,0:T(8,128)(2,1)S(1)} %bitcast.38), channel_id=1, source_target_pairs={{0,1},{1,0},{2,3},{3,2},{4,5},{5,4},{6,7},{7,6},{8,9},{9,8},{10,11... | collective-permute-start | bytes 786440 | tf_op jit(solution)/shard_map/ppermute | solution.py:437
  66.5 14.2 %collective-permute-start.20 = (bf16[256,1024]{1,0:T(8,128)(2,1)S(1)}, bf16[256,1024]{1,0:T(8,128)(2,1)S(1)}, u32[]{:S(2)}, u32[]{:S(2)}) collective-permute-start(bf16[256,1024]{1,0:T(8,128)(2,1)S(1)} %share_chunk.6.rest_4_), channel_id=1, source_target_pairs={{0,2},{2,0},{1,3},{3,1},{4,6},{6,4},{5,7},{7,5},{8,10},{10,8},{9,1... | collective-permute-start | bytes 1572872 | tf_op jit(solution)/shard_map/ppermute | solution.py:443
  70.8 21.2 %collective-permute-start.21 = (bf16[256,1024]{1,0:T(8,128)(2,1)S(1)}, bf16[256,1024]{1,0:T(8,128)(2,1)S(1)}, u32[]{:S(2)}, u32[]{:S(2)}) collective-permute-start(bf16[256,1024]{1,0:T(8,128)(2,1)S(1)} %share_chunk.7.rest_16_), channel_id=1, source_target_pairs={{0,2},{2,0},{1,3},{3,1},{4,6},{6,4},{5,7},{7,5},{8,10},{10,8},{9,1... | collective-permute-start | bytes 1572872 | tf_op jit(solution)/shard_map/ppermute | solution.py:443
  (2 other events, 4.0 us)
